TPU v7x, 32 devices: a whole 2x2x4 slice. The times are simulated.
32 devices in a mesh: dp: 2 (over core), row: 4 (over y, x), col: 4 (over z).
Axes of the slice: x: 2, y: 2, z: 4, core: 2. Of those that a mesh axis runs over, the one named last changes fastest.
Arguments:
- layer_in: bfloat16 [768, 4096], P(None, ('dp', 'row', 'col')), may hold values from -6 to 6
- lengths: int32 [2], P('dp'), may hold values from 512 to 2048, as said below
- w_attn: bfloat16 [768, 3, 768], P('col', None, 'row'), may hold values from -0.21875 to 0.21875
- b_attn: bfloat16 [2, 768], P(None, 'row'), may hold values from -3 to 3
- w_mixer: bfloat16 [768, 768], P('col', 'row'), may hold values from -6 to 6
- b_mixer: bfloat16 [768], P('col'), may hold values from -3 to 3
- gain_one: bfloat16 [768], P('col'), may hold values from 0.5 to 1.5
- shift_one: bfloat16 [768], P('col'), may hold values from -3 to 3
- w_expand: bfloat16 [768, 3072], P('col', 'row'), may hold values from -0.21875 to 0.21875
- b_expand: bfloat16 [3072], P('row'), may hold values from -3 to 3
- w_reduce: bfloat16 [768, 3072], P('col', 'row'), may hold values from -0.109375 to 0.109375
- b_reduce: bfloat16 [768], P('col'), may hold values from -3 to 3
- gain_two: bfloat16 [768], P('col'), may hold values from 0.5 to 1.5
- shift_two: bfloat16 [768], P('col'), may hold values from -3 to 3
- out_grad: bfloat16 [768, 4096], P(None, ('dp', 'row', 'col')), may hold values from -6 to 6
Outputs:
- layer_out: bfloat16 [768, 4096], P(None, ('dp', 'row', 'col'))
- grad_input: float32 [768, 4096], P(None, ('dp', 'row', 'col'))
- grad_attn: float32 [768, 3, 768], P('col', None, 'row')
- grad_attnbias: float32 [2, 768], P(None, 'row')
- grad_mixer: float32 [768, 768], P('col', 'row')
- grad_mixerbias: float32 [768], P('col')
- grad_gainone: float32 [768], P('col')
- grad_shiftone: float32 [768], P('col')
- grad_expand: float32 [768, 3072], P('col', 'row')
- grad_expandbias: float32 [3072], P('row')
- grad_reduce: float32 [768, 3072], P('col', 'row')
- grad_reducebias: float32 [768], P('col')
- grad_gaintwo: float32 [768], P('col')
- grad_shifttwo: float32 [768], P('col')
Inputs may be any that keep to these rules, and one draw needn't show every extreme that they name: lengths[s] slots of sequence s are valid, the rest are padding; some sequence fills all 2048 slots.
All inputs are finite; a program needn't handle non-finite values.
Results may differ from a plain program's by a relative error of at most 0.018.
Values may be sent and summed in bfloat16 or wider, within the bound.
A program may use at most 448 MiB of HBM per device.

v0:
```python
import jax
import jax.numpy as jnp
from jax import lax
from jax.sharding import PartitionSpec as P

D = 768
H = 12


EPSILON = 1e-12
NEGATIVE = -1000000000.0


def exact_gelu(values):
    return jax.nn.gelu(values, approximate=False)


def rounded(values):
    return lax.optimization_barrier(values.astype(jnp.bfloat16)).astype(jnp.float32)


def outer_prod(left_in, right_in):
    return lax.dot_general(
        left_in, right_in, (((0,), (0,)), ((), ())), preferred_element_type=jnp.float32
    )


def gather_rows(shard_in):
    return lax.all_gather(shard_in, "row", axis=0, tiled=True)


def row_sum(source, weight):
    return lax.psum_scatter(
        lax.dot_general(
            source, weight, (((1,), (1,)), ((), ())), preferred_element_type=jnp.float32
        ),
        "row",
        scatter_dimension=0,
        tiled=True,
    )


def normalize(values, gain_vec, shift_vec):
    row_mean = jnp.mean(values, 1, keepdims=True)
    centered = values - row_mean
    row_var = jnp.mean(centered * centered, 1, keepdims=True)
    row_scale = lax.rsqrt(row_var + EPSILON)
    normed = centered * row_scale
    return (normed * gain_vec + shift_vec, normed, row_scale)


def normalize_back(upstream, normed, row_scale, gain_vec):
    scaled = upstream * gain_vec
    mean_plain = jnp.mean(scaled, 1, keepdims=True)
    mean_cross = jnp.mean(scaled * normed, 1, keepdims=True)
    return row_scale * (scaled - mean_plain - normed * mean_cross)


def block_scores(query_block, keys_all, key_valid, score_scale):
    scores = (
        jnp.einsum("qhd,khd->hqk", query_block, keys_all, preferred_element_type=jnp.float32)
        * score_scale
    )
    return jnp.where(key_valid[None, None, :], scores, NEGATIVE)


def attend_forward(queries, keys_all, values_all, key_valid, block_rows, score_scale):
    n_blocks = queries.shape[0] // block_rows
    grouped = queries.reshape(n_blocks, block_rows, queries.shape[1], queries.shape[2])

    def one_block(query_block):
        scores = block_scores(query_block, keys_all, key_valid, score_scale)
        top_score = jnp.max(scores, 2, keepdims=True)
        exp_scores = jnp.exp(scores - top_score)
        row_total = jnp.sum(exp_scores, 2, keepdims=True)
        weights = (exp_scores / row_total).astype(jnp.bfloat16)
        context = jnp.einsum(
            "hqk,khd->qhd", weights, values_all, preferred_element_type=jnp.float32
        )
        return (context.astype(jnp.bfloat16), top_score, row_total)

    context, top_scores, row_totals = lax.map(one_block, grouped)
    return (context.reshape(queries.shape), top_scores, row_totals)


def block_backward(
    query_block, grad_block, top_score, row_total, keys_all, values_all, key_valid, score_scale
):
    scores = block_scores(query_block, keys_all, key_valid, score_scale)
    probs_full = jnp.exp(scores - top_score) / row_total
    weights = probs_full.astype(jnp.bfloat16)
    grad_weights = jnp.einsum(
        "qhd,khd->hqk", grad_block, values_all, preferred_element_type=jnp.float32
    )
    row_inner = jnp.sum(probs_full * grad_weights, 2, keepdims=True)
    grad_scores = (probs_full * (grad_weights - row_inner)).astype(jnp.bfloat16)
    grad_query = (
        jnp.einsum("hqk,khd->qhd", grad_scores, keys_all, preferred_element_type=jnp.float32)
        * score_scale
    )
    return (weights, grad_scores, grad_query, row_inner)


def attend_backward(
    queries,
    keys_all,
    values_all,
    key_valid,
    top_scores,
    row_totals,
    grad_context,
    block_rows,
    score_scale,
):
    n_blocks = queries.shape[0] // block_rows
    grouped = queries.reshape(n_blocks, block_rows, queries.shape[1], queries.shape[2])
    grad_grouped = grad_context.reshape(grouped.shape)

    def one_step(running, block_items):
        grad_keys, grad_values = running
        query_block, grad_block, top_score, row_total = block_items
        weights, grad_scores, grad_query, row_inner = block_backward(
            query_block,
            grad_block,
            top_score,
            row_total,
            keys_all,
            values_all,
            key_valid,
            score_scale,
        )
        grad_keys = (
            grad_keys
            + jnp.einsum(
                "hqk,qhd->khd", grad_scores, query_block, preferred_element_type=jnp.float32
            )
            * score_scale
        )
        grad_values = grad_values + jnp.einsum(
            "hqk,qhd->khd", weights, grad_block, preferred_element_type=jnp.float32
        )
        return ((grad_keys, grad_values), (grad_query, row_inner))

    zeros_kv = jnp.zeros(keys_all.shape, jnp.float32)
    (grad_keys, grad_values), (grad_queries, row_inners) = lax.scan(
        one_step, (zeros_kv, zeros_kv), (grouped, grad_grouped, top_scores, row_totals)
    )
    return (grad_queries.reshape(queries.shape), grad_keys, grad_values, row_inners)


def on_device(
    layer_in,
    lengths,
    w_attn,
    b_attn,
    w_mixer,
    b_mixer,
    gain_one,
    shift_one,
    w_expand,
    b_expand,
    w_reduce,
    b_reduce,
    gain_two,
    shift_two,
    out_grad,
):
    n_row = lax.axis_size("row")
    n_col = lax.axis_size("col")
    row_index = lax.axis_index("row")
    col_index = lax.axis_index("col")
    rows_here = layer_in.shape[1]
    cols_here = rows_here * n_row
    seq_slots = cols_here * n_col
    feat_here = w_attn.shape[2]
    units_here = w_expand.shape[1]
    col_feats = w_mixer.shape[0]
    head_size = D // H
    head_count = feat_here // head_size
    score_scale = head_size ** (-0.5)
    block_rows = min(512, cols_here)
    length = lengths[0]
    slot_ids = jnp.arange(seq_slots)
    key_pos = (
        slot_ids % cols_here // rows_here * (rows_here * n_col)
        + slot_ids // cols_here * rows_here
        + slot_ids % rows_here
    )
    key_valid = key_pos < length
    own_pos = row_index * (rows_here * n_col) + col_index * rows_here + jnp.arange(rows_here)
    row_valid = (own_pos < length).astype(jnp.float32)[:, None]
    (
        attn_w,
        mixer_w,
        expand_w,
        reduce_w,
        mixer_bias,
        gain_a,
        shift_a,
        reduce_bias,
        gain_b,
        shift_b,
    ) = (
        lax.all_gather(w_attn, "col", axis=0, tiled=True),
        lax.all_gather(w_mixer, "col", axis=0, tiled=True),
        lax.all_gather(w_expand, "col", axis=0, tiled=True),
        lax.all_gather(w_reduce, "col", axis=0, tiled=True),
        lax.all_gather(b_mixer, "col", axis=0, tiled=True),
        lax.all_gather(gain_one, "col", axis=0, tiled=True),
        lax.all_gather(shift_one, "col", axis=0, tiled=True),
        lax.all_gather(b_reduce, "col", axis=0, tiled=True),
        lax.all_gather(gain_two, "col", axis=0, tiled=True),
        lax.all_gather(shift_two, "col", axis=0, tiled=True),
    )
    feat_total = attn_w.shape[0]
    qkv_w = attn_w.reshape(feat_total, 3 * feat_here)
    x_own = layer_in.T
    x_rows = gather_rows(x_own)
    projected = jnp.dot(x_rows, qkv_w, preferred_element_type=jnp.float32).reshape(
        cols_here, 3, feat_here
    )
    queries = (projected[:, 0] + b_attn[0]).astype(jnp.bfloat16)
    keys_own = projected[:, 1].astype(jnp.bfloat16)
    values_own = (projected[:, 2] + b_attn[1]).astype(jnp.bfloat16)
    keys_all, values_all = (
        lax.all_gather(keys_own, "col", axis=0, tiled=True),
        lax.all_gather(values_own, "col", axis=0, tiled=True),
    )
    query_heads = queries.reshape(cols_here, head_count, head_size)
    key_heads = keys_all.reshape(seq_slots, head_count, head_size)
    value_heads = values_all.reshape(seq_slots, head_count, head_size)
    context, top_scores, row_totals = attend_forward(
        query_heads, key_heads, value_heads, key_valid, block_rows, score_scale
    )
    context = context.reshape(cols_here, feat_here)
    mixed = row_sum(context, mixer_w)
    first_sum = x_own.astype(jnp.float32) + mixed + mixer_bias
    hidden, normed_one, scale_one = normalize(first_sum, gain_a, shift_a)
    hidden_rows = gather_rows(hidden.astype(jnp.bfloat16))
    inner = jnp.dot(hidden_rows, expand_w, preferred_element_type=jnp.float32) + b_expand
    active = exact_gelu(inner).astype(jnp.bfloat16)
    reduced = row_sum(active, reduce_w)
    second_sum = hidden + reduced + reduce_bias
    output, normed_two, scale_two = normalize(second_sum, gain_b, shift_b)
    layer_out = (output * row_valid).T.astype(jnp.bfloat16)
    upstream = out_grad.T.astype(jnp.float32) * row_valid
    gain_two_part = jnp.sum(upstream * normed_two, 0)
    shift_two_part = jnp.sum(upstream, 0)
    grad_second = normalize_back(upstream, normed_two, scale_two, gain_b)
    grad_reduced = grad_second.astype(jnp.bfloat16)
    reduce_b_part = jnp.sum(grad_reduced.astype(jnp.float32), 0)
    grad_red_rows = gather_rows(grad_reduced)
    grad_reduce_w = outer_prod(grad_red_rows, active)
    grad_active = jnp.dot(grad_red_rows, reduce_w, preferred_element_type=jnp.float32)
    gelu_pull = jax.vjp(exact_gelu, inner)[1]
    grad_inner = gelu_pull(rounded(grad_active))[0].astype(jnp.bfloat16)
    grad_expand_w = outer_prod(hidden_rows, grad_inner)
    expand_b_rows = jnp.sum(grad_inner.astype(jnp.float32), 0)
    grad_hidden = row_sum(grad_inner, expand_w) + grad_second
    gain_one_part = jnp.sum(grad_hidden * normed_one, 0)
    shift_one_part = jnp.sum(grad_hidden, 0)
    grad_first = normalize_back(grad_hidden, normed_one, scale_one, gain_a)
    grad_mixed = grad_first.astype(jnp.bfloat16)
    mixer_b_part = jnp.sum(grad_mixed.astype(jnp.float32), 0)
    grad_mix_rows = gather_rows(grad_mixed)
    grad_mixer_w = outer_prod(grad_mix_rows, context)
    grad_context = jnp.dot(grad_mix_rows, mixer_w, preferred_element_type=jnp.float32).astype(
        jnp.bfloat16
    )
    grad_ctx_heads = grad_context.reshape(cols_here, head_count, head_size)
    grad_queries, grad_keys, grad_values, row_inners = attend_backward(
        query_heads,
        key_heads,
        value_heads,
        key_valid,
        top_scores,
        row_totals,
        grad_ctx_heads,
        block_rows,
        score_scale,
    )
    grad_keys_own, grad_values_own = (
        lax.psum_scatter(
            grad_keys.reshape(seq_slots, feat_here).astype(jnp.bfloat16),
            "col",
            scatter_dimension=0,
            tiled=True,
        ).astype(jnp.float32),
        lax.psum_scatter(
            grad_values.reshape(seq_slots, feat_here).astype(jnp.bfloat16),
            "col",
            scatter_dimension=0,
            tiled=True,
        ).astype(jnp.float32),
    )
    grad_attn_out = jnp.concatenate(
        [grad_queries.reshape(cols_here, feat_here), grad_keys_own, grad_values_own], 1
    ).astype(jnp.bfloat16)
    grad_attn_w = outer_prod(x_rows, grad_attn_out).reshape(feat_total, 3, feat_here)
    bias_rows = jnp.sum(grad_attn_out.astype(jnp.float32), 0).reshape(3, feat_here)
    attn_b_rows = jnp.stack([bias_rows[0], bias_rows[2]])
    grad_x_attn = row_sum(grad_attn_out, qkv_w)
    grad_input = (grad_x_attn + grad_first).T
    grad_attn_w, grad_mixer_w, grad_expand_w, grad_reduce_w = (
        lax.psum_scatter(
            grad_attn_w.astype(jnp.bfloat16), "col", scatter_dimension=0, tiled=True
        ).astype(jnp.float32),
        lax.psum_scatter(
            grad_mixer_w.astype(jnp.bfloat16), "col", scatter_dimension=0, tiled=True
        ).astype(jnp.float32),
        lax.psum_scatter(
            grad_expand_w.astype(jnp.bfloat16), "col", scatter_dimension=0, tiled=True
        ).astype(jnp.float32),
        lax.psum_scatter(
            grad_reduce_w.astype(jnp.bfloat16), "col", scatter_dimension=0, tiled=True
        ).astype(jnp.float32),
    )
    grad_attn_w, grad_mixer_w, grad_expand_w, grad_reduce_w = (
        lax.psum(grad_attn_w.astype(jnp.bfloat16), "dp").astype(jnp.float32),
        lax.psum(grad_mixer_w.astype(jnp.bfloat16), "dp").astype(jnp.float32),
        lax.psum(grad_expand_w.astype(jnp.bfloat16), "dp").astype(jnp.float32),
        lax.psum(grad_reduce_w.astype(jnp.bfloat16), "dp").astype(jnp.float32),
    )
    attn_b_full = lax.dynamic_update_slice_in_dim(
        jnp.zeros((2, feat_here * n_row), jnp.float32), attn_b_rows, row_index * feat_here, 1
    )
    expand_b_full = lax.dynamic_update_slice_in_dim(
        jnp.zeros((units_here * n_row,), jnp.float32), expand_b_rows, row_index * units_here, 0
    )
    (
        attn_b_sum,
        expand_b_sum,
        mixer_b_sum,
        gain_one_sum,
        shift_one_sum,
        reduce_b_sum,
        gain_two_sum,
        shift_two_sum,
    ) = lax.psum(
        (
            attn_b_full,
            expand_b_full,
            mixer_b_part,
            gain_one_part,
            shift_one_part,
            reduce_b_part,
            gain_two_part,
            shift_two_part,
        ),
        ("dp", "row", "col"),
    )
    col_start = col_index * col_feats
    grad_attn_b = lax.dynamic_slice_in_dim(attn_b_sum, row_index * feat_here, feat_here, 1)
    grad_expand_b = lax.dynamic_slice_in_dim(expand_b_sum, row_index * units_here, units_here, 0)
    grad_mixer_b = lax.dynamic_slice_in_dim(mixer_b_sum, col_start, col_feats, 0)
    grad_gain_one = lax.dynamic_slice_in_dim(gain_one_sum, col_start, col_feats, 0)
    grad_shift_one = lax.dynamic_slice_in_dim(shift_one_sum, col_start, col_feats, 0)
    grad_reduce_b = lax.dynamic_slice_in_dim(reduce_b_sum, col_start, col_feats, 0)
    grad_gain_two = lax.dynamic_slice_in_dim(gain_two_sum, col_start, col_feats, 0)
    grad_shift_two = lax.dynamic_slice_in_dim(shift_two_sum, col_start, col_feats, 0)
    return (
        layer_out,
        grad_input,
        grad_attn_w,
        grad_attn_b,
        grad_mixer_w,
        grad_mixer_b,
        grad_gain_one,
        grad_shift_one,
        grad_expand_w,
        grad_expand_b,
        grad_reduce_w,
        grad_reduce_b,
        grad_gain_two,
        grad_shift_two,
    )


def solution(mesh):
    return jax.shard_map(
        on_device,
        mesh=mesh,
        in_specs=(
            P(None, ("dp", "row", "col")),
            P("dp"),
            P("col", None, "row"),
            P(None, "row"),
            P("col", "row"),
            P("col"),
            P("col"),
            P("col"),
            P("col", "row"),
            P("row"),
            P("col", "row"),
            P("col"),
            P("col"),
            P("col"),
            P(None, ("dp", "row", "col")),
        ),
        out_specs=(
            P(None, ("dp", "row", "col")),
            P(None, ("dp", "row", "col")),
            P("col", None, "row"),
            P(None, "row"),
            P("col", "row"),
            P("col"),
            P("col"),
            P("col"),
            P("col", "row"),
            P("row"),
            P("col", "row"),
            P("col"),
            P("col"),
            P("col"),
        ),
        check_vma=False,
    )
```

profile of v0, /device:TPU:25, one launch (start us, length us, event | category | flops | bytes accessed | tf_op | source)
XLA Modules:
  0.0 521.1 jit_solution(6010787880880753846)
XLA Ops:
  9.4 1.1 copy.40
  10.5 1.2 copy.41
  11.7 9.4 %all_gather.48 = bf16[512,768]{1,0:T(8,128)(2,1)S(1)} all-gather(bf16[128,768]{1,0:T(8,128)(2,1)S(1)} %bitcast.101), channel_id=1, replica_groups=mesh['dp'=2,'row'=4,'col'=4] {'row'}, dimensions={0}, use_global_device_ids=true | all-gather | bytes 983040 | tf_op jit(solution)/shard_map/all_gather | solution.py:29
  21.1 27.1 %all_gather.49 = bf16[768,3,192]{2,1,0:T(4,128)(2,1)S(1)} all-gather(bf16[192,3,192]{2,1,0:T(4,128)(2,1)S(1)} %copy.41), channel_id=1, replica_groups=mesh['dp'=2,'row'=4,'col'=4] {'col'}, dimensions={0}, use_global_device_ids=true | all-gather | bytes 1105920 | tf_op jit(solution)/shard_map/all_gather | solution.py:204
  52.1 13.2 %all_gather.52 = bf16[768,192]{1,0:T(8,128)(2,1)S(1)} all-gather(bf16[192,192]{1,0:T(8,128)(2,1)S(1)} %copy-done.19), channel_id=1, replica_groups=mesh['dp'=2,'row'=4,'col'=4] {'col'}, dimensions={0}, use_global_device_ids=true | all-gather | bytes 368640 | tf_op jit(solution)/shard_map/all_gather | solution.py:205
  65.4 15.4 %all-gather = bf16[2048,1,192]{0,2,1:T(8,128)(2,1)S(1)} all-gather(bf16[512,1,192]{0,2,1:T(8,128)(2,1)} %slice.48), channel_id=2, replica_groups=mesh['dp'=2,'row'=4,'col'=4] {'col'}, dimensions={0}, use_global_device_ids=true | all-gather | bytes 983040 | tf_op jit(solution)/shard_map/all_gather | solution.py:226
  80.8 15.5 %all_gather.50 = bf16[2048,192]{0,1:T(8,128)(2,1)S(1)} all-gather(bf16[512,192]{0,1:T(8,128)(2,1)S(1)} %fusion.36), channel_id=1, replica_groups=mesh['dp'=2,'row'=4,'col'=4] {'col'}, dimensions={0}, use_global_device_ids=true | all-gather | bytes 983040 | tf_op jit(solution)/shard_map/all_gather | solution.py:227
  96.3 6.9 %fusion.76 = (f32[3,512]{1,0:T(4,128)S(1)}, f32[3,512,2048]{2,1,0:T(8,128)}) fusion(pred[2048]{0:T(1024)(128)(4,1)S(1)} %fusion.56, bf16[2048,3,64]{0,2,1:T(8,128)(2,1)S(1)} %bitcast.98, f32[512,3,64]{0,2,1:T(8,128)S(1)} %bitcast.102, f32[3,64]{1,0:T(4,128)S(1)} %reshape.173), kind=kOutput, calls=%fused_computation.141 | convolution fusion | flops 415434752 | bytes 13771520 | tf_op jit(solution)/shard_map/while/body/eval_jaxpr/sub | solution.py:74
  103.3 6.7 %fusion.28 = bf16[3,64,512]{2,1,0:T(8,128)(2,1)S(1)} fusion(bf16[2048,3,64]{0,2,1:T(8,128)(2,1)S(1)} %bitcast.106, f32[3,512,2048]{2,1,0:T(8,128)} %get-tuple-element.156, f32[3,512]{1,0:T(4,128)S(1)} %get-tuple-element.155), kind=kOutput, calls=%fused_computation.52 | convolution fusion | flops 409042944 | bytes 13572096 | tf_op jit(solution)/shard_map/while/body/eval_jaxpr/hqk,khd->qhd/dot_general | solution.py:77
  110.7 1.6 fusion.77
  116.3 11.6 %all-reduce.7 = (bf16[768]{0:T(1024)(128)(2,1)S(1)}, bf16[768]{0:T(1024)(128)(2,1)S(1)}, bf16[768]{0:T(1024)(128)(2,1)S(1)}, bf16[768]{0:T(1024)(128)(2,1)S(1)},...) all-reduce(bf16[768]{0:T(1024)(128)(2,1)S(1)} %dynamic-update-slice, ...), channel_id=1, replica_groups=mesh['dp'=2,'row'=4,'col'=4] {'col'}, use_global_device_ids=true, to_apply=%add | all-reduce | flops 4608 | bytes 18432
  127.9 24.1 %reduce-scatter.11.cloned.1.call-done = f32[128,768]{1,0:T(8,128)} async-done(((f32[512,768]{1,0:T(8,128)}), f32[128,768]{1,0:T(8,128)}) %reduce-scatter.11.cloned.1.call-update) | async-done | bytes 393232 | tf_op jit(solution)/shard_map/reduce_scatter | solution.py:33
  152.0 1.1 fusion.74
  153.5 9.3 %all_gather.56 = bf16[512,768]{1,0:T(8,128)(2,1)S(1)} all-gather(bf16[128,768]{1,0:T(8,128)(2,1)S(1)} %fusion.40), channel_id=1, replica_groups=mesh['dp'=2,'row'=4,'col'=4] {'row'}, dimensions={0}, use_global_device_ids=true | all-gather | bytes 983040 | tf_op jit(solution)/shard_map/all_gather | solution.py:29
  162.9 6.8 %multiply_convert_fusion.1 = (bf16[512,768]{1,0:T(8,128)(2,1)}, f32[512,768]{1,0:T(8,128)}, f32[512,768]{1,0:T(8,128)}) fusion(f32[768]{0:T(1024)S(1)} %convert_element_type.181, bf16[512,768]{1,0:T(8,128)(2,1)S(1)} %all_gather.56, bf16[768,768]{1,0:T(8,128)(2,1)} %all-gather.4.cloned.1.call-done), kind=kOutput, calls=%fused_computation.29 | convolution fusion | flops 629932032 | bytes 5901312 | tf_op jit(solution)/shard_map/dot_general | solution.py:240
  169.7 12.8 %all-gather.6.cloned.1.call-done = bf16[768,768]{1,0:T(8,128)(2,1)} async-done(((bf16[192,768]{1,0:T(8,128)(2,1)}), bf16[768,768]{1,0:T(8,128)(2,1)}) %all-gather.6.cloned.1.call-update) | async-done | bytes 1179664 | tf_op jit(solution)/shard_map/all_gather | solution.py:207
  182.5 3.5 fusion.78
  187.1 31.0 %reduce-scatter.13.cloned.1.call-done = f32[128,768]{1,0:T(8,128)} async-done(((f32[512,768]{1,0:T(8,128)}), f32[128,768]{1,0:T(8,128)}) %reduce-scatter.13.cloned.1.call-update) | async-done | bytes 393232 | tf_op jit(solution)/shard_map/reduce_scatter | solution.py:33
  218.0 1.2 fusion.72
  220.0 9.5 %all_gather.62 = bf16[512,768]{1,0:T(8,128)(2,1)S(1)} all-gather(bf16[128,768]{1,0:T(8,128)(2,1)S(1)} %get-tuple-element.139), channel_id=1, replica_groups=mesh['dp'=2,'row'=4,'col'=4] {'row'}, dimensions={0}, use_global_device_ids=true | all-gather | bytes 983040 | tf_op jit(solution)/shard_map/all_gather | solution.py:29
  231.7 1.3 convert_reduce_fusion
  233.9 2.0 fusion.79
  236.1 32.8 %reduce-scatter.15.cloned.1.call-done = f32[128,768]{1,0:T(8,128)} async-done(((f32[512,768]{1,0:T(8,128)}), f32[128,768]{1,0:T(8,128)}) %reduce-scatter.15.cloned.1.call-update) | async-done | bytes 393232 | tf_op jit(solution)/shard_map/reduce_scatter | solution.py:33
  268.9 2.1 multiply_reduce_fusion.1
  270.9 1.5 convert_reduce_fusion.3
  272.5 9.6 %all_gather.63 = bf16[512,768]{1,0:T(8,128)(2,1)S(1)} all-gather(bf16[128,768]{1,0:T(8,128)(2,1)S(1)} %get-tuple-element.143), channel_id=1, replica_groups=mesh['dp'=2,'row'=4,'col'=4] {'row'}, dimensions={0}, use_global_device_ids=true | all-gather | bytes 983040 | tf_op jit(solution)/shard_map/all_gather | solution.py:29
  282.5 6.9 %fusion.10 = bf16[3,64,2048]{2,1,0:T(8,128)(2,1)} fusion(bf16[512,3,64]{0,2,1:T(8,128)(2,1)S(1)} %bitcast.113, f32[3,512,2048]{2,1,0:T(8,128)} %get-tuple-element.156, f32[3,512]{1,0:T(4,128)S(1)} %copy-done.27), kind=kOutput, calls=%fused_computation.16 | convolution fusion | flops 409337856 | bytes 13572096 | tf_op jit(solution)/shard_map/while/body/eval_jaxpr/hqk,qhd->khd/dot_general | solution.py:139
  290.0 5.7 %multiply_reduce_fusion = (f32[3,512]{1,0:T(4,128)S(1)}, f32[3,512,2048]{2,1,0:T(8,128)}) fusion(f32[3,512,2048]{2,1,0:T(8,128)S(1)} %bitcast.96, f32[3,512]{1,0:T(4,128)S(1)} %copy-done.27, bf16[512,3,64]{0,2,1:T(8,128)(2,1)S(1)} %bitcast.114, bf16[2048,3,64]{0,2,1:T(8,128)(2,1)S(1)} %bitcast.107), kind=kOutput, calls=%fused_computation.2 | convolution fusion | flops 412088832 | bytes 26161152 | tf_op jit(solution)/shard_map/while/body/eval_jaxpr/qhd,khd->hqk/dot_general | solution.py:92
  295.7 9.2 %multiply_convert_fusion = bf16[3,512,2048]{2,1,0:T(8,128)(2,1)S(1)} fusion(f32[3,512,2048]{2,1,0:T(8,128)} %get-tuple-element.159, f32[3,512]{1,0:T(4,128)S(1)} %get-tuple-element.158, f32[3,512,2048]{2,1,0:T(8,128)} %get-tuple-element.156, f32[3,512]{1,0:T(4,128)S(1)} %copy-done.27), kind=kLoop, calls=%fused_computation.1 | loop fusion | flops 12582912 | bytes 31469568 | tf_op jit(solution)/shard_map/while/body/eval_jaxpr/convert_element_type | solution.py:96
  304.9 2.8 fusion.9
  308.0 3.2 convolution_convert_fusion
  311.3 3.3 convolution_convert_fusion.1
  314.7 1.2 convolution_convert_fusion.4
  316.0 4.9 fusion.31
  320.9 21.8 %reduce-scatter.17.cloned.1.call-done = bf16[512,192]{0,1:T(8,128)(2,1)} async-done(((bf16[2048,192]{0,1:T(8,128)(2,1)}), bf16[512,192]{0,1:T(8,128)(2,1)}) %reduce-scatter.17.cloned.1.call-update) | async-done | bytes 196624 | tf_op jit(solution)/shard_map/reduce_scatter | solution.py:283
  342.7 1.6 convolution_convert_fusion.2
  344.3 1.4 copy.44
  345.9 28.0 %reduce-scatter.29.cloned.1.call-done = bf16[192,768]{1,0:T(8,128)(2,1)} async-done(((bf16[768,768]{1,0:T(8,128)(2,1)}), bf16[192,768]{1,0:T(8,128)(2,1)}) %reduce-scatter.29.cloned.1.call-update) | async-done | bytes 294928 | tf_op jit(solution)/shard_map/reduce_scatter | solution.py:314
  373.9 30.2 %reduce-scatter.27.cloned.1.call-done = bf16[192,768]{1,0:T(8,128)(2,1)} async-done(((bf16[768,768]{1,0:T(8,128)(2,1)}), bf16[192,768]{1,0:T(8,128)(2,1)}) %reduce-scatter.27.cloned.1.call-update) | async-done | bytes 294928 | tf_op jit(solution)/shard_map/reduce_scatter | solution.py:311
  404.0 20.0 %reduce-scatter.25.cloned.1.call-done = bf16[192,192]{1,0:T(8,128)(2,1)} async-done(((bf16[768,192]{1,0:T(8,128)(2,1)}), bf16[192,192]{1,0:T(8,128)(2,1)}) %reduce-scatter.25.cloned.1.call-update) | async-done | bytes 73744 | tf_op jit(solution)/shard_map/reduce_scatter | solution.py:308
  424.0 31.6 %reduce-scatter.23.cloned.1.call-done = bf16[192,3,192]{2,0,1:T(8,128)(2,1)} async-done(((bf16[768,3,192]{2,0,1:T(8,128)(2,1)}), bf16[192,3,192]{2,0,1:T(8,128)(2,1)}) %reduce-scatter.23.cloned.1.call-update) | async-done | bytes 221200 | tf_op jit(solution)/shard_map/reduce_scatter | solution.py:305
  455.9 2.0 fusion.66
  460.2 40.6 %all-reduce.6 = (f32[2,768]{1,0:T(2,128)S(1)}, f32[768]{0:T(1024)S(1)}, f32[768]{0:T(1024)S(1)}, f32[768]{0:T(1024)S(1)}, f32[3072]{0:T(1024)S(1)}, /*index=5*/f...) all-reduce(f32[2,768]{1,0:T(2,128)S(1)} %dynamic_update_slice.17, ...), channel_id=1, replica_groups=mesh['dp'=2,'row'=4,'col'=4] {'dp','row','col'}, use_global_device_ids=true, to_apply=%region_20.21 | all-reduce | flops 9216 | bytes 73728 | tf_op jit(solution)/shard_map/psum | solution.py:339
  505.9 1.6 convert_element_type.209
  507.6 1.8 convert_element_type.206
  509.4 1.8 convert_element_type.212
  512.1 1.0 add_bitcast_fusion
  513.1 0.9 copy.46
  (176 shorter events, 23.7 us)
Async XLA Ops:
  8.0 144.0 %reduce-scatter.11.cloned.1.call-start = ((), (), s32[]{:S(2)}) async-start(), calls=%async_computation.10 | async-start | bytes 1966080 | tf_op jit(solution)/shard_map/reduce_scatter | solution.py:33
  21.1 28.0 %copy-start.1 = (bf16[512,768]{1,0:T(8,128)(2,1)}, bf16[512,768]{1,0:T(8,128)(2,1)S(1)}, u32[]{:S(2)}) copy-start(bf16[512,768]{1,0:T(8,128)(2,1)S(1)} %all_gather.48) | copy-start | bytes 2359300
  49.2 2.9 copy-start.19
  65.3 31.0 %copy-start.6 = (f32[512,1,192]{0,2,1:T(8,128)S(1)}, f32[512,1,192]{0,2,1:T(8,128)}, u32[]{:S(2)}) copy-start(f32[512,1,192]{0,2,1:T(8,128)} %slice.38) | copy-start | bytes 1179652
  96.3 7.0 %copy-start.8 = (bf16[2048,192]{0,1:T(8,128)(2,1)}, bf16[2048,192]{0,1:T(8,128)(2,1)S(1)}, u32[]{:S(2)}) copy-start(bf16[2048,192]{0,1:T(8,128)(2,1)S(1)} %all_gather.50) | copy-start | bytes 2359300
  103.3 6.7 %copy-start.26 = (f32[3,512]{1,0:T(4,128)}, f32[3,512]{1,0:T(4,128)S(1)}, u32[]{:S(2)}) copy-start(f32[3,512]{1,0:T(4,128)S(1)} %get-tuple-element.155) | copy-start | bytes 18436
  112.3 1.3 copy-start.37
  112.3 2.6 copy-start.31
  112.3 2.8 copy-start.32
  112.3 3.1 copy-start.33
  112.3 3.3 copy-start.34
  112.3 3.5 copy-start.35
  112.3 3.7 copy-start.36
  112.3 15.6 %copy-start.28 = (bf16[768]{0:T(1024)(128)(2,1)S(1)}, bf16[768]{0:T(1024)(128)(2,1)}, u32[]{:S(2)}) copy-start(bf16[768]{0:T(1024)(128)(2,1)} %param.24) | copy-start | bytes 4612
  112.4 50.5 %all-gather.4.cloned.1.call-start = ((), (), s32[]{:S(2)}) async-start(), calls=%async_computation.11 | async-start | bytes 1474560 | tf_op jit(solution)/shard_map/all_gather | solution.py:206
  112.9 69.6 %all-gather.6.cloned.1.call-start = ((), (), s32[]{:S(2)}) async-start(), calls=%async_computation.12 | async-start | bytes 1474560 | tf_op jit(solution)/shard_map/all_gather | solution.py:207
  113.5 104.5 %reduce-scatter.13.cloned.1.call-start = ((), (), s32[]{:S(2)}) async-start(), calls=%async_computation.13 | async-start | bytes 1966080 | tf_op jit(solution)/shard_map/reduce_scatter | solution.py:33
  162.9 6.8 %copy-start.10 = (bf16[512,768]{1,0:T(8,128)(2,1)}, bf16[512,768]{1,0:T(8,128)(2,1)S(1)}, u32[]{:S(2)}) copy-start(bf16[512,768]{1,0:T(8,128)(2,1)S(1)} %all_gather.56) | copy-start | bytes 2359300
  186.0 82.9 %reduce-scatter.15.cloned.1.call-start = ((), (), s32[]{:S(2)}) async-start(), calls=%async_computation.14 | async-start | bytes 1966080 | tf_op jit(solution)/shard_map/reduce_scatter | solution.py:33
  187.1 81.8 %copy-start.24 = (f32[128]{0:T(128)}, f32[128]{0:T(128)S(1)}, u32[]{:S(2)}) copy-start(f32[128]{0:T(128)S(1)} %compare_convert_fusion) | copy-start | bytes 1540
  219.3 10.3 %copy-start.30 = (bf16[768,768]{1,0:T(8,128)(2,1)S(1)}, bf16[768,768]{1,0:T(8,128)(2,1)}, u32[]{:S(2)}) copy-start(bf16[768,768]{1,0:T(8,128)(2,1)} %all-gather.6.cloned.1.call-done) | copy-start | bytes 3538948
  229.5 1.7 copy-start.3
  229.6 2.2 copy-start.4
  231.7 2.2 copy-start.29
  236.0 84.9 %reduce-scatter.19.cloned.1.call-start = ((), (), s32[]{:S(2)}) async-start(), calls=%async_computation.16 | async-start | bytes 983040 | tf_op jit(solution)/shard_map/reduce_scatter | solution.py:289
  270.9 11.6 %copy-start.27 = (f32[3,512]{1,0:T(4,128)S(1)}, f32[3,512]{1,0:T(4,128)}, u32[]{:S(2)}) copy-start(f32[3,512]{1,0:T(4,128)} %copy-done.26) | copy-start | bytes 18436
  272.5 17.0 %slice-start = ((s8[12582912]{0:T(1024)(128)(4,1)}), s8[4194304]{0:T(1024)(128)(4,1)S(1)}, s32[]{:S(2)}) async-start(s8[12582912]{0:T(1024)(128)(4,1)} %bitcast.95), calls=%async_computation.23 | async-start | bytes 8388608
  282.5 7.0 %slice-start.1 = ((s8[12582912]{0:T(1024)(128)(4,1)}), s8[4194304]{0:T(1024)(128)(4,1)S(1)}, s32[]{:S(2)}) async-start(s8[12582912]{0:T(1024)(128)(4,1)} %bitcast.95), calls=%async_computation.24 | async-start | bytes 8388608
  282.5 7.0 %slice-start.2 = ((s8[12582912]{0:T(1024)(128)(4,1)}), s8[4194304]{0:T(1024)(128)(4,1)S(1)}, s32[]{:S(2)}) async-start(s8[12582912]{0:T(1024)(128)(4,1)} %bitcast.95), calls=%async_computation.25 | async-start | bytes 8388608
  282.5 7.4 %copy-start.9 = (bf16[2048,192]{0,1:T(8,128)(2,1)S(1)}, bf16[2048,192]{0,1:T(8,128)(2,1)}, u32[]{:S(2)}) copy-start(bf16[2048,192]{0,1:T(8,128)(2,1)} %copy-done.8) | copy-start | bytes 2359300
  295.7 47.0 %reduce-scatter.17.cloned.1.call-start = ((), (), s32[]{:S(2)}) async-start(), calls=%async_computation.15 | async-start | bytes 983040 | tf_op jit(solution)/shard_map/reduce_scatter | solution.py:283
  295.7 9.2 %copy-start.7 = (f32[512,1,192]{0,2,1:T(8,128)S(1)}, f32[512,1,192]{0,2,1:T(8,128)}, u32[]{:S(2)}) copy-start(f32[512,1,192]{0,2,1:T(8,128)} %slice.38) | copy-start | bytes 1179652
  304.9 3.0 copy-start
  308.0 65.9 %reduce-scatter.29.cloned.1.call-start = ((), (), s32[]{:S(2)}) async-start(), calls=%async_computation.21 | async-start | bytes 1474560 | tf_op jit(solution)/shard_map/reduce_scatter | solution.py:314
  311.3 3.4 copy-start.13
  311.3 92.8 %reduce-scatter.27.cloned.1.call-start = ((), (), s32[]{:S(2)}) async-start(), calls=%async_computation.20 | async-start | bytes 1474560 | tf_op jit(solution)/shard_map/reduce_scatter | solution.py:311
  314.7 109.3 %reduce-scatter.25.cloned.1.call-start = ((), (), s32[]{:S(2)}) async-start(), calls=%async_computation.19 | async-start | bytes 491520 | tf_op jit(solution)/shard_map/reduce_scatter | solution.py:308
  315.9 26.8 %copy-start.2 = (bf16[512,768]{1,0:T(8,128)(2,1)S(1)}, bf16[512,768]{1,0:T(8,128)(2,1)}, u32[]{:S(2)}) copy-start(bf16[512,768]{1,0:T(8,128)(2,1)} %copy-done.1) | copy-start | bytes 2359300
  315.9 139.6 %reduce-scatter.23.cloned.1.call-start = ((), (), s32[]{:S(2)}) async-start(), calls=%async_computation.18 | async-start | bytes 1474560 | tf_op jit(solution)/shard_map/reduce_scatter | solution.py:305
  345.8 110.1 %copy-start.17 = (bf16[512,192]{0,1:T(8,128)(2,1)S(1)}, bf16[512,192]{0,1:T(8,128)(2,1)}, u32[]{:S(2)}) copy-start(bf16[512,192]{0,1:T(8,128)(2,1)} %reduce-scatter.19.cloned.1.call-done) | copy-start | bytes 589828
  345.8 110.1 %copy-start.18 = (bf16[512,192]{0,1:T(8,128)(2,1)S(1)}, bf16[512,192]{0,1:T(8,128)(2,1)}, u32[]{:S(2)}) copy-start(bf16[512,192]{0,1:T(8,128)(2,1)} %reduce-scatter.17.cloned.1.call-done) | copy-start | bytes 589828
  345.8 160.1 %all-reduce.11.cloned.1.call-start = ((), (), s32[]{:S(2)}) async-start(), calls=%async_computation.22 | async-start | bytes 1966080 | tf_op jit(solution)/shard_map/psum | solution.py:319
  455.6 56.5 %reduce-scatter.21.cloned.1.call-start = ((), (), s32[]{:S(2)}) async-start(), calls=%async_computation.17 | async-start | bytes 1966080 | tf_op jit(solution)/shard_map/reduce_scatter | solution.py:33
  457.8 2.3 copy-start.20
  457.8 2.3 copy-start.21
  457.8 2.3 copy-start.22
  459.9 52.1 %copy-start.5 = (f32[128,768]{1,0:T(8,128)S(1)}, f32[128,768]{1,0:T(8,128)}, u32[]{:S(2)}) copy-start(f32[128,768]{1,0:T(8,128)} %get-tuple-element.144) | copy-start | bytes 1179652
  505.9 5.3 %copy-start.15 = (bf16[192,768]{1,0:T(8,128)(2,1)S(1)}, bf16[192,768]{1,0:T(8,128)(2,1)}, u32[]{:S(2)}) copy-start(bf16[192,768]{1,0:T(8,128)(2,1)} %get-tuple-element.137) | copy-start | bytes 884740
  (6 other events, 4.8 us)
Sparse Core Ops, SparseCore 0:
  112.5 39.5 reduce-scatter.10
  186.1 31.8 reduce-scatter.12
  236.1 32.6 reduce-scatter.14
  455.7 21.4 all-reduce.10
  480.1 31.4 reduce-scatter.20
Sparse Core Ops, SparseCore 1:
  114.4 37.2 all-gather.3
  153.1 29.4 all-gather.5
  295.8 22.0 reduce-scatter.18
  320.2 22.5 reduce-scatter.16
  345.0 28.8 reduce-scatter.28
  376.2 27.8 reduce-scatter.26
  406.8 17.2 reduce-scatter.24
  426.3 29.2 reduce-scatter.22
where the time goes:
time: 525 us; the launch traced here: 521 us
  waiting for transfers between devices  233 us (44%)
  blocking collectives  161 us (31%)
  matrix products  61 us (12%)
  other arithmetic  26.5 us (5%)
  local copies, waits for them, and re-layouts  20.7 us (4%)
  between operations  17.3 us (3%)
    reduce_scatter x4, waiting for transfers between devices, row_sum(): lax.psum_scatter(lax.dot_general(source, weight, (((1,), (1,)), ((), ()))...  87.9 us
    psum x1, blocking collectives, on_device(): lax.psum((attn_b_full, expand_b_full, mixer_b_part, gain_one_part, shift_...  40.6 us
    all_gather x4, blocking collectives, gather_rows(): return lax.all_gather(shard_in, 'row', axis=0, tiled=True)  37.9 us
    reduce_scatter x1, waiting for transfers between devices, on_device(): lax.psum_scatter(grad_attn_w.astype(jnp.bfloat16), 'col', scatter_dimensi...  31.6 us
    reduce_scatter x1, waiting for transfers between devices, on_device(): lax.psum_scatter(grad_expand_w.astype(jnp.bfloat16), 'col', scatter_dimen...  30.2 us
    reduce_scatter x1, waiting for transfers between devices, on_device(): lax.psum_scatter(grad_reduce_w.astype(jnp.bfloat16), 'col', scatter_dimen...  28 us
    all_gather x1, blocking collectives, on_device(): lax.all_gather(w_attn, 'col', axis=0, tiled=True)  27.1 us
    reduce_scatter x1, waiting for transfers between devices, on_device(): lax.psum_scatter(grad_keys.reshape(seq_slots, feat_here).astype(jnp.bfloa...  21.8 us
  transfers between devices with their start and end apart: 13, of which 9 were waited for; matrix products, arithmetic and copies ran while one was open for 10% of the time, Pallas kernels for 0%

commit v1 on v0

v1 whole, which is shorter than its diff:
```python
import functools
from types import SimpleNamespace

import jax
import jax.numpy as jnp
from jax import lax
from jax.experimental import pallas as pl
from jax.experimental.pallas import tpu as pltpu
from jax.sharding import PartitionSpec as P

D = 768
H = 12
EPSILON = 1e-12
NEGATIVE = -1000000000.0
MESH = pl.DeviceIdType.MESH
F32 = jnp.float32
BF16 = jnp.bfloat16


def dot_nn(left_in, right_in):
    return lax.dot_general(
        left_in, right_in, (((1,), (0,)), ((), ())), preferred_element_type=F32
    )


def dot_nt(left_in, right_in):
    return lax.dot_general(
        left_in, right_in, (((1,), (1,)), ((), ())), preferred_element_type=F32
    )


def turned(values):
    return values.astype(F32).T


def normalize(values):
    row_mean = jnp.mean(values, 1, keepdims=True)
    centered = values - row_mean
    row_var = jnp.mean(centered * centered, 1, keepdims=True)
    row_scale = lax.rsqrt(row_var + EPSILON)
    return centered * row_scale, row_scale


def normalize_back(upstream, normed, row_scale, gain_vec):
    scaled = upstream * gain_vec
    mean_plain = jnp.mean(scaled, 1, keepdims=True)
    mean_cross = jnp.mean(scaled * normed, 1, keepdims=True)
    return row_scale * (scaled - mean_plain - normed * mean_cross)


def column_sum(values):
    return jnp.sum(values, 0, keepdims=True)


class Slots:
    def __init__(self):
        self.base = {}
        self.total = 0

    def add(self, name, count):
        self.base[name] = self.total
        self.total += count


def slots_of(R, C):
    slots = Slots()
    for name in ("x", "mix", "hid", "red", "gr", "gh", "gm", "dx", "gv_row"):
        slots.add(name, R)
    for name in ("vec", "gv_col", "ab_col", "kv_right", "kv_left", "dkv_right", "dkv_left"):
        slots.add(name, C)
    for name in ("w1", "w2", "w3"):
        slots.add(name, C)
        slots.add(name + "_dp", C)
        slots.add("d" + name, C)
        slots.add("d" + name + "_dp", 1)
        slots.add("d" + name + "_out", 1)
    for name in ("gv_dp", "ab_dp"):
        slots.add(name, 1)
    return slots


def layer_kernel(dims, names, *refs):
    e = SimpleNamespace(**dict(zip(names, refs)))
    R, C, T, S, F, U, RB = dims.R, dims.C, dims.T, dims.S, dims.F, dims.U, dims.RB
    NH, HS, N1 = dims.NH, dims.HS, dims.N1
    slots = slots_of(R, C)
    me_d = lax.axis_index("dp")
    me_r = lax.axis_index("row")
    me_c = lax.axis_index("col")

    def to_row(step):
        return {"row": lax.rem(me_r + step, R)}

    def to_col(step):
        return {"col": lax.rem(me_c + step, C)}

    partner = {"dp": 1 - me_d}

    def copy(src, dst, family, at, where):
        number = slots.base[family] + at
        return pltpu.make_async_remote_copy(
            src_ref=src,
            dst_ref=dst,
            send_sem=e.send_sems.at[number],
            recv_sem=e.recv_sems.at[number],
            device_id=where,
            device_id_type=MESH,
        )

    barrier = pltpu.get_barrier_semaphore()
    pl.semaphore_signal(barrier, inc=1, device_id=partner, device_id_type=MESH)
    for i in range(1, R):
        pl.semaphore_signal(barrier, inc=1, device_id=to_row(i), device_id_type=MESH)
    for i in range(1, C):
        pl.semaphore_signal(barrier, inc=1, device_id=to_col(i), device_id_type=MESH)
    e.xg[me_r] = turned(e.x_t[...]).astype(BF16)
    pl.semaphore_wait(barrier, 1 + (R - 1) + (C - 1))

    def w_slot(ref, c):
        if dims.flat:
            return ref.at[pl.ds(pl.multiple_of(c * RB, RB), RB)]
        return ref.at[c]

    def half_of(width, d):
        return pl.ds(pl.multiple_of(d * (width // 2), width // 2), width // 2)

    def weight_copy(name, own, full, width, i):
        mine = half_of(width, me_d)
        return copy(own.at[:, mine], w_slot(full, me_c).at[:, mine], name, i, to_col(i))

    def weight_pass(name, full, width, i):
        mine = half_of(width, me_d)
        there = w_slot(full, lax.rem(me_c - i + C, C)).at[:, mine]
        return copy(there, there, name + "_dp", i, partner)

    def weight_start(name, own, full, width):
        for i in range(1, C):
            weight_copy(name, own, full, width, i).start()
        w_slot(full, me_c)[...] = own[...]

    def weight_share(name, own, full, width):
        for i in range(1, C):
            weight_copy(name, own, full, width, i).wait_recv()
            weight_pass(name, full, width, i).start()

    def weight_end(name, own, full, flat, width):
        for i in range(1, C):
            weight_pass(name, full, width, i).wait_recv()
        if not dims.flat:
            flat[...] = full[...].astype(F32).reshape(C * RB, width).astype(BF16)

    def weight_close(name, own, full, width):
        for i in range(1, C):
            weight_copy(name, own, full, width, i).wait_send()
            weight_pass(name, full, width, i).wait_send()

    w1 = ("w1", e.w1, e.w1g, N1)
    w2 = ("w2", e.w2, e.w2g, U)
    w3 = ("w3", e.w3, e.w3g, U)
    w1f = e.w1g if dims.flat else e.w1f
    w2f = e.w2g if dims.flat else e.w2f
    w3f = e.w3g if dims.flat else e.w3f

    def x_copy(i):
        return copy(e.xg.at[me_r], e.xg.at[me_r], "x", i, to_row(i))

    def vec_copy(i):
        return copy(e.vec, e.vecr.at[i], "vec", i, to_col(i))

    for i in range(1, R):
        x_copy(i).start()
    weight_start(*w1)
    for i in range(1, C):
        vec_copy(i).start()
    length = e.length[0]

    weight_share(*w1)
    weight_end("w1", e.w1, e.w1g, w1f, N1)

    def project(i):
        rb = lax.rem(me_r - i + R, R)
        if i:
            x_copy(i).wait_recv()
        tokens = pl.ds(pl.multiple_of(rb * T, T), T)
        block = e.xg[rb]
        proj = dot_nn(block, w1f[:, : 3 * F])
        q = (proj[:, :F] + e.b_attn[0:1, :]).astype(BF16).astype(F32) * (HS ** (-0.5))
        k = proj[:, F : 2 * F]
        v = proj[:, 2 * F :] + e.b_attn[1:2, :]
        e.kv[me_c, pl.ds(0, F), tokens] = k.T.astype(BF16)
        e.kv[me_c, pl.ds(F, F), tokens] = v.T.astype(BF16)
        e.q_t[:, tokens] = q.T.astype(BF16)
        for h in range(NH):
            e.q_h[h, tokens, :] = q[:, h * HS : (h + 1) * HS].astype(BF16)
        e.x_rows_t[:, tokens] = turned(block).astype(BF16)

    for i in range(R):
        project(i)

    right = {"col": lax.rem(me_c + 1, C)}
    left = {"col": lax.rem(me_c + C - 1, C)}

    def kv_right(b):
        return copy(e.kv.at[b], e.kv.at[b], "kv_right", b, right)

    def kv_left(b):
        return copy(e.kv.at[b], e.kv.at[b], "kv_left", b, left)

    def key_valid(b):
        lane = lax.broadcasted_iota(jnp.int32, (1, S), 1)
        return (lane // T * (T * C) + b * T + lane % T) < length

    TQ = dims.TQ
    e.top[...] = jnp.full(e.top.shape, -3e38, F32)
    e.total[...] = jnp.zeros(e.total.shape, F32)
    e.acc[...] = jnp.zeros(e.acc.shape, F32)

    def attend(b):
        valid = key_valid(b)

        def tile(t, carry):
            rows = pl.ds(pl.multiple_of(t * TQ, TQ), TQ)
            for h in range(NH):
                keys = e.kv[b, h * HS : (h + 1) * HS, :]
                values = e.kv[b, F + h * HS : F + (h + 1) * HS, :]
                scores = dot_nn(e.q_h[h, rows, :], keys)
                scores = jnp.where(valid, scores, NEGATIVE)
                old = e.top[h, rows, :]
                new = jnp.maximum(old, jnp.max(scores, 1, keepdims=True))
                shrink = jnp.exp(old - new)
                probs = jnp.exp(scores - new)
                e.top[h, rows, :] = new
                e.total[h, rows, :] = shrink * e.total[h, rows, :] + jnp.sum(
                    probs, 1, keepdims=True
                )
                e.acc[h, rows, :] = shrink * e.acc[h, rows, :] + dot_nt(
                    probs.astype(BF16), values
                )
            return carry

        lax.fori_loop(0, S // TQ, tile, 0)

    @pl.when(me_c < C - 1)
    def _():
        kv_right(me_c).start()

    @pl.when(me_c > 0)
    def _():
        kv_left(me_c).start()

    attend(me_c)

    def kv_step(s, carry):
        from_left = me_c - s
        from_right = me_c + s

        @pl.when(from_left >= 0)
        def _():
            kv_right(from_left).wait_recv()

            @pl.when(me_c < C - 1)
            def _():
                kv_right(from_left).start()

        @pl.when(from_right < C)
        def _():
            kv_left(from_right).wait_recv()

            @pl.when(me_c > 0)
            def _():
                kv_left(from_right).start()

        @pl.when(from_left >= 0)
        def _():
            attend(from_left)

        @pl.when(from_right < C)
        def _():
            attend(from_right)

        return carry

    lax.fori_loop(1, C, kv_step, 0)

    def kv_close(b, carry):
        @pl.when((b <= me_c) & (me_c < C - 1))
        def _():
            kv_right(b).wait_send()

        @pl.when((b >= me_c) & (me_c > 0))
        def _():
            kv_left(b).wait_send()

        return carry

    lax.fori_loop(0, C, kv_close, 0)
    weight_start(*w2)
    weight_start(*w3)

    for h in range(NH):
        inverse = 1.0 / e.total[h]
        e.total[h] = inverse
        context = e.acc[h] * inverse
        e.acc[h] = context
        e.ctx[:, h * HS : (h + 1) * HS] = context.astype(BF16)

    vec = e.vec[...]
    for i in range(1, C):
        vec_copy(i).wait_recv()
        vec = vec + e.vecr[i]
    e.vecs[...] = vec

    def vector(at):
        return e.vecs[at : at + 1, :]

    def blk_rows(rb):
        return pl.ds(pl.multiple_of(rb * T, T), T)

    def sum_copy(family, i, where):
        return copy(e.stage.at[i], e.landing.at[slots.base[family] // R, i], family, i, where)

    for i in list(range(1, R)) + [0]:
        rb = lax.rem(me_r + i, R)
        part = dot_nt(e.ctx[blk_rows(rb), :], w1f[:, 3 * F :])
        if i:
            e.stage[0, i] = part.astype(BF16)
            copy(e.stage.at[0, i], e.landing.at[0, i], "mix", i, to_row(i)).start()
        else:
            e.own[...] = part

    def collect(number, family):
        total = e.own[...]
        for i in range(1, R):
            copy(e.stage.at[number, i], e.landing.at[number, i], family, i, to_row(i)).wait_recv()
            total = total + e.landing[number, i].astype(F32)
        return total

    first_sum = turned(e.x_t[...]) + collect(0, "mix") + vector(0)
    normed, scale = normalize(first_sum)
    hidden = normed * vector(1) + vector(2)
    e.n1[...] = normed
    e.r1[...] = scale
    e.hidden[...] = hidden
    e.hid_g[me_r] = hidden.astype(BF16)

    def share(ref, family, i):
        return copy(ref.at[me_r], ref.at[me_r], family, i, to_row(i))

    for i in range(1, R):
        share(e.hid_g, "hid", i).start()
    weight_share(*w2)
    weight_end("w2", e.w2, e.w2g, w2f, U)

    def spread(number, family, part, i, rb):
        if i:
            e.stage[number, i] = part.astype(BF16)
            copy(
                e.stage.at[number, i], e.landing.at[number, i], family, i, to_row(R - i)
            ).start()
        else:
            e.own[...] = part

    for i in range(R):
        rb = lax.rem(me_r - i + R, R)
        if i:
            share(e.hid_g, "hid", i).wait_recv()
        inner = dot_nn(e.hid_g[rb], w2f[...]) + e.b_expand[...]
        cdf = 0.5 * (1.0 + lax.erf(inner * (0.5**0.5)))
        active = (inner * cdf).astype(BF16)
        slope = cdf + inner * (jnp.exp(-0.5 * inner * inner) * 0.3989422804014327)
        e.active[blk_rows(rb), :] = active
        e.slope[blk_rows(rb), :] = slope
        if i == 0:
            weight_share(*w3)
            weight_end("w3", e.w3, e.w3g, w3f, U)
        spread(1, "red", dot_nt(e.active[blk_rows(rb), :], w3f[...]), i, rb)
    for i in range(R):
        rb = lax.rem(me_r - i + R, R)
        e.hid_t[:, blk_rows(rb)] = turned(e.hid_g[rb]).astype(BF16)

    second_sum = e.hidden[...] + collect(1, "red") + vector(3)
    normed, scale = normalize(second_sum)
    slot = lax.broadcasted_iota(jnp.int32, (T, 1), 0) + (me_r * (T * C) + me_c * T)
    row_valid = (slot < length).astype(F32)
    upstream = turned(e.out_grad[...]) * row_valid
    g_second = normalize_back(upstream, normed, scale, vector(4))
    g_reduced = g_second.astype(BF16)
    e.gr_g[me_r] = g_reduced
    for i in range(1, R):
        share(e.gr_g, "gr", i).start()
    e.layer_out[...] = ((normed * vector(4) + vector(5)) * row_valid).T.astype(BF16)
    e.g_second[...] = g_second
    e.gv[4:5, :] = column_sum(upstream * normed)
    e.gv[5:6, :] = column_sum(upstream)
    e.gv[3:4, :] = column_sum(g_reduced.astype(F32))
    e.gv[7:8, :] = jnp.zeros((1, D), F32)

    unit_sum = jnp.zeros((1, U), F32)
    for i in range(R):
        rb = lax.rem(me_r - i + R, R)
        if i:
            share(e.gr_g, "gr", i).wait_recv()
        g_active = dot_nn(e.gr_g[rb], w3f[...]).astype(BF16).astype(F32)
        g_inner = (g_active * e.slope[blk_rows(rb), :]).astype(BF16)
        e.g_inner[blk_rows(rb), :] = g_inner
        unit_sum = unit_sum + column_sum(g_inner.astype(F32))
        spread(2, "gh", dot_nt(e.g_inner[blk_rows(rb), :], w2f[...]), i, rb)
    e.gu[0:1, :] = unit_sum
    for i in range(R):
        rb = lax.rem(me_r - i + R, R)
        e.gr_t[:, blk_rows(rb)] = turned(e.gr_g[rb]).astype(BF16)

    TR = dims.TR

    def other_copy(name, k):
        return copy(e.dw_out.at[k], e.dw_in.at[k], name + "_dp", 0, partner)

    def weight_product(k, lhs_ref, rhs_of, transposed):
        product = dot_nt if transposed else dot_nn

        def tile(t, carry):
            rows = pl.ds(pl.multiple_of(t * TR, TR), TR)
            lhs = lhs_ref[rows, :]
            e.dw_out[k, rows, :] = product(lhs, rhs_of(1 - me_d)).astype(BF16)
            return carry

        def own_tile(t, carry):
            rows = pl.ds(pl.multiple_of(t * TR, TR), TR)
            lhs = lhs_ref[rows, :]
            e.dw_own[rows, :] = product(lhs, rhs_of(me_d))
            return carry

        return tile, own_tile

    def d_copy(name, k, i):
        return copy(e.dw_stage.at[k, lax.rem(me_c + i, C)], e.dw_land.at[k, i], name, i, to_col(i))

    def weight_grad(name, k, lhs_ref, rhs_of, transposed):
        tile, own_tile = weight_product(k, lhs_ref, rhs_of, transposed)
        lax.fori_loop(0, D // TR, tile, 0)
        other_copy(name, k).start()
        lax.fori_loop(0, D // TR, own_tile, 0)
        other_copy(name, k).wait_recv()

    def weight_send(name, k):
        if dims.flat:
            for c in range(C):
                rows = slice(c * RB, (c + 1) * RB)
                total = e.dw_own[rows, :] + e.dw_in[k, rows, :].astype(F32)
                e.dw_stage[k, c] = total.astype(BF16)
        else:
            total = e.dw_own[...] + e.dw_in[k].astype(F32)
            e.dw_stage[k] = total.reshape(C, RB, N1 // 2).astype(BF16)
        for i in range(1, C):
            d_copy(name, k, i).start()

    def result_copy(name, k):
        mine = half_of(N1, me_d)
        return copy(e.dw.at[k, :, mine], e.dw.at[k, :, mine], name + "_out", 0, partner)

    def weight_collect(name, k):
        total = e.dw_stage[k, me_c].astype(F32)
        for i in range(1, C):
            d_copy(name, k, i).wait_recv()
            total = total + e.dw_land[k, i].astype(F32)
        e.dw[k, :, half_of(N1, me_d)] = total
        result_copy(name, k).start()

    weight_grad(
        "dw3", 2, e.gr_t, lambda d: e.active[:, half_of(U, d)], False
    )
    weight_send("dw3", 2)
    weight_grad(
        "dw2", 1, e.hid_t, lambda d: e.g_inner[:, half_of(U, d)], False
    )
    weight_send("dw2", 1)

    g_hidden = collect(2, "gh") + e.g_second[...]
    normed = e.n1[...]
    g_first = normalize_back(g_hidden, normed, e.r1[...], vector(1))
    g_mixed = g_first.astype(BF16)
    for i in range(1, R):
        share(e.hid_g, "hid", i).wait_send()
    e.hid_g[me_r] = g_mixed
    for i in range(1, R):
        share(e.hid_g, "gm", i).start()
    e.g_first[...] = g_first
    e.gv[1:2, :] = column_sum(g_hidden * normed)
    e.gv[2:3, :] = column_sum(g_hidden)
    e.gv[0:1, :] = column_sum(g_mixed.astype(F32))
    e.gv[6:7, :] = jnp.zeros((1, D), F32)

    def gv_dp():
        return copy(e.gall.at[0], e.gall.at[1], "gv_dp", 0, partner)

    e.gall[0, 0:8, :D] = e.gv[...]
    e.gall[0, 8:16, :U] = jnp.broadcast_to(e.gu[0:1, :], (8, U))
    gv_dp().start()

    for i in range(R):
        rb = lax.rem(me_r - i + R, R)
        if i:
            share(e.hid_g, "gm", i).wait_recv()
        rows = blk_rows(rb)
        g_context = dot_nn(e.hid_g[rb], w1f[:, 3 * F :]).astype(BF16).astype(F32)
        e.gc_t[:, rows] = g_context.T.astype(BF16)
        for h in range(NH):
            part = g_context[:, h * HS : (h + 1) * HS]
            e.gc_h[h, rows, :] = part.astype(BF16)
            e.inner_sum[h, rows, :] = jnp.sum(part * e.acc[h, rows, :], 1, keepdims=True)
        e.gr_t[:, rows] = turned(e.hid_g[rb]).astype(BF16)

    gv_dp().wait_recv()
    e.gall[2] = e.gall[0] + e.gall[1]

    def gv_col(i):
        return copy(e.gall.at[2], e.gcol.at[i], "gv_col", i, to_col(i))

    for i in range(1, C):
        gv_col(i).start()

    e.dq[...] = jnp.zeros(e.dq.shape, F32)

    def attend_back(b):
        valid = key_valid(b)
        for h in range(NH):
            krows = slice(h * HS, (h + 1) * HS)
            vrows = slice(F + h * HS, F + (h + 1) * HS)

            def tile(t, carry):
                d_keys, d_values = carry
                rows = pl.ds(pl.multiple_of(t * TQ, TQ), TQ)
                keys = e.kv[b, krows, :]
                values = e.kv[b, vrows, :]
                scores = dot_nn(e.q_h[h, rows, :], keys)
                scores = jnp.where(valid, scores, NEGATIVE)
                probs = jnp.exp(scores - e.top[h, rows, :]) * e.total[h, rows, :]
                g_weights = dot_nn(e.gc_h[h, rows, :], values)
                g_scores = (probs * (g_weights - e.inner_sum[h, rows, :])).astype(BF16)
                e.dq[h, rows, :] += dot_nt(g_scores, keys)
                d_keys = d_keys + dot_nn(e.q_t[krows, rows], g_scores)
                d_values = d_values + dot_nn(e.gc_t[krows, rows], probs.astype(BF16))
                return d_keys, d_values

            zero = jnp.zeros((HS, S), F32)
            d_keys, d_values = lax.fori_loop(0, S // TQ, tile, (zero, zero))
            e.dkv[krows, :] = d_keys
            e.dkv[vrows, :] = d_values

    NB = dims.NB

    def dkv_right(b):
        return copy(
            e.kv.at[b], e.dkv_in.at[0, lax.rem(C - 1 - b, NB)], "dkv_right", b, right
        )

    def dkv_left(b):
        return copy(e.kv.at[b], e.dkv_in.at[1, lax.rem(b, NB)], "dkv_left", b, left)

    def dkv_send(way, b):
        order = C - 1 - b if way == 0 else b
        if C - 1 > NB:

            @pl.when(order >= NB)
            def _():
                pl.semaphore_wait(e.credits.at[way], 1)

        (dkv_right if way == 0 else dkv_left)(b).start()

    def dkv_take(way, b):
        order = C - 1 - b if way == 0 else b
        (dkv_right if way == 0 else dkv_left)(b).wait_recv()
        e.dkv[...] += e.dkv_in[way, lax.rem(order, NB)].astype(F32)
        if C - 1 > NB:
            sends = C - me_c if way == 0 else me_c + 1

            @pl.when(order + NB < sends)
            def _():
                pl.semaphore_signal(
                    e.credits.at[way],
                    inc=1,
                    device_id=left if way == 0 else right,
                    device_id_type=MESH,
                )

    def dkv_step(s, carry):
        far_right = C - 1 - s
        far_left = s

        @pl.when(far_right > me_c)
        def _():
            attend_back(far_right)

            @pl.when(me_c > 0)
            def _():
                dkv_take(0, far_right)

            e.kv[far_right] = e.dkv[...].astype(BF16)
            dkv_send(0, far_right)

        @pl.when(far_left < me_c)
        def _():
            attend_back(far_left)

            @pl.when(me_c < C - 1)
            def _():
                dkv_take(1, far_left)

            e.kv[far_left] = e.dkv[...].astype(BF16)
            dkv_send(1, far_left)

        return carry

    lax.fori_loop(0, C - 1, dkv_step, 0)
    attend_back(me_c)

    for h in range(NH):
        e.dqkv[h * HS : (h + 1) * HS, :] = (e.dq[h] * (HS ** (-0.5))).T.astype(BF16)

    for i in range(1, C):
        gv_col(i).wait_recv()
    gsum = e.gall[2]
    for i in range(1, C):
        gsum = gsum + e.gcol[i]
    e.gsum[...] = gsum

    def gv_row(i):
        return copy(e.gsum.at[pl.ds(0, 8)], e.grow.at[i], "gv_row", i, to_row(i))

    for i in range(1, R):
        gv_row(i).start()

    @pl.when(me_c > 0)
    def _():
        dkv_take(0, me_c)

    @pl.when(me_c < C - 1)
    def _():
        dkv_take(1, me_c)

    e.dqkv[F : 3 * F, :] = e.dkv[...].astype(BF16)

    for i in list(range(1, R)) + [0]:
        rb = lax.rem(me_r + i, R)
        part = dot_nn(w1f[:, : 3 * F], e.dqkv[:, blk_rows(rb)])
        if i:
            e.dx_stage[i] = part.astype(BF16)
            copy(e.dx_stage.at[i], e.dx_land.at[i], "dx", i, to_row(i)).start()
        else:
            e.dx_own[...] = part

    def packed_tile(t, carry):
        rows = pl.ds(pl.multiple_of(t * TR, TR), TR)
        e.dw1[rows, : 3 * F] = dot_nt(e.x_rows_t[rows, :], e.dqkv[...])
        e.dw1[rows, 3 * F :] = dot_nn(e.gr_t[rows, :], e.ctx[...])
        return carry

    lax.fori_loop(0, D // TR, packed_tile, 0)
    e.dw_out[0] = e.dw1[:, half_of(N1, 1 - me_d)].astype(BF16)
    other_copy("dw1", 0).start()
    sums = dot_nt(jnp.ones((8, S), BF16), e.dqkv[...])
    e.ab[0] = sums

    def ab_dp():
        return copy(e.ab.at[0], e.ab.at[1], "ab_dp", 0, partner)

    def ab_col(i):
        return copy(e.ab.at[2], e.abcol.at[i], "ab_col", i, to_col(i))

    ab_dp().start()
    e.dw_own[...] = e.dw1[:, half_of(N1, me_d)]
    other_copy("dw1", 0).wait_recv()
    weight_send("dw1", 0)
    ab_dp().wait_recv()
    e.ab[2] = e.ab[0] + e.ab[1]
    for i in range(1, C):
        ab_col(i).start()

    weight_collect("dw3", 2)
    weight_collect("dw2", 1)

    total = e.dx_own[...] + e.g_first[...].T
    for i in range(1, R):
        copy(e.dx_stage.at[i], e.dx_land.at[i], "dx", i, to_row(i)).wait_recv()
        total = total + e.dx_land[i].astype(F32)
    e.grad_input[...] = total

    vsum = e.gsum[0:8, :D]
    for i in range(1, R):
        gv_row(i).wait_recv()
        vsum = vsum + e.grow[i][:, :D]
    e.gvec[...] = vsum
    e.gunit[...] = e.gsum[8:16, :U]
    asum = e.ab[2]
    for i in range(1, C):
        ab_col(i).wait_recv()
        asum = asum + e.abcol[i]
    e.gab[...] = asum
    weight_collect("dw1", 0)
    for name, k in (("dw3", 2), ("dw2", 1), ("dw1", 0)):
        result_copy(name, k).wait_recv()

    weight_close(*w1)
    weight_close(*w2)
    weight_close(*w3)
    for i in range(1, R):
        x_copy(i).wait_send()
        copy(e.stage.at[0, i], e.landing.at[0, i], "mix", i, to_row(i)).wait_send()
        copy(e.stage.at[1, i], e.landing.at[1, i], "red", i, to_row(i)).wait_send()
        share(e.gr_g, "gr", i).wait_send()
        copy(e.stage.at[2, i], e.landing.at[2, i], "gh", i, to_row(i)).wait_send()
        share(e.hid_g, "gm", i).wait_send()
        copy(e.dx_stage.at[i], e.dx_land.at[i], "dx", i, to_row(i)).wait_send()
        gv_row(i).wait_send()
    gv_dp().wait_send()
    ab_dp().wait_send()
    for i in range(1, C):
        vec_copy(i).wait_send()
        gv_col(i).wait_send()
        ab_col(i).wait_send()
    for name, k in (("dw3", 2), ("dw2", 1), ("dw1", 0)):
        other_copy(name, k).wait_send()
        for i in range(1, C):
            d_copy(name, k, i).wait_send()
        result_copy(name, k).wait_send()

    def dkv_close(s, carry):
        @pl.when(C - 1 - s > me_c)
        def _():
            dkv_right(C - 1 - s).wait_send()

        @pl.when(s < me_c)
        def _():
            dkv_left(s).wait_send()

        return carry

    lax.fori_loop(0, C - 1, dkv_close, 0)


def run_layer(x_t, length, w1, w2, w3, vec, b_attn, b_expand, out_grad):
    R = lax.axis_size("row")
    C = lax.axis_size("col")
    T = x_t.shape[1]
    S = T * R
    F = b_attn.shape[1]
    U = w2.shape[1]
    RB = w1.shape[0]
    HS = D // H
    dims = SimpleNamespace(
        R=R, C=C, T=T, S=S, F=F, U=U, RB=RB, HS=HS, NH=F // HS, N1=4 * F,
        flat=RB % 16 == 0, TQ=min(256, S), TR=256, NB=min(C, 4),
    )
    N1 = dims.N1
    NH = dims.NH
    slots = slots_of(R, C)
    wide = max(D, U)
    w_shape = (lambda n: (C * RB, n)) if dims.flat else (lambda n: (C, RB, n))
    inputs = dict(
        x_t=x_t, length=length, w1=w1, w2=w2, w3=w3, vec=vec, b_attn=b_attn,
        b_expand=b_expand, out_grad=out_grad,
    )
    outputs = dict(
        layer_out=((D, T), BF16),
        grad_input=((D, T), F32),
        dw=((3, RB, N1), F32),
        gvec=((8, D), F32),
        gunit=((8, U), F32),
        gab=((8, 3 * F), F32),
    )
    scratch = dict(
        xg=((R, T, D), BF16),
        w1g=(w_shape(N1), BF16),
        w2g=(w_shape(U), BF16),
        w3g=(w_shape(U), BF16),
        vecr=((C, 8, D), F32),
        vecs=((8, D), F32),
        kv=((C, 2 * F, S), BF16),
        q_t=((F, S), BF16),
        q_h=((NH, S, HS), BF16),
        x_rows_t=((D, S), BF16),
        top=((NH, S, 1), F32),
        total=((NH, S, 1), F32),
        acc=((NH, S, HS), F32),
        ctx=((S, F), BF16),
        stage=((3, R, T, D), BF16),
        landing=((3, R, T, D), BF16),
        own=((T, D), F32),
        n1=((T, D), F32),
        r1=((T, 1), F32),
        hidden=((T, D), F32),
        hid_g=((R, T, D), BF16),
        active=((S, U), BF16),
        slope=((S, U), F32),
        hid_t=((D, S), BF16),
        g_second=((T, D), F32),
        gr_g=((R, T, D), BF16),
        gr_t=((D, S), BF16),
        g_inner=((S, U), BF16),
        gv=((8, D), F32),
        gu=((8, U), F32),
        gall=((3, 16, wide), F32),
        gcol=((C, 16, wide), F32),
        gsum=((16, wide), F32),
        grow=((R, 8, wide), F32),
        dw_out=((3, D, N1 // 2), BF16),
        dw_in=((3, D, N1 // 2), BF16),
        dw_own=((D, N1 // 2), F32),
        dw_stage=((3, C, RB, N1 // 2), BF16),
        dw_land=((3, C, RB, N1 // 2), BF16),
        dw1=((D, N1), F32),
        g_first=((T, D), F32),
        gc_t=((F, S), BF16),
        gc_h=((NH, S, HS), BF16),
        inner_sum=((NH, S, 1), F32),
        dq=((NH, S, HS), F32),
        dkv=((2 * F, S), F32),
        dkv_in=((2, dims.NB, 2 * F, S), BF16),
        dqkv=((3 * F, S), BF16),
        dx_stage=((R, D, T), BF16),
        dx_land=((R, D, T), BF16),
        dx_own=((D, T), F32),
        ab=((3, 8, 3 * F), F32),
        abcol=((C, 8, 3 * F), F32),
    )
    if not dims.flat:
        scratch.update(
            w1f=((C * RB, N1), BF16), w2f=((C * RB, U), BF16), w3f=((C * RB, U), BF16)
        )
    names = list(inputs) + list(outputs) + list(scratch) + ["send_sems", "recv_sems", "credits"]
    vmem = pl.BlockSpec(memory_space=pltpu.VMEM)
    in_specs = [
        pl.BlockSpec(memory_space=pltpu.SMEM) if name == "length" else vmem for name in inputs
    ]
    results = pl.pallas_call(
        functools.partial(layer_kernel, dims, names),
        out_shape=[jax.ShapeDtypeStruct(s, t) for s, t in outputs.values()],
        in_specs=in_specs,
        out_specs=[vmem] * len(outputs),
        scratch_shapes=[pltpu.VMEM(s, t) for s, t in scratch.values()]
        + [pltpu.SemaphoreType.DMA((slots.total,)), pltpu.SemaphoreType.DMA((slots.total,))]
        + [pltpu.SemaphoreType.REGULAR((2,))],
        compiler_params=pltpu.CompilerParams(
            collective_id=0, has_side_effects=True, vmem_limit_bytes=63 * 2**20
        ),
        name="layer",
    )(*inputs.values())
    return dict(zip(outputs, results))


def on_device(
    layer_in,
    lengths,
    w_attn,
    b_attn,
    w_mixer,
    b_mixer,
    gain_one,
    shift_one,
    w_expand,
    b_expand,
    w_reduce,
    b_reduce,
    gain_two,
    shift_two,
    out_grad,
):
    col_index = lax.axis_index("col")
    rows = w_mixer.shape[0]
    feats = w_mixer.shape[1]
    w1 = jnp.concatenate([w_attn.reshape(rows, 3 * feats), w_mixer], 1)
    own = jnp.stack([b_mixer, gain_one, shift_one, b_reduce, gain_two, shift_two]).astype(F32)
    vec = lax.dynamic_update_slice(jnp.zeros((8, D), F32), own, (0, col_index * rows))
    out = run_layer(
        layer_in,
        lengths,
        w1,
        w_expand,
        w_reduce,
        vec,
        b_attn.astype(F32),
        b_expand.astype(F32)[None],
        out_grad,
    )
    gvec = lax.dynamic_slice(out["gvec"], (0, col_index * rows), (8, rows))
    dw1 = out["dw"][0]
    gab = out["gab"]
    return (
        out["layer_out"],
        out["grad_input"],
        dw1[:, : 3 * feats].reshape(rows, 3, feats),
        jnp.stack([gab[0, :feats], gab[0, 2 * feats :]]),
        dw1[:, 3 * feats :],
        gvec[0],
        gvec[1],
        gvec[2],
        out["dw"][1],
        out["gunit"][0],
        out["dw"][2],
        gvec[3],
        gvec[4],
        gvec[5],
    )


def solution(mesh):
    return jax.shard_map(
        on_device,
        mesh=mesh,
        in_specs=(
            P(None, ("dp", "row", "col")),
            P("dp"),
            P("col", None, "row"),
            P(None, "row"),
            P("col", "row"),
            P("col"),
            P("col"),
            P("col"),
            P("col", "row"),
            P("row"),
            P("col", "row"),
            P("col"),
            P("col"),
            P("col"),
            P(None, ("dp", "row", "col")),
        ),
        out_specs=(
            P(None, ("dp", "row", "col")),
            P(None, ("dp", "row", "col")),
            P("col", None, "row"),
            P(None, "row"),
            P("col", "row"),
            P("col"),
            P("col"),
            P("col"),
            P("col", "row"),
            P("row"),
            P("col", "row"),
            P("col"),
            P("col"),
            P("col"),
        ),
        check_vma=False,
    )
```

time: 525 us -> 227 us (0.43)
  waiting for transfers between devices: 233 us -> 0 us
  Pallas kernels: 0 us -> 202 us
  blocking collectives: 161 us -> 0 us
  matrix products: 61 us -> 0 us
  other arithmetic: 26.5 us -> 3.55 us
  between operations: 17.3 us -> 1.35 us
    reduce_scatter x10 -> x0, waiting for transfers between devices: 219 us -> none  [the longest x4 87.9 us: row_sum(): lax.psum_scatter(lax.dot_general(source, weight, (((1,), (1,)), ((), ()))...]
    pallas_call x0 -> x1, Pallas kernels: none -> 202 us  [run_layer(): pl.pallas_call(functools.partial(layer_kernel, dims, names), out_shape=[j...]
    all_gather x8 -> x0, blocking collectives: 109 us -> none  [the longest x4 37.9 us: gather_rows(): return lax.all_gather(shard_in, 'row', axis=0, tiled=True)]
    dot_general x17 -> x0, matrix products: 54.1 us -> none  [the longest x4 9.34 us: outer_prod(): lax.dot_general(left_in, right_in, (((0,), (0,)), ((), ())), preferred_el...]
    psum x1 -> x0, blocking collectives: 40.6 us -> none  [on_device(): lax.psum((attn_b_full, expand_b_full, mixer_b_part, gain_one_part, shift_...]
    convert_element_type x15 -> x2, other arithmetic: 15.6 us -> 1.26 us  [the longest x1 1.26 us: on_device(): b_attn.astype(F32)]
    all_gather x2 -> x0, waiting for transfers between devices: 12.8 us -> none  [the longest x1 12.8 us: on_device(): lax.all_gather(w_reduce, 'col', axis=0, tiled=True)]
    unnamed x1 -> x0, blocking collectives: 11.6 us -> none
  transfers between devices with their start and end apart: 13 -> 0, of which waited for: 9 -> 0; matrix products, arithmetic and copies ran while one was open for 10% -> 0% of each run, Pallas kernels for 0% -> 0%
where the time goes in v1:
time: 227 us; the launch traced here: 224 us
  Pallas kernels  202 us (89%)
  local copies, waits for them, and re-layouts  16.2 us (7%)
  other arithmetic  3.55 us (2%)
    pallas_call x1, Pallas kernels, run_layer(): pl.pallas_call(functools.partial(layer_kernel, dims, names), out_shape=[j...  202 us

profile of v1, /device:TPU:25, one launch (start us, length us, event | category | flops | bytes accessed | tf_op | source)
XLA Modules:
  0.0 223.6 jit_solution(3105722434973559665)
XLA Ops:
  1.3 0.7 stack.24
  2.0 0.7 stack.25
  2.6 0.7 stack.26
  3.3 0.7 stack.27
  3.9 0.7 stack.28
  4.6 0.7 stack.29
  5.3 1.3 convert_element_type.8.refs_6_
  6.5 1.3 reshape.36.refs_7_
  7.8 0.6 dynamic_update_slice.3.refs_5_
  8.4 0.0 copy-start.2
  8.5 1.1 copy.31
  9.6 0.2 copy.32
  9.8 1.7 pad_maximum_fusion.refs_2_
  11.5 0.0 copy-done.2
  11.5 202.5 %layer.1 = (bf16[768,128]{1,0:T(8,128)(2,1)}, f32[768,128]{1,0:T(8,128)}, f32[3,192,768]{2,1,0:T(8,128)}, f32[8,768]{1,0:T(8,128)}, f32[8,768]{1,0:T(8,128)}, /*index=5*/f32[8,576]{1,0:T(8,128)}) custom-call(bf16[768,128]{1,0:T(8,128)(2,1)} %refs_0_.1, s32[1]{0:T(128)S(6)} %copy.38.refs_1_, bf16[192,768]{1,0:T(8,128)(2,1)} %pad_maximum_fusion.refs_2_, ...), custom_call_target="tpu_custom_call" | custom-call | tf_op jit(solution)/shard_map/layer/pallas_call | solution.py:835
  214.0 1.3 slice_reduce_fusion
  215.3 1.6 fusion
  216.9 0.6 pad_maximum_fusion.1
  217.5 2.5 %slice_bitcast_fusion = (f32[192,768]{1,0:T(8,128)}, f32[192,768]{1,0:T(8,128)}, f32[192,768]{1,0:T(8,128)S(1)}) fusion(f32[3,192,768]{2,1,0:T(8,128)} %get-tuple-element.22), kind=kLoop, calls=%fused_computation | loop fusion | bytes 3538944 | tf_op jit(solution)/shard_map/squeeze | solution.py:899
  220.0 0.0 copy-start.1
  220.0 0.8 slice.57
  220.8 0.0 copy-start
  220.9 0.2 copy.33
  221.1 1.1 copy.34
  222.2 0.0 copy-done.1
  222.2 0.7 copy.39
  222.8 0.0 copy-done
  222.8 0.7 copy.40
  (4 shorter events, 0.1 us)
Async XLA Ops:
  8.4 3.0 %copy-start.2 = (f32[8,768]{1,0:T(8,128)}, f32[8,768]{1,0:T(8,128)S(1)}, u32[]{:S(2)}) copy-start(f32[8,768]{1,0:T(8,128)S(1)} %dynamic_update_slice.3.refs_5_) | copy-start | bytes 73732
  220.0 2.1 copy-start.1
  220.8 2.0 copy-start

commit v2 on v1

--- a/solution.py
+++ b/solution.py
@@ -68,7 +68,7 @@
         slots.add(name, R)
     for name in ("vec", "gv_col", "ab_col", "kv_right", "kv_left", "dkv_right", "dkv_left"):
         slots.add(name, C)
-    for name in ("w1", "w2", "w3"):
+    for name in ("wkv", "wqm", "w2", "w3"):
         slots.add(name, C)
         slots.add(name + "_dp", C)
         slots.add("d" + name, C)
@@ -82,7 +82,7 @@
 def layer_kernel(dims, names, *refs):
     e = SimpleNamespace(**dict(zip(names, refs)))
     R, C, T, S, F, U, RB = dims.R, dims.C, dims.T, dims.S, dims.F, dims.U, dims.RB
-    NH, HS, N1 = dims.NH, dims.HS, dims.N1
+    NH, HS, HB = dims.NH, dims.HS, dims.HB
     slots = slots_of(R, C)
     me_d = lax.axis_index("dp")
     me_r = lax.axis_index("row")
@@ -114,88 +114,113 @@
     for i in range(1, C):
         pl.semaphore_signal(barrier, inc=1, device_id=to_col(i), device_id_type=MESH)
     e.xg[me_r] = turned(e.x_t[...]).astype(BF16)
+    e.wkv[:, :F] = e.w_attn[1]
+    e.wkv[:, F:] = e.w_attn[2]
+    e.wqm[:, :F] = e.w_attn[0]
+    e.wqm[:, F:] = e.w_mixer[...]
+    e.vecr[me_c] = e.small[0:8, :]
     pl.semaphore_wait(barrier, 1 + (R - 1) + (C - 1))
 
-    def w_slot(ref, c):
+    def w_rows(ref, c, d):
+        if not dims.flat:
+            return ref.at[c]
+        return ref.at[pl.ds(pl.multiple_of(c * RB + d * HB, HB), HB)]
+
+    def weight_copy(name, i):
+        own = getattr(e, name)
         if dims.flat:
-            return ref.at[pl.ds(pl.multiple_of(c * RB, RB), RB)]
-        return ref.at[c]
-
-    def half_of(width, d):
-        return pl.ds(pl.multiple_of(d * (width // 2), width // 2), width // 2)
-
-    def weight_copy(name, own, full, width, i):
-        mine = half_of(width, me_d)
-        return copy(own.at[:, mine], w_slot(full, me_c).at[:, mine], name, i, to_col(i))
-
-    def weight_pass(name, full, width, i):
-        mine = half_of(width, me_d)
-        there = w_slot(full, lax.rem(me_c - i + C, C)).at[:, mine]
+            own = own.at[pl.ds(pl.multiple_of(me_d * HB, HB), HB)]
+        return copy(own, w_rows(getattr(e, name + "_g"), me_c, me_d), name, i, to_col(i))
+
+    def weight_pass(name, i):
+        there = w_rows(getattr(e, name + "_g"), lax.rem(me_c - i + C, C), me_d)
         return copy(there, there, name + "_dp", i, partner)
 
-    def weight_start(name, own, full, width):
+    def weight_start(name, which=None):
         for i in range(1, C):
-            weight_copy(name, own, full, width, i).start()
-        w_slot(full, me_c)[...] = own[...]
-
-    def weight_share(name, own, full, width):
+            if which is None:
+                weight_copy(name, i).start()
+            else:
+                to = lax.rem(me_c + i, C)
+                inner = (to > 0) & (to < C - 1)
+                pl.when(inner if which == "inner" else jnp.logical_not(inner))(
+                    weight_copy(name, i).start
+                )
+
+    def weight_own(name):
+        full = getattr(e, name + "_g")
+        if dims.flat:
+            full[pl.ds(pl.multiple_of(me_c * RB, RB), RB), :] = getattr(e, name)[...]
+        else:
+            full[me_c] = getattr(e, name)[...]
+
+    def weight_share(name):
         for i in range(1, C):
-            weight_copy(name, own, full, width, i).wait_recv()
-            weight_pass(name, full, width, i).start()
-
-    def weight_end(name, own, full, flat, width):
+            weight_copy(name, i).wait_recv()
+            if dims.flat:
+                weight_pass(name, i).start()
+
+    def weight_end(name):
+        if dims.flat:
+            for i in range(1, C):
+                weight_pass(name, i).wait_recv()
+        else:
+            full = getattr(e, name + "_g")
+            flat = full[...].astype(F32).reshape(C * RB, full.shape[2])
+            getattr(e, name + "_f")[...] = flat.astype(BF16)
+
+    def weight_close(name):
         for i in range(1, C):
-            weight_pass(name, full, width, i).wait_recv()
-        if not dims.flat:
-            flat[...] = full[...].astype(F32).reshape(C * RB, width).astype(BF16)
-
-    def weight_close(name, own, full, width):
-        for i in range(1, C):
-            weight_copy(name, own, full, width, i).wait_send()
-            weight_pass(name, full, width, i).wait_send()
-
-    w1 = ("w1", e.w1, e.w1g, N1)
-    w2 = ("w2", e.w2, e.w2g, U)
-    w3 = ("w3", e.w3, e.w3g, U)
-    w1f = e.w1g if dims.flat else e.w1f
-    w2f = e.w2g if dims.flat else e.w2f
-    w3f = e.w3g if dims.flat else e.w3f
+            weight_copy(name, i).wait_send()
+            if dims.flat:
+                weight_pass(name, i).wait_send()
+
+    wkv, wqm, w2f, w3f = [
+        getattr(e, name + ("_g" if dims.flat else "_f")) for name in ("wkv", "wqm", "w2", "w3")
+    ]
 
     def x_copy(i):
         return copy(e.xg.at[me_r], e.xg.at[me_r], "x", i, to_row(i))
 
     def vec_copy(i):
-        return copy(e.vec, e.vecr.at[i], "vec", i, to_col(i))
+        return copy(e.vecr.at[me_c], e.vecr.at[me_c], "vec", i, to_col(i))
 
     for i in range(1, R):
         x_copy(i).start()
-    weight_start(*w1)
+    weight_start("wkv")
+    length = e.length[0]
+    for name in ("wkv", "wqm", "w2", "w3"):
+        weight_own(name)
+
+    weight_share("wkv")
+    weight_start("wqm")
     for i in range(1, C):
         vec_copy(i).start()
-    length = e.length[0]
-
-    weight_share(*w1)
-    weight_end("w1", e.w1, e.w1g, w1f, N1)
-
-    def project(i):
+    weight_end("wkv")
+
+    for i in range(R):
         rb = lax.rem(me_r - i + R, R)
         if i:
             x_copy(i).wait_recv()
         tokens = pl.ds(pl.multiple_of(rb * T, T), T)
-        block = e.xg[rb]
-        proj = dot_nn(block, w1f[:, : 3 * F])
-        q = (proj[:, :F] + e.b_attn[0:1, :]).astype(BF16).astype(F32) * (HS ** (-0.5))
-        k = proj[:, F : 2 * F]
-        v = proj[:, 2 * F :] + e.b_attn[1:2, :]
-        e.kv[me_c, pl.ds(0, F), tokens] = k.T.astype(BF16)
-        e.kv[me_c, pl.ds(F, F), tokens] = v.T.astype(BF16)
-        e.q_t[:, tokens] = q.T.astype(BF16)
-        for h in range(NH):
-            e.q_h[h, tokens, :] = q[:, h * HS : (h + 1) * HS].astype(BF16)
-        e.x_rows_t[:, tokens] = turned(block).astype(BF16)
-
-    for i in range(R):
-        project(i)
+        both = dot_nn(e.xg[rb], wkv[...])
+        values = both[:, F:] + e.small[7:8, :]
+        e.kv[me_c, pl.ds(0, F), tokens] = both[:, :F].T.astype(BF16)
+        e.kv[me_c, pl.ds(F, F), tokens] = values.T.astype(BF16)
+
+    def make_queries():
+        weight_share("wqm")
+        weight_end("wqm")
+        e.mix[...] = wqm[:, F:]
+        for i in range(R):
+            tokens = pl.ds(i * T, T)
+            block = e.xg[i]
+            q = dot_nn(block, wqm[:, :F]) + e.small[6:7, :]
+            q = q.astype(BF16).astype(F32) * (HS ** (-0.5))
+            e.q_t[:, tokens] = q.T.astype(BF16)
+            for h in range(NH):
+                e.q_h[h, tokens, :] = q[:, h * HS : (h + 1) * HS].astype(BF16)
+            e.x_rows_t[:, tokens] = turned(block).astype(BF16)
 
     right = {"col": lax.rem(me_c + 1, C)}
     left = {"col": lax.rem(me_c + C - 1, C)}
@@ -248,6 +273,7 @@
     def _():
         kv_left(me_c).start()
 
+    make_queries()
     attend(me_c)
 
     def kv_step(s, carry):
@@ -269,6 +295,11 @@
             @pl.when(me_c > 0)
             def _():
                 kv_left(from_right).start()
+
+        @pl.when(s == min(2, C - 1))
+        def _():
+            weight_start("w2", "inner")
+            weight_start("w3", "inner")
 
         @pl.when(from_left >= 0)
         def _():
@@ -294,8 +325,8 @@
         return carry
 
     lax.fori_loop(0, C, kv_close, 0)
-    weight_start(*w2)
-    weight_start(*w3)
+    weight_start("w2", "outer")
+    weight_start("w3", "outer")
 
     for h in range(NH):
         inverse = 1.0 / e.total[h]
@@ -304,11 +335,12 @@
         e.acc[h] = context
         e.ctx[:, h * HS : (h + 1) * HS] = context.astype(BF16)
 
-    vec = e.vec[...]
     for i in range(1, C):
         vec_copy(i).wait_recv()
-        vec = vec + e.vecr[i]
-    e.vecs[...] = vec
+    for c in range(C):
+        e.vecs[:, c * RB : (c + 1) * RB] = e.vecr[c][:, :RB]
+    for k in range(U // F):
+        e.bias[:, k * F : (k + 1) * F] = e.small[8 + k : 9 + k, :]
 
     def vector(at):
         return e.vecs[at : at + 1, :]
@@ -316,12 +348,9 @@
     def blk_rows(rb):
         return pl.ds(pl.multiple_of(rb * T, T), T)
 
-    def sum_copy(family, i, where):
-        return copy(e.stage.at[i], e.landing.at[slots.base[family] // R, i], family, i, where)
-
     for i in list(range(1, R)) + [0]:
         rb = lax.rem(me_r + i, R)
-        part = dot_nt(e.ctx[blk_rows(rb), :], w1f[:, 3 * F :])
+        part = dot_nt(e.ctx[blk_rows(rb), :], e.mix[...])
         if i:
             e.stage[0, i] = part.astype(BF16)
             copy(e.stage.at[0, i], e.landing.at[0, i], "mix", i, to_row(i)).start()
@@ -348,8 +377,8 @@
 
     for i in range(1, R):
         share(e.hid_g, "hid", i).start()
-    weight_share(*w2)
-    weight_end("w2", e.w2, e.w2g, w2f, U)
+    weight_share("w2")
+    weight_end("w2")
 
     def spread(number, family, part, i, rb):
         if i:
@@ -364,15 +393,15 @@
         rb = lax.rem(me_r - i + R, R)
         if i:
             share(e.hid_g, "hid", i).wait_recv()
-        inner = dot_nn(e.hid_g[rb], w2f[...]) + e.b_expand[...]
+        inner = dot_nn(e.hid_g[rb], w2f[...]) + e.bias[...]
         cdf = 0.5 * (1.0 + lax.erf(inner * (0.5**0.5)))
         active = (inner * cdf).astype(BF16)
         slope = cdf + inner * (jnp.exp(-0.5 * inner * inner) * 0.3989422804014327)
         e.active[blk_rows(rb), :] = active
         e.slope[blk_rows(rb), :] = slope
         if i == 0:
-            weight_share(*w3)
-            weight_end("w3", e.w3, e.w3g, w3f, U)
+            weight_share("w3")
+            weight_end("w3")
         spread(1, "red", dot_nt(e.active[blk_rows(rb), :], w3f[...]), i, rb)
     for i in range(R):
         rb = lax.rem(me_r - i + R, R)
@@ -412,68 +441,73 @@
 
     TR = dims.TR
 
-    def other_copy(name, k):
-        return copy(e.dw_out.at[k], e.dw_in.at[k], name + "_dp", 0, partner)
-
-    def weight_product(k, lhs_ref, rhs_of, transposed):
-        product = dot_nt if transposed else dot_nn
-
+    def half_rows(c, d):
+        if not dims.flat:
+            return pl.ds(c * RB, RB)
+        return pl.ds(pl.multiple_of(c * RB + d * HB, HB), HB)
+
+    def other_copy(name):
+        return copy(getattr(e, name + "_out"), getattr(e, name + "_in"), name + "_dp", 0, partner)
+
+    def d_copy(name, i):
+        stage = getattr(e, name + "_in").at[lax.rem(me_c + i, C)]
+        return copy(stage, getattr(e, name + "_land").at[i], name, i, to_col(i))
+
+    def row_tiles(fill):
         def tile(t, carry):
-            rows = pl.ds(pl.multiple_of(t * TR, TR), TR)
-            lhs = lhs_ref[rows, :]
-            e.dw_out[k, rows, :] = product(lhs, rhs_of(1 - me_d)).astype(BF16)
+            fill(pl.ds(pl.multiple_of(t * TR, TR), TR))
             return carry
 
-        def own_tile(t, carry):
-            rows = pl.ds(pl.multiple_of(t * TR, TR), TR)
-            lhs = lhs_ref[rows, :]
-            e.dw_own[rows, :] = product(lhs, rhs_of(me_d))
+        lax.fori_loop(0, D // TR, tile, 0)
+
+    def weight_swap(name, source):
+        def block(c, carry):
+            getattr(e, name + "_out")[c] = source[half_rows(c, 1 - me_d), :].astype(BF16)
             return carry
 
-        return tile, own_tile
-
-    def d_copy(name, k, i):
-        return copy(e.dw_stage.at[k, lax.rem(me_c + i, C)], e.dw_land.at[k, i], name, i, to_col(i))
-
-    def weight_grad(name, k, lhs_ref, rhs_of, transposed):
-        tile, own_tile = weight_product(k, lhs_ref, rhs_of, transposed)
-        lax.fori_loop(0, D // TR, tile, 0)
-        other_copy(name, k).start()
-        lax.fori_loop(0, D // TR, own_tile, 0)
-        other_copy(name, k).wait_recv()
-
-    def weight_send(name, k):
+        lax.fori_loop(0, C, block, 0)
+        other_copy(name).start()
+
+    def weight_send(name, source):
+        other_copy(name).wait_recv()
+
+        def block(c, carry):
+            total = source[half_rows(c, me_d), :] + getattr(e, name + "_in")[c].astype(F32)
+            getattr(e, name + "_in")[c] = total.astype(BF16)
+            return carry
+
+        lax.fori_loop(0, C, block, 0)
+        for i in range(1, C):
+            d_copy(name, i).start()
+
+    def result_part(name):
+        full = getattr(e, name + "_sum")
+        return full.at[pl.ds(pl.multiple_of(me_d * HB, HB), HB)] if dims.flat else full
+
+    def result_copy(name):
+        return copy(result_part(name), result_part(name), name + "_out", 0, partner)
+
+    def weight_collect(name):
+        total = getattr(e, name + "_in")[me_c].astype(F32)
+        for i in range(1, C):
+            d_copy(name, i).wait_recv()
+            total = total + getattr(e, name + "_land")[i].astype(F32)
+        result_part(name)[...] = total
         if dims.flat:
-            for c in range(C):
-                rows = slice(c * RB, (c + 1) * RB)
-                total = e.dw_own[rows, :] + e.dw_in[k, rows, :].astype(F32)
-                e.dw_stage[k, c] = total.astype(BF16)
-        else:
-            total = e.dw_own[...] + e.dw_in[k].astype(F32)
-            e.dw_stage[k] = total.reshape(C, RB, N1 // 2).astype(BF16)
-        for i in range(1, C):
-            d_copy(name, k, i).start()
-
-    def result_copy(name, k):
-        mine = half_of(N1, me_d)
-        return copy(e.dw.at[k, :, mine], e.dw.at[k, :, mine], name + "_out", 0, partner)
-
-    def weight_collect(name, k):
-        total = e.dw_stage[k, me_c].astype(F32)
-        for i in range(1, C):
-            d_copy(name, k, i).wait_recv()
-            total = total + e.dw_land[k, i].astype(F32)
-        e.dw[k, :, half_of(N1, me_d)] = total
-        result_copy(name, k).start()
-
-    weight_grad(
-        "dw3", 2, e.gr_t, lambda d: e.active[:, half_of(U, d)], False
-    )
-    weight_send("dw3", 2)
-    weight_grad(
-        "dw2", 1, e.hid_t, lambda d: e.g_inner[:, half_of(U, d)], False
-    )
-    weight_send("dw2", 1)
+            result_copy(name).start()
+
+    def fill_reduce(rows):
+        e.dw_f[rows, :] = dot_nn(e.gr_t[rows, :], e.active[...])
+
+    def fill_expand(rows):
+        e.dw_f[rows, :] = dot_nn(e.hid_t[rows, :], e.g_inner[...])
+
+    row_tiles(fill_reduce)
+    weight_swap("dw3", e.dw_f)
+    weight_send("dw3", e.dw_f)
+    row_tiles(fill_expand)
+    weight_swap("dw2", e.dw_f)
+    weight_send("dw2", e.dw_f)
 
     g_hidden = collect(2, "gh") + e.g_second[...]
     normed = e.n1[...]
@@ -502,7 +536,7 @@
         if i:
             share(e.hid_g, "gm", i).wait_recv()
         rows = blk_rows(rb)
-        g_context = dot_nn(e.hid_g[rb], w1f[:, 3 * F :]).astype(BF16).astype(F32)
+        g_context = dot_nn(e.hid_g[rb], e.mix[...]).astype(BF16).astype(F32)
         e.gc_t[:, rows] = g_context.T.astype(BF16)
         for h in range(NH):
             part = g_context[:, h * HS : (h + 1) * HS]
@@ -617,6 +651,16 @@
     for h in range(NH):
         e.dqkv[h * HS : (h + 1) * HS, :] = (e.dq[h] * (HS ** (-0.5))).T.astype(BF16)
 
+    def fill_query(rows):
+        e.dw_s[rows, :F] = dot_nt(e.x_rows_t[rows, :], e.dqkv[:F, :])
+        e.dw_s[rows, F:] = dot_nn(e.gr_t[rows, :], e.ctx[...])
+
+    row_tiles(fill_query)
+    weight_swap("dwqm", e.dw_s)
+    weight_send("dwqm", e.dw_s)
+    weight_collect("dw3")
+    weight_collect("dw2")
+
     for i in range(1, C):
         gv_col(i).wait_recv()
     gsum = e.gall[2]
@@ -642,24 +686,21 @@
 
     for i in list(range(1, R)) + [0]:
         rb = lax.rem(me_r + i, R)
-        part = dot_nn(w1f[:, : 3 * F], e.dqkv[:, blk_rows(rb)])
+        part = dot_nn(wqm[:, :F], e.dqkv[:F, blk_rows(rb)]) + dot_nn(
+            wkv[...], e.dqkv[F:, blk_rows(rb)]
+        )
         if i:
             e.dx_stage[i] = part.astype(BF16)
             copy(e.dx_stage.at[i], e.dx_land.at[i], "dx", i, to_row(i)).start()
         else:
             e.dx_own[...] = part
 
-    def packed_tile(t, carry):
-        rows = pl.ds(pl.multiple_of(t * TR, TR), TR)
-        e.dw1[rows, : 3 * F] = dot_nt(e.x_rows_t[rows, :], e.dqkv[...])
-        e.dw1[rows, 3 * F :] = dot_nn(e.gr_t[rows, :], e.ctx[...])
-        return carry
-
-    lax.fori_loop(0, D // TR, packed_tile, 0)
-    e.dw_out[0] = e.dw1[:, half_of(N1, 1 - me_d)].astype(BF16)
-    other_copy("dw1", 0).start()
-    sums = dot_nt(jnp.ones((8, S), BF16), e.dqkv[...])
-    e.ab[0] = sums
+    def fill_keys(rows):
+        e.dw_s[rows, :] = dot_nt(e.x_rows_t[rows, :], e.dqkv[F:, :])
+
+    row_tiles(fill_keys)
+    weight_swap("dwkv", e.dw_s)
+    e.ab[0] = dot_nt(jnp.ones((8, S), BF16), e.dqkv[...])
 
     def ab_dp():
         return copy(e.ab.at[0], e.ab.at[1], "ab_dp", 0, partner)
@@ -668,16 +709,13 @@
         return copy(e.ab.at[2], e.abcol.at[i], "ab_col", i, to_col(i))
 
     ab_dp().start()
-    e.dw_own[...] = e.dw1[:, half_of(N1, me_d)]
-    other_copy("dw1", 0).wait_recv()
-    weight_send("dw1", 0)
+    weight_send("dwkv", e.dw_s)
     ab_dp().wait_recv()
     e.ab[2] = e.ab[0] + e.ab[1]
     for i in range(1, C):
         ab_col(i).start()
 
-    weight_collect("dw3", 2)
-    weight_collect("dw2", 1)
+    weight_collect("dwqm")
 
     total = e.dx_own[...] + e.g_first[...].T
     for i in range(1, R):
@@ -689,20 +727,28 @@
     for i in range(1, R):
         gv_row(i).wait_recv()
         vsum = vsum + e.grow[i][:, :D]
-    e.gvec[...] = vsum
-    e.gunit[...] = e.gsum[8:16, :U]
+    mine = vsum[:, :RB]
+    for c in range(1, C):
+        mine = jnp.where(me_c == c, vsum[:, c * RB : (c + 1) * RB], mine)
+    e.g_vec[...] = mine
+    e.g_unit[...] = e.gsum[8:9, :U]
     asum = e.ab[2]
     for i in range(1, C):
         ab_col(i).wait_recv()
         asum = asum + e.abcol[i]
-    e.gab[...] = asum
-    weight_collect("dw1", 0)
-    for name, k in (("dw3", 2), ("dw2", 1), ("dw1", 0)):
-        result_copy(name, k).wait_recv()
-
-    weight_close(*w1)
-    weight_close(*w2)
-    weight_close(*w3)
+    e.g_ab[0:1, :] = asum[0:1, :F]
+    e.g_ab[1:2, :] = asum[0:1, 2 * F :]
+    weight_collect("dwkv")
+    if dims.flat:
+        for name in ("dw3", "dw2", "dwqm", "dwkv"):
+            result_copy(name).wait_recv()
+    e.g_attn[0] = e.dwqm_sum[:, :F]
+    e.g_mix[...] = e.dwqm_sum[:, F:]
+    e.g_attn[1] = e.dwkv_sum[:, :F]
+    e.g_attn[2] = e.dwkv_sum[:, F:]
+
+    for name in ("wkv", "wqm", "w2", "w3"):
+        weight_close(name)
     for i in range(1, R):
         x_copy(i).wait_send()
         copy(e.stage.at[0, i], e.landing.at[0, i], "mix", i, to_row(i)).wait_send()
@@ -718,11 +764,12 @@
         vec_copy(i).wait_send()
         gv_col(i).wait_send()
         ab_col(i).wait_send()
-    for name, k in (("dw3", 2), ("dw2", 1), ("dw1", 0)):
-        other_copy(name, k).wait_send()
+    for name in ("dw3", "dw2", "dwqm", "dwkv"):
+        other_copy(name).wait_send()
         for i in range(1, C):
-            d_copy(name, k, i).wait_send()
-        result_copy(name, k).wait_send()
+            d_copy(name, i).wait_send()
+        if dims.flat:
+            result_copy(name).wait_send()
 
     def dkv_close(s, carry):
         @pl.when(C - 1 - s > me_c)
@@ -738,43 +785,52 @@
     lax.fori_loop(0, C - 1, dkv_close, 0)
 
 
-def run_layer(x_t, length, w1, w2, w3, vec, b_attn, b_expand, out_grad):
+def run_layer(x_t, length, w_attn, w_mixer, w2, w3, small, out_grad):
     R = lax.axis_size("row")
     C = lax.axis_size("col")
     T = x_t.shape[1]
     S = T * R
-    F = b_attn.shape[1]
+    F = w_mixer.shape[1]
     U = w2.shape[1]
-    RB = w1.shape[0]
+    RB = w_mixer.shape[0]
+    flat = RB % 32 == 0
     HS = D // H
     dims = SimpleNamespace(
-        R=R, C=C, T=T, S=S, F=F, U=U, RB=RB, HS=HS, NH=F // HS, N1=4 * F,
-        flat=RB % 16 == 0, TQ=min(256, S), TR=256, NB=min(C, 4),
+        R=R, C=C, T=T, S=S, F=F, U=U, RB=RB, HS=HS, NH=F // HS,
+        flat=flat, HB=RB // 2 if flat else RB, TQ=min(256, S), TR=256, NB=min(C - 1, 3),
     )
-    N1 = dims.N1
+    HB = dims.HB
     NH = dims.NH
     slots = slots_of(R, C)
     wide = max(D, U)
     w_shape = (lambda n: (C * RB, n)) if dims.flat else (lambda n: (C, RB, n))
     inputs = dict(
-        x_t=x_t, length=length, w1=w1, w2=w2, w3=w3, vec=vec, b_attn=b_attn,
-        b_expand=b_expand, out_grad=out_grad,
+        x_t=x_t, length=length, w_attn=w_attn, w_mixer=w_mixer, w2=w2, w3=w3, small=small,
+        out_grad=out_grad,
     )
     outputs = dict(
         layer_out=((D, T), BF16),
         grad_input=((D, T), F32),
-        dw=((3, RB, N1), F32),
-        gvec=((8, D), F32),
-        gunit=((8, U), F32),
-        gab=((8, 3 * F), F32),
+        g_attn=((3, RB, F), F32),
+        g_mix=((RB, F), F32),
+        dw2_sum=((RB, U), F32),
+        dw3_sum=((RB, U), F32),
+        g_vec=((8, RB), F32),
+        g_unit=((1, U), F32),
+        g_ab=((2, F), F32),
     )
     scratch = dict(
         xg=((R, T, D), BF16),
-        w1g=(w_shape(N1), BF16),
-        w2g=(w_shape(U), BF16),
-        w3g=(w_shape(U), BF16),
-        vecr=((C, 8, D), F32),
+        wkv=((RB, 2 * F), BF16),
+        wqm=((RB, 2 * F), BF16),
+        wkv_g=(w_shape(2 * F), BF16),
+        wqm_g=(w_shape(2 * F), BF16),
+        w2_g=(w_shape(U), BF16),
+        w3_g=(w_shape(U), BF16),
+        mix=((D, F), BF16),
+        vecr=((C, 8, F), F32),
         vecs=((8, D), F32),
+        bias=((1, U), F32),
         kv=((C, 2 * F, S), BF16),
         q_t=((F, S), BF16),
         q_h=((NH, S, HS), BF16),
@@ -803,12 +859,10 @@
         gcol=((C, 16, wide), F32),
         gsum=((16, wide), F32),
         grow=((R, 8, wide), F32),
-        dw_out=((3, D, N1 // 2), BF16),
-        dw_in=((3, D, N1 // 2), BF16),
-        dw_own=((D, N1 // 2), F32),
-        dw_stage=((3, C, RB, N1 // 2), BF16),
-        dw_land=((3, C, RB, N1 // 2), BF16),
-        dw1=((D, N1), F32),
+        dw_f=((D, U), F32),
+        dw_s=((D, 2 * F), F32),
+        dwqm_sum=((RB, 2 * F), F32),
+        dwkv_sum=((RB, 2 * F), F32),
         g_first=((T, D), F32),
         gc_t=((F, S), BF16),
         gc_h=((NH, S, HS), BF16),
@@ -823,10 +877,11 @@
         ab=((3, 8, 3 * F), F32),
         abcol=((C, 8, 3 * F), F32),
     )
-    if not dims.flat:
-        scratch.update(
-            w1f=((C * RB, N1), BF16), w2f=((C * RB, U), BF16), w3f=((C * RB, U), BF16)
-        )
+    for name, width in (("wkv", 2 * F), ("wqm", 2 * F), ("w2", U), ("w3", U)):
+        for part in ("out", "in", "land"):
+            scratch["d" + name + "_" + part] = ((C, HB, width), BF16)
+        if not dims.flat:
+            scratch[name + "_f"] = ((C * RB, width), BF16)
     names = list(inputs) + list(outputs) + list(scratch) + ["send_sems", "recv_sems", "credits"]
     vmem = pl.BlockSpec(memory_space=pltpu.VMEM)
     in_specs = [
@@ -865,41 +920,43 @@
     shift_two,
     out_grad,
 ):
-    col_index = lax.axis_index("col")
     rows = w_mixer.shape[0]
     feats = w_mixer.shape[1]
-    w1 = jnp.concatenate([w_attn.reshape(rows, 3 * feats), w_mixer], 1)
-    own = jnp.stack([b_mixer, gain_one, shift_one, b_reduce, gain_two, shift_two]).astype(F32)
-    vec = lax.dynamic_update_slice(jnp.zeros((8, D), F32), own, (0, col_index * rows))
+    units = w_expand.shape[1]
+    own = jnp.stack([b_mixer, gain_one, shift_one, b_reduce, gain_two, shift_two])
+    small = jnp.concatenate(
+        [
+            jnp.pad(own, ((0, 0), (0, feats - rows))),
+            b_attn,
+            b_expand.reshape(units // feats, feats),
+        ]
+    ).astype(F32)
     out = run_layer(
         layer_in,
         lengths,
-        w1,
+        jnp.transpose(w_attn, (1, 0, 2)),
+        w_mixer,
         w_expand,
         w_reduce,
-        vec,
-        b_attn.astype(F32),
-        b_expand.astype(F32)[None],
+        small,
         out_grad,
     )
-    gvec = lax.dynamic_slice(out["gvec"], (0, col_index * rows), (8, rows))
-    dw1 = out["dw"][0]
-    gab = out["gab"]
+    g_vec = out["g_vec"]
     return (
         out["layer_out"],
         out["grad_input"],
-        dw1[:, : 3 * feats].reshape(rows, 3, feats),
-        jnp.stack([gab[0, :feats], gab[0, 2 * feats :]]),
-        dw1[:, 3 * feats :],
-        gvec[0],
-        gvec[1],
-        gvec[2],
-        out["dw"][1],
-        out["gunit"][0],
-        out["dw"][2],
-        gvec[3],
-        gvec[4],
-        gvec[5],
+        jnp.transpose(out["g_attn"], (1, 0, 2)),
+        out["g_ab"],
+        out["g_mix"],
+        g_vec[0],
+        g_vec[1],
+        g_vec[2],
+        out["dw2_sum"],
+        out["g_unit"][0],
+        out["dw3_sum"],
+        g_vec[3],
+        g_vec[4],
+        g_vec[5],
     )
 
 

time: 227 us -> 204 us (0.90); the launches traced: 224 us -> 204 us
  Pallas kernels: 202 us -> 188 us
  local copies, waits for them, and re-layouts: 16.2 us -> 12.9 us
    pallas_call x1, Pallas kernels: 202 us -> 188 us  [run_layer(): pl.pallas_call(functools.partial(layer_kernel, dims, names), out_shape=[j...]
    unnamed x10 -> x33, local copies, waits for them, and re-layouts: 3.64 us -> 10.5 us
    another operation x7 -> x6, local copies, waits for them, and re-layouts: 3.98 us -> 0.03 us  [on_device(): jnp.stack([b_mixer, gain_one, shift_one, b_reduce, gain_two, shift_two])]
    squeeze x1 -> x0, local copies, waits for them, and re-layouts: 2.54 us -> none  [on_device(): out['dw'][2]]
    slice x5 -> x1, local copies, waits for them, and re-layouts: 3.96 us -> 1.51 us  [on_device(): g_vec[5]]
where the time goes in v2:
time: 204 us
  Pallas kernels  188 us (92%)
  local copies, waits for them, and re-layouts  12.9 us (6%)
    pallas_call x1, Pallas kernels, run_layer(): pl.pallas_call(functools.partial(layer_kernel, dims, names), out_shape=[j...  188 us
    unnamed x33, local copies, waits for them, and re-layouts  10.5 us

profile of v2, /device:TPU:25, one launch (start us, length us, event | category | flops | bytes accessed | tf_op | source)
XLA Modules:
  0.0 203.8 jit_solution(1295433879715957199)
XLA Ops:
  0.6 0.0 copy-start.7
  0.7 0.8 reshape.31
  1.4 0.0 copy-done.7
  1.4 0.0 copy-start.8
  1.4 0.6 copy-done.8
  2.1 0.0 copy-start.9
  2.1 0.6 copy-done.9
  2.7 0.0 copy-start.10
  2.8 0.6 copy-done.10
  3.4 0.0 copy-start.11
  3.4 0.6 copy-done.11
  4.1 0.0 copy-start.12
  4.1 0.6 copy-done.12
  4.7 0.0 copy-start.6
  4.7 0.7 copy-done.6
  5.4 0.6 convert_element_type.3.refs_6_
  6.7 187.7 %layer.1 = (bf16[768,128]{1,0:T(8,128)(2,1)}, f32[768,128]{1,0:T(8,128)}, f32[3,192,192]{2,1,0:T(8,128)}, f32[192,192]{1,0:T(8,128)}, f32[192,768]{1,0:T(8,128)}...) custom-call(bf16[768,128]{1,0:T(8,128)(2,1)} %refs_0_.1, s32[1]{0:T(128)S(6)} %copy.36.refs_1_, ...), custom_call_target="tpu_custom_call" | custom-call | tf_op jit(solution)/shard_map/layer/pallas_call | solution.py:890
  194.4 0.0 copy-start.3
  194.4 1.5 fusion
  195.9 1.3 reduce
  197.2 0.0 copy-start.2
  197.2 1.7 copy.37
  198.9 0.0 copy-done.3
  198.9 0.7 copy.38
  199.6 0.0 copy-done.2
  199.6 0.0 copy-start.5
  199.6 0.0 copy-start.4
  199.6 0.0 copy-start.1
  199.6 0.8 copy.39
  200.5 0.0 copy-done.5
  200.5 0.6 copy.40
  201.0 0.0 copy-done.4
  201.0 0.7 copy.41
  201.7 0.0 copy-done.1
  201.7 0.0 copy-start
  201.7 0.8 copy.42
  202.5 0.5 copy-done
  203.0 0.8 copy.43
  (7 shorter events, 0.1 us)
Async XLA Ops:
  0.6 0.8 copy-start.7
  1.4 0.7 copy-start.8
  2.1 0.7 copy-start.9
  2.7 0.7 copy-start.10
  3.4 0.7 copy-start.11
  4.1 0.7 copy-start.12
  4.7 0.7 copy-start.6
  194.4 4.5 %copy-start.3 = (f32[768,128]{1,0:T(8,128)S(1)}, f32[768,128]{1,0:T(8,128)}, u32[]{:S(2)}) copy-start(f32[768,128]{1,0:T(8,128)} %get-tuple-element.53) | copy-start | bytes 1179652
  197.2 2.4 %copy-start.2 = (f32[3,192,192]{2,1,0:T(8,128)S(1)}, f32[3,192,192]{2,1,0:T(8,128)}, u32[]{:S(2)}) copy-start(f32[3,192,192]{2,1,0:T(8,128)} %get-tuple-element.25) | copy-start | bytes 1327108
  199.6 0.8 copy-start.5
  199.6 1.4 copy-start.4
  199.6 2.1 %copy-start.1 = (f32[192,768]{1,0:T(8,128)S(1)}, f32[192,768]{1,0:T(8,128)}, u32[]{:S(2)}) copy-start(f32[192,768]{1,0:T(8,128)} %get-tuple-element.60) | copy-start | bytes 1769476
  201.7 1.3 copy-start

commit v3 on v2

--- a/solution.py
+++ b/solution.py
@@ -352,16 +352,16 @@
         rb = lax.rem(me_r + i, R)
         part = dot_nt(e.ctx[blk_rows(rb), :], e.mix[...])
         if i:
-            e.stage[0, i] = part.astype(BF16)
-            copy(e.stage.at[0, i], e.landing.at[0, i], "mix", i, to_row(i)).start()
+            e.stage[0, i - 1] = part.astype(BF16)
+            copy(e.stage.at[0, i - 1], e.landing.at[0, i - 1], "mix", i, to_row(i)).start()
         else:
             e.own[...] = part
 
     def collect(number, family):
         total = e.own[...]
         for i in range(1, R):
-            copy(e.stage.at[number, i], e.landing.at[number, i], family, i, to_row(i)).wait_recv()
-            total = total + e.landing[number, i].astype(F32)
+            copy(e.stage.at[number, i - 1], e.landing.at[number, i - 1], family, i, to_row(i)).wait_recv()
+            total = total + e.landing[number, i - 1].astype(F32)
         return total
 
     first_sum = turned(e.x_t[...]) + collect(0, "mix") + vector(0)
@@ -382,9 +382,9 @@
 
     def spread(number, family, part, i, rb):
         if i:
-            e.stage[number, i] = part.astype(BF16)
+            e.stage[number, i - 1] = part.astype(BF16)
             copy(
-                e.stage.at[number, i], e.landing.at[number, i], family, i, to_row(R - i)
+                e.stage.at[number, i - 1], e.landing.at[number, i - 1], family, i, to_row(R - i)
             ).start()
         else:
             e.own[...] = part
@@ -555,7 +555,7 @@
 
     e.dq[...] = jnp.zeros(e.dq.shape, F32)
 
-    def attend_back(b):
+    def attend_back(b, to):
         valid = key_valid(b)
         for h in range(NH):
             krows = slice(h * HS, (h + 1) * HS)
@@ -578,8 +578,8 @@
 
             zero = jnp.zeros((HS, S), F32)
             d_keys, d_values = lax.fori_loop(0, S // TQ, tile, (zero, zero))
-            e.dkv[krows, :] = d_keys
-            e.dkv[vrows, :] = d_values
+            e.dkv[to, krows, :] = d_keys
+            e.dkv[to, vrows, :] = d_values
 
     NB = dims.NB
 
@@ -599,12 +599,25 @@
             def _():
                 pl.semaphore_wait(e.credits.at[way], 1)
 
-        (dkv_right if way == 0 else dkv_left)(b).start()
-
-    def dkv_take(way, b):
+        if way == 0:
+
+            @pl.when(b < C - 1)
+            def _():
+                dkv_right(b + 1).wait_send()
+
+            dkv_right(b).start()
+        else:
+
+            @pl.when(b > 0)
+            def _():
+                dkv_left(b - 1).wait_send()
+
+            dkv_left(b).start()
+
+    def dkv_take(way, b, to):
         order = C - 1 - b if way == 0 else b
         (dkv_right if way == 0 else dkv_left)(b).wait_recv()
-        e.dkv[...] += e.dkv_in[way, lax.rem(order, NB)].astype(F32)
+        e.dkv[to] += e.dkv_in[way, lax.rem(order, NB)].astype(F32)
         if C - 1 > NB:
             sends = C - me_c if way == 0 else me_c + 1
 
@@ -617,36 +630,49 @@
                     device_id_type=MESH,
                 )
 
+    inner_device = (me_c > 0) & (me_c < C - 1)
+
+    @pl.when(inner_device)
+    def _():
+        attend_back(me_c, 2)
+
     def dkv_step(s, carry):
-        far_right = C - 1 - s
-        far_left = s
-
-        @pl.when(far_right > me_c)
+        from_left = C - 1 + me_c - s
+        from_right = s - (C - 1 - me_c)
+
+        @pl.when(s >= me_c)
         def _():
-            attend_back(far_right)
-
+            attend_back(from_left, 0)
+
+        @pl.when(from_right >= 0)
+        def _():
+            attend_back(from_right, 1)
+
+        @pl.when(s >= me_c)
+        def _():
             @pl.when(me_c > 0)
             def _():
-                dkv_take(0, far_right)
-
-            e.kv[far_right] = e.dkv[...].astype(BF16)
-            dkv_send(0, far_right)
-
-        @pl.when(far_left < me_c)
+                dkv_take(0, from_left, 0)
+
+            e.kv[from_left] = e.dkv[0].astype(BF16)
+            dkv_send(0, from_left)
+
+        @pl.when(from_right >= 0)
         def _():
-            attend_back(far_left)
-
             @pl.when(me_c < C - 1)
             def _():
-                dkv_take(1, far_left)
-
-            e.kv[far_left] = e.dkv[...].astype(BF16)
-            dkv_send(1, far_left)
+                dkv_take(1, from_right, 1)
+
+            e.kv[from_right] = e.dkv[1].astype(BF16)
+            dkv_send(1, from_right)
 
         return carry
 
     lax.fori_loop(0, C - 1, dkv_step, 0)
-    attend_back(me_c)
+
+    @pl.when(jnp.logical_not(inner_device))
+    def _():
+        attend_back(me_c, 2)
 
     for h in range(NH):
         e.dqkv[h * HS : (h + 1) * HS, :] = (e.dq[h] * (HS ** (-0.5))).T.astype(BF16)
@@ -676,13 +702,13 @@
 
     @pl.when(me_c > 0)
     def _():
-        dkv_take(0, me_c)
+        dkv_take(0, me_c, 2)
 
     @pl.when(me_c < C - 1)
     def _():
-        dkv_take(1, me_c)
-
-    e.dqkv[F : 3 * F, :] = e.dkv[...].astype(BF16)
+        dkv_take(1, me_c, 2)
+
+    e.dqkv[F : 3 * F, :] = e.dkv[2].astype(BF16)
 
     for i in list(range(1, R)) + [0]:
         rb = lax.rem(me_r + i, R)
@@ -690,8 +716,8 @@
             wkv[...], e.dqkv[F:, blk_rows(rb)]
         )
         if i:
-            e.dx_stage[i] = part.astype(BF16)
-            copy(e.dx_stage.at[i], e.dx_land.at[i], "dx", i, to_row(i)).start()
+            e.dx_stage[i - 1] = part.astype(BF16)
+            copy(e.dx_stage.at[i - 1], e.dx_land.at[i - 1], "dx", i, to_row(i)).start()
         else:
             e.dx_own[...] = part
 
@@ -719,8 +745,8 @@
 
     total = e.dx_own[...] + e.g_first[...].T
     for i in range(1, R):
-        copy(e.dx_stage.at[i], e.dx_land.at[i], "dx", i, to_row(i)).wait_recv()
-        total = total + e.dx_land[i].astype(F32)
+        copy(e.dx_stage.at[i - 1], e.dx_land.at[i - 1], "dx", i, to_row(i)).wait_recv()
+        total = total + e.dx_land[i - 1].astype(F32)
     e.grad_input[...] = total
 
     vsum = e.gsum[0:8, :D]
@@ -751,12 +777,12 @@
         weight_close(name)
     for i in range(1, R):
         x_copy(i).wait_send()
-        copy(e.stage.at[0, i], e.landing.at[0, i], "mix", i, to_row(i)).wait_send()
-        copy(e.stage.at[1, i], e.landing.at[1, i], "red", i, to_row(i)).wait_send()
+        copy(e.stage.at[0, i - 1], e.landing.at[0, i - 1], "mix", i, to_row(i)).wait_send()
+        copy(e.stage.at[1, i - 1], e.landing.at[1, i - 1], "red", i, to_row(i)).wait_send()
         share(e.gr_g, "gr", i).wait_send()
-        copy(e.stage.at[2, i], e.landing.at[2, i], "gh", i, to_row(i)).wait_send()
+        copy(e.stage.at[2, i - 1], e.landing.at[2, i - 1], "gh", i, to_row(i)).wait_send()
         share(e.hid_g, "gm", i).wait_send()
-        copy(e.dx_stage.at[i], e.dx_land.at[i], "dx", i, to_row(i)).wait_send()
+        copy(e.dx_stage.at[i - 1], e.dx_land.at[i - 1], "dx", i, to_row(i)).wait_send()
         gv_row(i).wait_send()
     gv_dp().wait_send()
     ab_dp().wait_send()
@@ -771,18 +797,13 @@
         if dims.flat:
             result_copy(name).wait_send()
 
-    def dkv_close(s, carry):
-        @pl.when(C - 1 - s > me_c)
-        def _():
-            dkv_right(C - 1 - s).wait_send()
-
-        @pl.when(s < me_c)
-        def _():
-            dkv_left(s).wait_send()
-
-        return carry
-
-    lax.fori_loop(0, C - 1, dkv_close, 0)
+    @pl.when(me_c < C - 1)
+    def _():
+        dkv_right(me_c + 1).wait_send()
+
+    @pl.when(me_c > 0)
+    def _():
+        dkv_left(me_c - 1).wait_send()
 
 
 def run_layer(x_t, length, w_attn, w_mixer, w2, w3, small, out_grad):
@@ -839,8 +860,8 @@
         total=((NH, S, 1), F32),
         acc=((NH, S, HS), F32),
         ctx=((S, F), BF16),
-        stage=((3, R, T, D), BF16),
-        landing=((3, R, T, D), BF16),
+        stage=((3, R - 1, T, D), BF16),
+        landing=((3, R - 1, T, D), BF16),
         own=((T, D), F32),
         n1=((T, D), F32),
         r1=((T, 1), F32),
@@ -868,11 +889,11 @@
         gc_h=((NH, S, HS), BF16),
         inner_sum=((NH, S, 1), F32),
         dq=((NH, S, HS), F32),
-        dkv=((2 * F, S), F32),
+        dkv=((3, 2 * F, S), F32),
         dkv_in=((2, dims.NB, 2 * F, S), BF16),
         dqkv=((3 * F, S), BF16),
-        dx_stage=((R, D, T), BF16),
-        dx_land=((R, D, T), BF16),
+        dx_stage=((R - 1, D, T), BF16),
+        dx_land=((R - 1, D, T), BF16),
         dx_own=((D, T), F32),
         ab=((3, 8, 3 * F), F32),
         abcol=((C, 8, 3 * F), F32),

time: 204 us -> 188 us (0.922)
  Pallas kernels: 188 us -> 171 us
    pallas_call x1, Pallas kernels: 188 us -> 171 us  [run_layer(): pl.pallas_call(functools.partial(layer_kernel, dims, names), out_shape=[j...]
where the time goes in v3:
time: 188 us; the launch traced here: 187 us
  Pallas kernels  171 us (91%)
  local copies, waits for them, and re-layouts  12.9 us (7%)
  other arithmetic  1.9 us (1%)
    pallas_call x1, Pallas kernels, run_layer(): pl.pallas_call(functools.partial(layer_kernel, dims, names), out_shape=[j...  171 us
    unnamed x33, local copies, waits for them, and re-layouts  10.5 us

profile of v3, /device:TPU:25, one launch (start us, length us, event | category | flops | bytes accessed | tf_op | source)
XLA Modules:
  0.0 187.3 jit_solution(1994604917287248951)
XLA Ops:
  0.6 0.0 copy-start.7
  0.7 0.8 reshape.31
  1.4 0.0 copy-done.7
  1.4 0.0 copy-start.8
  1.4 0.6 copy-done.8
  2.1 0.0 copy-start.9
  2.1 0.6 copy-done.9
  2.7 0.0 copy-start.10
  2.8 0.6 copy-done.10
  3.4 0.0 copy-start.11
  3.4 0.6 copy-done.11
  4.1 0.0 copy-start.12
  4.1 0.6 copy-done.12
  4.7 0.0 copy-start.6
  4.7 0.7 copy-done.6
  5.4 0.6 convert_element_type.3.refs_6_
  6.7 171.2 %layer.1 = (bf16[768,128]{1,0:T(8,128)(2,1)}, f32[768,128]{1,0:T(8,128)}, f32[3,192,192]{2,1,0:T(8,128)}, f32[192,192]{1,0:T(8,128)}, f32[192,768]{1,0:T(8,128)}...) custom-call(bf16[768,128]{1,0:T(8,128)(2,1)} %refs_0_.1, s32[1]{0:T(128)S(6)} %copy.36.refs_1_, ...), custom_call_target="tpu_custom_call" | custom-call | tf_op jit(solution)/shard_map/layer/pallas_call | solution.py:911
  177.9 0.0 copy-start.3
  177.9 1.5 fusion
  179.4 1.3 reduce
  180.7 0.0 copy-start.2
  180.7 1.7 copy.37
  182.4 0.0 copy-done.3
  182.4 0.7 copy.38
  183.1 0.0 copy-done.2
  183.1 0.0 copy-start.5
  183.1 0.0 copy-start.4
  183.1 0.0 copy-start.1
  183.1 0.8 copy.39
  183.9 0.0 copy-done.5
  183.9 0.6 copy.40
  184.5 0.0 copy-done.4
  184.5 0.7 copy.41
  185.2 0.0 copy-done.1
  185.2 0.0 copy-start
  185.2 0.8 copy.42
  186.0 0.5 copy-done
  186.5 0.8 copy.43
  (7 shorter events, 0.1 us)
Async XLA Ops:
  0.6 0.8 copy-start.7
  1.4 0.7 copy-start.8
  2.1 0.7 copy-start.9
  2.7 0.7 copy-start.10
  3.4 0.7 copy-start.11
  4.1 0.7 copy-start.12
  4.7 0.7 copy-start.6
  177.9 4.5 %copy-start.3 = (f32[768,128]{1,0:T(8,128)S(1)}, f32[768,128]{1,0:T(8,128)}, u32[]{:S(2)}) copy-start(f32[768,128]{1,0:T(8,128)} %get-tuple-element.53) | copy-start | bytes 1179652
  180.7 2.4 %copy-start.2 = (f32[3,192,192]{2,1,0:T(8,128)S(1)}, f32[3,192,192]{2,1,0:T(8,128)}, u32[]{:S(2)}) copy-start(f32[3,192,192]{2,1,0:T(8,128)} %get-tuple-element.25) | copy-start | bytes 1327108
  183.1 0.8 copy-start.5
  183.1 1.4 copy-start.4
  183.1 2.1 %copy-start.1 = (f32[192,768]{1,0:T(8,128)S(1)}, f32[192,768]{1,0:T(8,128)}, u32[]{:S(2)}) copy-start(f32[192,768]{1,0:T(8,128)} %get-tuple-element.60) | copy-start | bytes 1769476
  185.2 1.3 copy-start

commit v4 on v3

--- a/solution.py
+++ b/solution.py
@@ -118,7 +118,10 @@
     e.wkv[:, F:] = e.w_attn[2]
     e.wqm[:, :F] = e.w_attn[0]
     e.wqm[:, F:] = e.w_mixer[...]
-    e.vecr[me_c] = e.small[0:8, :]
+    vectors = (e.b_mixer, e.gain_one, e.shift_one, e.b_reduce, e.gain_two, e.shift_two)
+    for k, ref in enumerate(vectors):
+        e.vecr[me_c, k : k + 1, :RB] = ref[...].astype(F32).reshape(1, RB)
+    e.bias[...] = e.b_expand[...].astype(F32).reshape(1, U)
     pl.semaphore_wait(barrier, 1 + (R - 1) + (C - 1))
 
     def w_rows(ref, c, d):
@@ -204,7 +207,7 @@
             x_copy(i).wait_recv()
         tokens = pl.ds(pl.multiple_of(rb * T, T), T)
         both = dot_nn(e.xg[rb], wkv[...])
-        values = both[:, F:] + e.small[7:8, :]
+        values = both[:, F:] + e.b_attn[1:2, :].astype(F32)
         e.kv[me_c, pl.ds(0, F), tokens] = both[:, :F].T.astype(BF16)
         e.kv[me_c, pl.ds(F, F), tokens] = values.T.astype(BF16)
 
@@ -215,7 +218,7 @@
         for i in range(R):
             tokens = pl.ds(i * T, T)
             block = e.xg[i]
-            q = dot_nn(block, wqm[:, :F]) + e.small[6:7, :]
+            q = dot_nn(block, wqm[:, :F]) + e.b_attn[0:1, :].astype(F32)
             q = q.astype(BF16).astype(F32) * (HS ** (-0.5))
             e.q_t[:, tokens] = q.T.astype(BF16)
             for h in range(NH):
@@ -339,8 +342,6 @@
         vec_copy(i).wait_recv()
     for c in range(C):
         e.vecs[:, c * RB : (c + 1) * RB] = e.vecr[c][:, :RB]
-    for k in range(U // F):
-        e.bias[:, k * F : (k + 1) * F] = e.small[8 + k : 9 + k, :]
 
     def vector(at):
         return e.vecs[at : at + 1, :]
@@ -806,7 +807,7 @@
         dkv_left(me_c - 1).wait_send()
 
 
-def run_layer(x_t, length, w_attn, w_mixer, w2, w3, small, out_grad):
+def run_layer(x_t, length, w_attn, w_mixer, w2, w3, out_grad, b_attn, b_expand, **vectors):
     R = lax.axis_size("row")
     C = lax.axis_size("col")
     T = x_t.shape[1]
@@ -826,8 +827,8 @@
     wide = max(D, U)
     w_shape = (lambda n: (C * RB, n)) if dims.flat else (lambda n: (C, RB, n))
     inputs = dict(
-        x_t=x_t, length=length, w_attn=w_attn, w_mixer=w_mixer, w2=w2, w3=w3, small=small,
-        out_grad=out_grad,
+        x_t=x_t, length=length, w_attn=w_attn, w_mixer=w_mixer, w2=w2, w3=w3, out_grad=out_grad,
+        b_attn=b_attn, b_expand=b_expand, **vectors,
     )
     outputs = dict(
         layer_out=((D, T), BF16),
@@ -924,6 +925,36 @@
     return dict(zip(outputs, results))
 
 
+def finish_kernel(*refs):
+    big_in, rows, unit, big_out, vecs, unit_out = (
+        refs[:7], refs[7], refs[8], refs[9:16], refs[16:22], refs[22],
+    )
+    for src, dst in zip(big_in, big_out):
+        dst[...] = src[...]
+    for k, ref in enumerate(vecs):
+        ref[...] = rows[k : k + 1, :].reshape(ref.shape)
+    unit_out[...] = unit[...].reshape(unit_out.shape)
+
+
+def finish(out):
+    big = [
+        out[name]
+        for name in ("layer_out", "grad_input", "g_attn", "g_mix", "dw2_sum", "dw3_sum", "g_ab")
+    ]
+    rows = out["g_vec"].shape[1]
+    units = out["g_unit"].shape[1]
+    vmem = pl.BlockSpec(memory_space=pltpu.VMEM)
+    shapes = [jax.ShapeDtypeStruct(a.shape, a.dtype) for a in big]
+    shapes += [jax.ShapeDtypeStruct((rows,), F32)] * 6 + [jax.ShapeDtypeStruct((units,), F32)]
+    return pl.pallas_call(
+        finish_kernel,
+        out_shape=shapes,
+        in_specs=[vmem] * 9,
+        out_specs=[vmem] * 14,
+        name="finish",
+    )(*big, out["g_vec"], out["g_unit"])
+
+
 def on_device(
     layer_in,
     lengths,
@@ -941,17 +972,6 @@
     shift_two,
     out_grad,
 ):
-    rows = w_mixer.shape[0]
-    feats = w_mixer.shape[1]
-    units = w_expand.shape[1]
-    own = jnp.stack([b_mixer, gain_one, shift_one, b_reduce, gain_two, shift_two])
-    small = jnp.concatenate(
-        [
-            jnp.pad(own, ((0, 0), (0, feats - rows))),
-            b_attn,
-            b_expand.reshape(units // feats, feats),
-        ]
-    ).astype(F32)
     out = run_layer(
         layer_in,
         lengths,
@@ -959,25 +979,32 @@
         w_mixer,
         w_expand,
         w_reduce,
-        small,
         out_grad,
+        b_attn,
+        b_expand,
+        b_mixer=b_mixer,
+        gain_one=gain_one,
+        shift_one=shift_one,
+        b_reduce=b_reduce,
+        gain_two=gain_two,
+        shift_two=shift_two,
     )
-    g_vec = out["g_vec"]
+    layer_out, grad_input, g_attn, g_mix, g_expand, g_reduce, g_ab, *vecs, g_unit = finish(out)
     return (
-        out["layer_out"],
-        out["grad_input"],
-        jnp.transpose(out["g_attn"], (1, 0, 2)),
-        out["g_ab"],
-        out["g_mix"],
-        g_vec[0],
-        g_vec[1],
-        g_vec[2],
-        out["dw2_sum"],
-        out["g_unit"][0],
-        out["dw3_sum"],
-        g_vec[3],
-        g_vec[4],
-        g_vec[5],
+        layer_out,
+        grad_input,
+        jnp.transpose(g_attn, (1, 0, 2)),
+        g_ab,
+        g_mix,
+        vecs[0],
+        vecs[1],
+        vecs[2],
+        g_expand,
+        g_unit,
+        g_reduce,
+        vecs[3],
+        vecs[4],
+        vecs[5],
     )
 
 

time: 188 us -> 176 us (0.936)
  local copies, waits for them, and re-layouts: 12.9 us -> 0 us
  Pallas kernels: 171 us -> 175 us
  other arithmetic: 1.9 us -> 0 us
    unnamed x33 -> x0, local copies, waits for them, and re-layouts: 10.5 us -> none
    pallas_call x0 -> x1, Pallas kernels: none -> 3.24 us  [finish(): pl.pallas_call(finish_kernel, out_shape=shapes, in_specs=[vmem] * 9, out_...]
where the time goes in v4:
time: 176 us
  Pallas kernels  175 us (99%)
    pallas_call x1, Pallas kernels, run_layer(): pl.pallas_call(functools.partial(layer_kernel, dims, names), out_shape=[j...  171 us

profile of v4, /device:TPU:25, one launch (start us, length us, event | category | flops | bytes accessed | tf_op | source)
XLA Modules:
  0.0 176.0 jit_solution(6783278666969371578)
XLA Ops:
  1.3 171.3 %layer.1 = (bf16[768,128]{1,0:T(8,128)(2,1)}, f32[768,128]{1,0:T(8,128)}, f32[3,192,192]{2,1,0:T(8,128)}, f32[192,192]{1,0:T(8,128)}, f32[192,768]{1,0:T(8,128)}...) custom-call(bf16[768,128]{1,0:T(8,128)(2,1)} %refs_0_.1, s32[1]{0:T(128)S(6)} %copy.29.refs_1_, ...), custom_call_target="tpu_custom_call" | custom-call | tf_op jit(solution)/shard_map/layer/pallas_call | solution.py:912
  172.6 3.2 %finish.1 = (bf16[768,128]{1,0:T(8,128)(2,1)}, f32[768,128]{1,0:T(8,128)}, f32[3,192,192]{2,1,0:T(8,128)}, f32[192,192]{1,0:T(8,128)}, f32[192,768]{1,0:T(8,128)...) custom-call(bf16[768,128]{1,0:T(8,128)(2,1)} %get-tuple-element.37.r, ...), custom_call_target="tpu_custom_call" | custom-call | tf_op jit(solution)/shard_map/finish/pallas_call | solution.py:949

commit v5 on v4

--- a/solution.py
+++ b/solution.py
@@ -64,8 +64,11 @@
 
 def slots_of(R, C):
     slots = Slots()
-    for name in ("x", "mix", "hid", "red", "gr", "gh", "gm", "dx", "gv_row"):
-        slots.add(name, R)
+    for name in ("x", "hid", "gr", "gm"):
+        slots.add(name, 4)
+    for name in ("mix", "red", "gh", "dx"):
+        slots.add(name, 3)
+    slots.add("gv_row", R)
     for name in ("vec", "gv_col", "ab_col", "kv_right", "kv_left", "dkv_right", "dkv_left"):
         slots.add(name, C)
     for name in ("wkv", "wqm", "w2", "w3"):
@@ -74,8 +77,11 @@
         slots.add("d" + name, C)
         slots.add("d" + name + "_dp", 1)
         slots.add("d" + name + "_out", 1)
-    for name in ("gv_dp", "ab_dp"):
+    for name in ("kv_pass", "dkv_pass"):
+        slots.add(name, C)
+    for name in ("gv_dp", "ab_dp", "len"):
         slots.add(name, 1)
+    slots.add("swap", 4)
     return slots
 
 
@@ -95,6 +101,16 @@
         return {"col": lax.rem(me_c + step, C)}
 
     partner = {"dp": 1 - me_d}
+
+    HC = C // 2
+    half, place = me_c // HC, lax.rem(me_c, HC)
+    mine = me_d * HC + place
+    swapped = me_d != half
+    stays = me_d == half
+
+    def swap_copy(src, dst, at):
+        where = {"dp": 1 - me_d, "col": lax.rem(me_c + HC, C)}
+        return copy(src, dst, "swap", at, where)
 
     def copy(src, dst, family, at, where):
         number = slots.base[family] + at
@@ -113,7 +129,12 @@
         pl.semaphore_signal(barrier, inc=1, device_id=to_row(i), device_id_type=MESH)
     for i in range(1, C):
         pl.semaphore_signal(barrier, inc=1, device_id=to_col(i), device_id_type=MESH)
-    e.xg[me_r] = turned(e.x_t[...]).astype(BF16)
+    pl.semaphore_signal(
+        barrier,
+        inc=1,
+        device_id={"dp": 1 - me_d, "col": lax.rem(me_c + HC, C)},
+        device_id_type=MESH,
+    )
     e.wkv[:, :F] = e.w_attn[1]
     e.wkv[:, F:] = e.w_attn[2]
     e.wqm[:, :F] = e.w_attn[0]
@@ -122,7 +143,22 @@
     for k, ref in enumerate(vectors):
         e.vecr[me_c, k : k + 1, :RB] = ref[...].astype(F32).reshape(1, RB)
     e.bias[...] = e.b_expand[...].astype(F32).reshape(1, U)
-    pl.semaphore_wait(barrier, 1 + (R - 1) + (C - 1))
+    e.lens[me_d] = jnp.full((8, 128), e.length[0].astype(F32), F32)
+    pl.semaphore_wait(barrier, 2 + (R - 1) + (C - 1))
+
+    @pl.when(swapped)
+    def _():
+        swap_copy(e.x_t, e.x_in, 0).start()
+
+    @pl.when(stays)
+    def _():
+        e.x_in[...] = e.x_t[...]
+        e.og_in[...] = e.out_grad[...]
+
+    def len_copy():
+        return copy(e.lens.at[me_d], e.lens.at[me_d], "len", 0, partner)
+
+    len_copy().start()
 
     def w_rows(ref, c, d):
         if not dims.flat:
@@ -139,16 +175,9 @@
         there = w_rows(getattr(e, name + "_g"), lax.rem(me_c - i + C, C), me_d)
         return copy(there, there, name + "_dp", i, partner)
 
-    def weight_start(name, which=None):
+    def weight_start(name):
         for i in range(1, C):
-            if which is None:
-                weight_copy(name, i).start()
-            else:
-                to = lax.rem(me_c + i, C)
-                inner = (to > 0) & (to < C - 1)
-                pl.when(inner if which == "inner" else jnp.logical_not(inner))(
-                    weight_copy(name, i).start
-                )
+            weight_copy(name, i).start()
 
     def weight_own(name):
         full = getattr(e, name + "_g")
@@ -182,34 +211,112 @@
         getattr(e, name + ("_g" if dims.flat else "_f")) for name in ("wkv", "wqm", "w2", "w3")
     ]
 
-    def x_copy(i):
-        return copy(e.xg.at[me_r], e.xg.at[me_r], "x", i, to_row(i))
+    beside = {"row": me_r + 1 - 2 * lax.rem(me_r, 2)}
+    across = {"row": lax.rem(me_r + 2, R)}
+    near, over, far = beside["row"], across["row"], R - 1 - me_r
+    low, high = pl.ds(0, T // 2), pl.ds(T // 2, T // 2)
+
+    def gather_copy(ref, family, at):
+        part, where = (
+            (ref.at[me_r], beside),
+            (ref.at[me_r], across),
+            (ref.at[near, low], across),
+            (ref.at[over, high], beside),
+        )[at]
+        return copy(part, part, family, at, where)
+
+    def gather_start(ref, family):
+        gather_copy(ref, family, 0).start()
+        gather_copy(ref, family, 1).start()
+
+    def gather_near(ref, family):
+        gather_copy(ref, family, 0).wait_recv()
+        gather_copy(ref, family, 2).start()
+
+    def gather_over(ref, family):
+        gather_copy(ref, family, 1).wait_recv()
+        gather_copy(ref, family, 3).start()
+
+    def gather_far(ref, family):
+        gather_copy(ref, family, 2).wait_recv()
+        gather_copy(ref, family, 3).wait_recv()
+
+    def gather_close(ref, family):
+        for at in range(4):
+            gather_copy(ref, family, at).wait_send()
+
+    def gathered(ref, family):
+        yield "own", me_r
+        gather_near(ref, family)
+        gather_over(ref, family)
+        yield "near", near
+        yield "over", over
+        gather_far(ref, family)
+        yield "far", far
+
+    def sum_copy(k, family, kind):
+        at = ("near", "over", "far").index(kind)
+        where = (beside, across, {"row": far})[at]
+        out, land, _ = e.sums[k]
+        return copy(out.at[at], land.at[at], family, at, where)
+
+    def sum_add(k, family, kind, part):
+        out, _, own = e.sums[k]
+        if kind == "own":
+            own[...] = part
+        else:
+            out[("near", "over", "far").index(kind)] = part.astype(BF16)
+            sum_copy(k, family, kind).start()
+
+    def sum_collect(k, family):
+        _, land, own = e.sums[k]
+        total = own[...]
+        for at, kind in enumerate(("near", "over", "far")):
+            sum_copy(k, family, kind).wait_recv()
+            total = total + land[at].astype(F32)
+        return total
+
+    def sum_close(k, family):
+        for kind in ("near", "over", "far"):
+            sum_copy(k, family, kind).wait_send()
+
+    e.sums = [
+        (getattr(e, f"out_{k}"), getattr(e, f"land_{k}"), own)
+        for k, own in ((0, e.own_0), (1, e.own_1), (0, e.own_0), (2, e.own_dx))
+    ]
 
     def vec_copy(i):
         return copy(e.vecr.at[me_c], e.vecr.at[me_c], "vec", i, to_col(i))
 
-    for i in range(1, R):
-        x_copy(i).start()
     weight_start("wkv")
-    length = e.length[0]
     for name in ("wkv", "wqm", "w2", "w3"):
         weight_own(name)
 
+    @pl.when(swapped)
+    def _():
+        swap_copy(e.x_t, e.x_in, 0).wait_recv()
+
+    e.xg[me_r] = turned(e.x_in[...]).astype(BF16)
+    gather_start(e.xg, "x")
     weight_share("wkv")
     weight_start("wqm")
+
+    @pl.when(swapped)
+    def _():
+        swap_copy(e.out_grad, e.og_in, 1).start()
+
+    len_copy().wait_recv()
+    length = e.lens[half][0:1, 0:1]
     for i in range(1, C):
         vec_copy(i).start()
     weight_end("wkv")
 
-    for i in range(R):
-        rb = lax.rem(me_r - i + R, R)
-        if i:
-            x_copy(i).wait_recv()
+    for _, rb in gathered(e.xg, "x"):
         tokens = pl.ds(pl.multiple_of(rb * T, T), T)
         both = dot_nn(e.xg[rb], wkv[...])
         values = both[:, F:] + e.b_attn[1:2, :].astype(F32)
-        e.kv[me_c, pl.ds(0, F), tokens] = both[:, :F].T.astype(BF16)
-        e.kv[me_c, pl.ds(F, F), tokens] = values.T.astype(BF16)
+        e.kv[mine, pl.ds(0, F), tokens] = both[:, :F].T.astype(BF16)
+        e.kv[mine, pl.ds(F, F), tokens] = values.T.astype(BF16)
 
     def make_queries():
         weight_share("wqm")
@@ -234,9 +341,12 @@
     def kv_left(b):
         return copy(e.kv.at[b], e.kv.at[b], "kv_left", b, left)
 
+    def kv_pass(b):
+        return copy(e.kv.at[b], e.kv.at[b], "kv_pass", b, partner)
+
     def key_valid(b):
         lane = lax.broadcasted_iota(jnp.int32, (1, S), 1)
-        return (lane // T * (T * C) + b * T + lane % T) < length
+        return (lane // T * (T * C) + b * T + lane % T).astype(F32) < length
 
     TQ = dims.TQ
     e.top[...] = jnp.full(e.top.shape, -3e38, F32)
@@ -268,68 +378,84 @@
 
         lax.fori_loop(0, S // TQ, tile, 0)
 
-    @pl.when(me_c < C - 1)
-    def _():
-        kv_right(me_c).start()
-
-    @pl.when(me_c > 0)
-    def _():
-        kv_left(me_c).start()
-
+    @pl.when(place < HC - 1)
+    def _():
+        kv_right(mine).start()
+
+    @pl.when(place > 0)
+    def _():
+        kv_left(mine).start()
+
+    kv_pass(mine).start()
     make_queries()
-    attend(me_c)
+    attend(mine)
+
+    def of_core(d, at):
+        return d * HC + at
+
+    kv_pass(of_core(1 - me_d, place)).wait_recv()
+    attend(of_core(1 - me_d, place))
 
     def kv_step(s, carry):
-        from_left = me_c - s
-        from_right = me_c + s
+        from_left = place - s
+        from_right = place + s
 
         @pl.when(from_left >= 0)
         def _():
-            kv_right(from_left).wait_recv()
-
-            @pl.when(me_c < C - 1)
+            b = of_core(me_d, from_left)
+            kv_right(b).wait_recv()
+            kv_pass(b).start()
+
+            @pl.when(place < HC - 1)
             def _():
-                kv_right(from_left).start()
-
-        @pl.when(from_right < C)
+                kv_right(b).start()
+
+        @pl.when(from_right < HC)
         def _():
-            kv_left(from_right).wait_recv()
-
-            @pl.when(me_c > 0)
+            b = of_core(me_d, from_right)
+            kv_left(b).wait_recv()
+            kv_pass(b).start()
+
+            @pl.when(place > 0)
             def _():
-                kv_left(from_right).start()
-
-        @pl.when(s == min(2, C - 1))
+                kv_left(b).start()
+
+        @pl.when(s == HC - 1)
         def _():
-            weight_start("w2", "inner")
-            weight_start("w3", "inner")
+            weight_start("w2")
+            weight_start("w3")
 
         @pl.when(from_left >= 0)
         def _():
-            attend(from_left)
-
-        @pl.when(from_right < C)
+            attend(of_core(me_d, from_left))
+            kv_pass(of_core(1 - me_d, from_left)).wait_recv()
+            attend(of_core(1 - me_d, from_left))
+
+        @pl.when(from_right < HC)
         def _():
-            attend(from_right)
+            attend(of_core(me_d, from_right))
+            kv_pass(of_core(1 - me_d, from_right)).wait_recv()
+            attend(of_core(1 - me_d, from_right))
 
         return carry
 
-    lax.fori_loop(1, C, kv_step, 0)
-
-    def kv_close(b, carry):
-        @pl.when((b <= me_c) & (me_c < C - 1))
+    lax.fori_loop(1, HC, kv_step, 0)
+
+    def kv_close(at, carry):
+        b = of_core(me_d, at)
+        kv_pass(b).wait_send()
+
+        @pl.when((at <= place) & (place < HC - 1))
         def _():
             kv_right(b).wait_send()
 
-        @pl.when((b >= me_c) & (me_c > 0))
+        @pl.when((at >= place) & (place > 0))
         def _():
             kv_left(b).wait_send()
 
         return carry
 
-    lax.fori_loop(0, C, kv_close, 0)
-    weight_start("w2", "outer")
-    weight_start("w3", "outer")
+    lax.fori_loop(0, HC, kv_close, 0)
 
     for h in range(NH):
         inverse = 1.0 / e.total[h]
@@ -349,23 +475,10 @@
     def blk_rows(rb):
         return pl.ds(pl.multiple_of(rb * T, T), T)
 
-    for i in list(range(1, R)) + [0]:
-        rb = lax.rem(me_r + i, R)
-        part = dot_nt(e.ctx[blk_rows(rb), :], e.mix[...])
-        if i:
-            e.stage[0, i - 1] = part.astype(BF16)
-            copy(e.stage.at[0, i - 1], e.landing.at[0, i - 1], "mix", i, to_row(i)).start()
-        else:
-            e.own[...] = part
-
-    def collect(number, family):
-        total = e.own[...]
-        for i in range(1, R):
-            copy(e.stage.at[number, i - 1], e.landing.at[number, i - 1], family, i, to_row(i)).wait_recv()
-            total = total + e.landing[number, i - 1].astype(F32)
-        return total
-
-    first_sum = turned(e.x_t[...]) + collect(0, "mix") + vector(0)
+    for kind, rb in (("far", far), ("near", near), ("over", over), ("own", me_r)):
+        sum_add(0, "mix", kind, dot_nt(e.ctx[blk_rows(rb), :], e.mix[...]))
+
+    first_sum = turned(e.x_in[...]) + sum_collect(0, "mix") + vector(0)
     normed, scale = normalize(first_sum)
     hidden = normed * vector(1) + vector(2)
     e.n1[...] = normed
@@ -373,52 +486,52 @@
     e.hidden[...] = hidden
     e.hid_g[me_r] = hidden.astype(BF16)
 
-    def share(ref, family, i):
-        return copy(ref.at[me_r], ref.at[me_r], family, i, to_row(i))
-
-    for i in range(1, R):
-        share(e.hid_g, "hid", i).start()
+    gather_start(e.hid_g, "hid")
     weight_share("w2")
     weight_end("w2")
 
-    def spread(number, family, part, i, rb):
-        if i:
-            e.stage[number, i - 1] = part.astype(BF16)
-            copy(
-                e.stage.at[number, i - 1], e.landing.at[number, i - 1], family, i, to_row(R - i)
-            ).start()
-        else:
-            e.own[...] = part
-
-    for i in range(R):
-        rb = lax.rem(me_r - i + R, R)
-        if i:
-            share(e.hid_g, "hid", i).wait_recv()
+    for kind, rb in gathered(e.hid_g, "hid"):
         inner = dot_nn(e.hid_g[rb], w2f[...]) + e.bias[...]
         cdf = 0.5 * (1.0 + lax.erf(inner * (0.5**0.5)))
         active = (inner * cdf).astype(BF16)
         slope = cdf + inner * (jnp.exp(-0.5 * inner * inner) * 0.3989422804014327)
         e.active[blk_rows(rb), :] = active
         e.slope[blk_rows(rb), :] = slope
-        if i == 0:
+        if kind == "own":
+            continue
+        if kind == "near":
             weight_share("w3")
             weight_end("w3")
-        spread(1, "red", dot_nt(e.active[blk_rows(rb), :], w3f[...]), i, rb)
+            sum_add(1, "red", "own", dot_nt(e.active[blk_rows(me_r), :], w3f[...]))
+        sum_add(1, "red", kind, dot_nt(e.active[blk_rows(rb), :], w3f[...]))
     for i in range(R):
-        rb = lax.rem(me_r - i + R, R)
-        e.hid_t[:, blk_rows(rb)] = turned(e.hid_g[rb]).astype(BF16)
-
-    second_sum = e.hidden[...] + collect(1, "red") + vector(3)
+        e.hid_t[:, i * T : (i + 1) * T] = turned(e.hid_g[i]).astype(BF16)
+    gather_close(e.hid_g, "hid")
+
+    second_sum = e.hidden[...] + sum_collect(1, "red") + vector(3)
     normed, scale = normalize(second_sum)
-    slot = lax.broadcasted_iota(jnp.int32, (T, 1), 0) + (me_r * (T * C) + me_c * T)
-    row_valid = (slot < length).astype(F32)
-    upstream = turned(e.out_grad[...]) * row_valid
+    slot = lax.broadcasted_iota(jnp.int32, (T, 1), 0) + (me_r * (T * C) + mine * T)
+    row_valid = (slot.astype(F32) < length).astype(F32)
+
+    @pl.when(swapped)
+    def _():
+        swap_copy(e.out_grad, e.og_in, 1).wait_recv()
+
+    upstream = turned(e.og_in[...]) * row_valid
     g_second = normalize_back(upstream, normed, scale, vector(4))
     g_reduced = g_second.astype(BF16)
     e.gr_g[me_r] = g_reduced
-    for i in range(1, R):
-        share(e.gr_g, "gr", i).start()
-    e.layer_out[...] = ((normed * vector(4) + vector(5)) * row_valid).T.astype(BF16)
+    gather_start(e.gr_g, "gr")
+    e.lo_out[...] = ((normed * vector(4) + vector(5)) * row_valid).T.astype(BF16)
+
+    @pl.when(swapped)
+    def _():
+        swap_copy(e.lo_out, e.layer_out, 2).start()
+
+    @pl.when(stays)
+    def _():
+        e.layer_out[...] = e.lo_out[...]
+
     e.g_second[...] = g_second
     e.gv[4:5, :] = column_sum(upstream * normed)
     e.gv[5:6, :] = column_sum(upstream)
@@ -426,19 +539,16 @@
     e.gv[7:8, :] = jnp.zeros((1, D), F32)
 
     unit_sum = jnp.zeros((1, U), F32)
-    for i in range(R):
-        rb = lax.rem(me_r - i + R, R)
-        if i:
-            share(e.gr_g, "gr", i).wait_recv()
+    sum_close(0, "mix")
+    for kind, rb in gathered(e.gr_g, "gr"):
         g_active = dot_nn(e.gr_g[rb], w3f[...]).astype(BF16).astype(F32)
         g_inner = (g_active * e.slope[blk_rows(rb), :]).astype(BF16)
         e.g_inner[blk_rows(rb), :] = g_inner
         unit_sum = unit_sum + column_sum(g_inner.astype(F32))
-        spread(2, "gh", dot_nt(e.g_inner[blk_rows(rb), :], w2f[...]), i, rb)
+        sum_add(2, "gh", kind, dot_nt(e.g_inner[blk_rows(rb), :], w2f[...]))
     e.gu[0:1, :] = unit_sum
     for i in range(R):
-        rb = lax.rem(me_r - i + R, R)
-        e.gr_t[:, blk_rows(rb)] = turned(e.gr_g[rb]).astype(BF16)
+        e.gr_t[:, i * T : (i + 1) * T] = turned(e.gr_g[i]).astype(BF16)
 
     TR = dims.TR
 
@@ -510,15 +620,12 @@
     weight_swap("dw2", e.dw_f)
     weight_send("dw2", e.dw_f)
 
-    g_hidden = collect(2, "gh") + e.g_second[...]
+    g_hidden = sum_collect(2, "gh") + e.g_second[...]
     normed = e.n1[...]
     g_first = normalize_back(g_hidden, normed, e.r1[...], vector(1))
     g_mixed = g_first.astype(BF16)
-    for i in range(1, R):
-        share(e.hid_g, "hid", i).wait_send()
     e.hid_g[me_r] = g_mixed
-    for i in range(1, R):
-        share(e.hid_g, "gm", i).start()
+    gather_start(e.hid_g, "gm")
     e.g_first[...] = g_first
     e.gv[1:2, :] = column_sum(g_hidden * normed)
     e.gv[2:3, :] = column_sum(g_hidden)
@@ -532,10 +639,7 @@
     e.gall[0, 8:16, :U] = jnp.broadcast_to(e.gu[0:1, :], (8, U))
     gv_dp().start()
 
-    for i in range(R):
-        rb = lax.rem(me_r - i + R, R)
-        if i:
-            share(e.hid_g, "gm", i).wait_recv()
+    for _, rb in gathered(e.hid_g, "gm"):
         rows = blk_rows(rb)
         g_context = dot_nn(e.hid_g[rb], e.mix[...]).astype(BF16).astype(F32)
         e.gc_t[:, rows] = g_context.T.astype(BF16)
@@ -545,14 +649,8 @@
             e.inner_sum[h, rows, :] = jnp.sum(part * e.acc[h, rows, :], 1, keepdims=True)
         e.gr_t[:, rows] = turned(e.hid_g[rb]).astype(BF16)
 
-    gv_dp().wait_recv()
-    e.gall[2] = e.gall[0] + e.gall[1]
-
     def gv_col(i):
         return copy(e.gall.at[2], e.gcol.at[i], "gv_col", i, to_col(i))
-
-    for i in range(1, C):
-        gv_col(i).start()
 
     e.dq[...] = jnp.zeros(e.dq.shape, F32)
 
@@ -584,17 +682,19 @@
 
     NB = dims.NB
 
-    def dkv_right(b):
+    def dkv_right(at):
+        b = of_core(me_d, at)
         return copy(
-            e.kv.at[b], e.dkv_in.at[0, lax.rem(C - 1 - b, NB)], "dkv_right", b, right
+            e.kv.at[b], e.dkv_in.at[0, lax.rem(HC - 1 - at, NB)], "dkv_right", at, right
         )
 
-    def dkv_left(b):
-        return copy(e.kv.at[b], e.dkv_in.at[1, lax.rem(b, NB)], "dkv_left", b, left)
-
-    def dkv_send(way, b):
-        order = C - 1 - b if way == 0 else b
-        if C - 1 > NB:
+    def dkv_left(at):
+        b = of_core(me_d, at)
+        return copy(e.kv.at[b], e.dkv_in.at[1, lax.rem(at, NB)], "dkv_left", at, left)
+
+    def dkv_send(way, at):
+        order = HC - 1 - at if way == 0 else at
+        if HC - 1 > NB:
 
             @pl.when(order >= NB)
             def _():
@@ -602,25 +702,25 @@
 
         if way == 0:
 
-            @pl.when(b < C - 1)
+            @pl.when(at < HC - 1)
             def _():
-                dkv_right(b + 1).wait_send()
-
-            dkv_right(b).start()
+                dkv_right(at + 1).wait_send()
+
+            dkv_right(at).start()
         else:
 
-            @pl.when(b > 0)
+            @pl.when(at > 0)
             def _():
-                dkv_left(b - 1).wait_send()
-
-            dkv_left(b).start()
-
-    def dkv_take(way, b, to):
-        order = C - 1 - b if way == 0 else b
-        (dkv_right if way == 0 else dkv_left)(b).wait_recv()
+                dkv_left(at - 1).wait_send()
+
+            dkv_left(at).start()
+
+    def dkv_take(way, at, to):
+        order = HC - 1 - at if way == 0 else at
+        (dkv_right if way == 0 else dkv_left)(at).wait_recv()
         e.dkv[to] += e.dkv_in[way, lax.rem(order, NB)].astype(F32)
-        if C - 1 > NB:
-            sends = C - me_c if way == 0 else me_c + 1
+        if HC - 1 > NB:
+            sends = HC - place if way == 0 else place + 1
 
             @pl.when(order + NB < sends)
             def _():
@@ -631,63 +731,104 @@
                     device_id_type=MESH,
                 )
 
-    inner_device = (me_c > 0) & (me_c < C - 1)
-
-    @pl.when(inner_device)
-    def _():
-        attend_back(me_c, 2)
+    def dkv_pass(at, to):
+        b = of_core(1 - me_d, at)
+        return copy(e.kv.at[b], e.dkv_par.at[to], "dkv_pass", at, partner)
+
+    def both_cores(at, to):
+        other = of_core(1 - me_d, at)
+        attend_back(other, to)
+        e.kv[other] = e.dkv[to].astype(BF16)
+        again = at < HC - 1 if to == 0 else at > 0
+        if HC > 2 and to < 2:
+
+            @pl.when(again)
+            def _():
+                pl.semaphore_wait(e.pass_credits.at[to], 1)
+
+        dkv_pass(at, to).start()
+        attend_back(of_core(me_d, at), to)
+        dkv_pass(at, to).wait_recv()
+        e.dkv[to] += e.dkv_par[to].astype(F32)
+        more = at > place + 1 if to == 0 else at < place - 1
+        if HC > 2 and to < 2:
+
+            @pl.when(more)
+            def _():
+                pl.semaphore_signal(
+                    e.pass_credits.at[to], inc=1, device_id=partner, device_id_type=MESH
+                )
 
     def dkv_step(s, carry):
-        from_left = C - 1 + me_c - s
-        from_right = s - (C - 1 - me_c)
-
-        @pl.when(s >= me_c)
+        from_left = HC - 1 + place - s
+        from_right = s - (HC - 1 - place)
+
+        @pl.when(s >= place)
         def _():
-            attend_back(from_left, 0)
+            both_cores(from_left, 0)
+
+            @pl.when(place > 0)
+            def _():
+                dkv_take(0, from_left, 0)
+
+            e.kv[of_core(me_d, from_left)] = e.dkv[0].astype(BF16)
+            dkv_send(0, from_left)
 
         @pl.when(from_right >= 0)
         def _():
-            attend_back(from_right, 1)
-
-        @pl.when(s >= me_c)
-        def _():
-            @pl.when(me_c > 0)
-            def _():
-                dkv_take(0, from_left, 0)
-
-            e.kv[from_left] = e.dkv[0].astype(BF16)
-            dkv_send(0, from_left)
-
-        @pl.when(from_right >= 0)
-        def _():
-            @pl.when(me_c < C - 1)
+            both_cores(from_right, 1)
+
+            @pl.when(place < HC - 1)
             def _():
                 dkv_take(1, from_right, 1)
 
-            e.kv[from_right] = e.dkv[1].astype(BF16)
+            e.kv[of_core(me_d, from_right)] = e.dkv[1].astype(BF16)
             dkv_send(1, from_right)
 
         return carry
 
-    lax.fori_loop(0, C - 1, dkv_step, 0)
-
-    @pl.when(jnp.logical_not(inner_device))
-    def _():
-        attend_back(me_c, 2)
+    lax.fori_loop(0, HC - 1, dkv_step, 0)
+    both_cores(place, 2)
 
     for h in range(NH):
         e.dqkv[h * HS : (h + 1) * HS, :] = (e.dq[h] * (HS ** (-0.5))).T.astype(BF16)
 
     def fill_query(rows):
-        e.dw_s[rows, :F] = dot_nt(e.x_rows_t[rows, :], e.dqkv[:F, :])
-        e.dw_s[rows, F:] = dot_nn(e.gr_t[rows, :], e.ctx[...])
+        e.dw_f[rows, :F] = dot_nt(e.x_rows_t[rows, :], e.dqkv[:F, :])
+        e.dw_f[rows, F : 2 * F] = dot_nn(e.gr_t[rows, :], e.ctx[...])
 
     row_tiles(fill_query)
-    weight_swap("dwqm", e.dw_s)
-    weight_send("dwqm", e.dw_s)
-    weight_collect("dw3")
-    weight_collect("dw2")
-
+    query_grad = e.dw_f.at[:, pl.ds(0, 2 * F)]
+    weight_swap("dwqm", query_grad)
+    gv_dp().wait_recv()
+    e.gall[2] = e.gall[0] + e.gall[1]
+    for i in range(1, C):
+        gv_col(i).start()
+    weight_send("dwqm", query_grad)
+
+    @pl.when(place > 0)
+    def _():
+        dkv_take(0, place, 2)
+
+    @pl.when(place < HC - 1)
+    def _():
+        dkv_take(1, place, 2)
+
+    e.dqkv[F : 3 * F, :] = e.dkv[2].astype(BF16)
+
+    def fill_keys(rows):
+        e.dw_f[rows, 2 * F :] = dot_nt(e.x_rows_t[rows, :], e.dqkv[F:, :])
+
+    row_tiles(fill_keys)
+    key_grad = e.dw_f.at[:, pl.ds(2 * F, 2 * F)]
+    weight_swap("dwkv", key_grad)
+
+    def input_part(kind, rb):
+        part = dot_nn(wqm[:, :F], e.dqkv[:F, blk_rows(rb)])
+        part = part + dot_nn(wkv[...], e.dqkv[F:, blk_rows(rb)])
+        sum_add(3, "dx", kind, part)
+
+    input_part("far", far)
     for i in range(1, C):
         gv_col(i).wait_recv()
     gsum = e.gall[2]
@@ -701,32 +842,6 @@
     for i in range(1, R):
         gv_row(i).start()
 
-    @pl.when(me_c > 0)
-    def _():
-        dkv_take(0, me_c, 2)
-
-    @pl.when(me_c < C - 1)
-    def _():
-        dkv_take(1, me_c, 2)
-
-    e.dqkv[F : 3 * F, :] = e.dkv[2].astype(BF16)
-
-    for i in list(range(1, R)) + [0]:
-        rb = lax.rem(me_r + i, R)
-        part = dot_nn(wqm[:, :F], e.dqkv[:F, blk_rows(rb)]) + dot_nn(
-            wkv[...], e.dqkv[F:, blk_rows(rb)]
-        )
-        if i:
-            e.dx_stage[i - 1] = part.astype(BF16)
-            copy(e.dx_stage.at[i - 1], e.dx_land.at[i - 1], "dx", i, to_row(i)).start()
-        else:
-            e.dx_own[...] = part
-
-    def fill_keys(rows):
-        e.dw_s[rows, :] = dot_nt(e.x_rows_t[rows, :], e.dqkv[F:, :])
-
-    row_tiles(fill_keys)
-    weight_swap("dwkv", e.dw_s)
     e.ab[0] = dot_nt(jnp.ones((8, S), BF16), e.dqkv[...])
 
     def ab_dp():
@@ -736,28 +851,40 @@
         return copy(e.ab.at[2], e.abcol.at[i], "ab_col", i, to_col(i))
 
     ab_dp().start()
-    weight_send("dwkv", e.dw_s)
+    weight_send("dwkv", key_grad)
     ab_dp().wait_recv()
     e.ab[2] = e.ab[0] + e.ab[1]
     for i in range(1, C):
         ab_col(i).start()
 
+    input_part("near", near)
+    input_part("over", over)
+    input_part("own", me_r)
+    e.own_dx[...] = sum_collect(3, "dx") + e.g_first[...].T
+
+    @pl.when(swapped)
+    def _():
+        swap_copy(e.lo_out, e.layer_out, 2).wait_send()
+        swap_copy(e.lo_out, e.layer_out, 2).wait_recv()
+        e.lo_out[...] = e.own_dx[...].astype(BF16)
+        swap_copy(e.lo_out, e.og_in, 3).start()
+
+    @pl.when(stays)
+    def _():
+        e.grad_input[...] = e.own_dx[...]
+
+    weight_collect("dw3")
+    weight_collect("dw2")
     weight_collect("dwqm")
-
-    total = e.dx_own[...] + e.g_first[...].T
-    for i in range(1, R):
-        copy(e.dx_stage.at[i - 1], e.dx_land.at[i - 1], "dx", i, to_row(i)).wait_recv()
-        total = total + e.dx_land[i - 1].astype(F32)
-    e.grad_input[...] = total
 
     vsum = e.gsum[0:8, :D]
     for i in range(1, R):
         gv_row(i).wait_recv()
         vsum = vsum + e.grow[i][:, :D]
-    mine = vsum[:, :RB]
+    picked = vsum[:, :RB]
     for c in range(1, C):
-        mine = jnp.where(me_c == c, vsum[:, c * RB : (c + 1) * RB], mine)
-    e.g_vec[...] = mine
+        picked = jnp.where(me_c == c, vsum[:, c * RB : (c + 1) * RB], picked)
+    e.g_vec[...] = picked
     e.g_unit[...] = e.gsum[8:9, :U]
     asum = e.ab[2]
     for i in range(1, C):
@@ -774,16 +901,26 @@
     e.g_attn[1] = e.dwkv_sum[:, :F]
     e.g_attn[2] = e.dwkv_sum[:, F:]
 
+    @pl.when(swapped)
+    def _():
+        swap_copy(e.lo_out, e.og_in, 3).wait_recv()
+        e.grad_input[...] = e.og_in[...].astype(F32)
+
+    @pl.when(swapped)
+    def _():
+        swap_copy(e.x_t, e.x_in, 0).wait_send()
+        swap_copy(e.out_grad, e.og_in, 1).wait_send()
+        swap_copy(e.lo_out, e.og_in, 3).wait_send()
+
+    len_copy().wait_send()
     for name in ("wkv", "wqm", "w2", "w3"):
         weight_close(name)
+    gather_close(e.xg, "x")
+    gather_close(e.gr_g, "gr")
+    gather_close(e.hid_g, "gm")
+    for k, family in ((1, "red"), (2, "gh"), (3, "dx")):
+        sum_close(k, family)
     for i in range(1, R):
-        x_copy(i).wait_send()
-        copy(e.stage.at[0, i - 1], e.landing.at[0, i - 1], "mix", i, to_row(i)).wait_send()
-        copy(e.stage.at[1, i - 1], e.landing.at[1, i - 1], "red", i, to_row(i)).wait_send()
-        share(e.gr_g, "gr", i).wait_send()
-        copy(e.stage.at[2, i - 1], e.landing.at[2, i - 1], "gh", i, to_row(i)).wait_send()
-        share(e.hid_g, "gm", i).wait_send()
-        copy(e.dx_stage.at[i - 1], e.dx_land.at[i - 1], "dx", i, to_row(i)).wait_send()
         gv_row(i).wait_send()
     gv_dp().wait_send()
     ab_dp().wait_send()
@@ -798,13 +935,16 @@
         if dims.flat:
             result_copy(name).wait_send()
 
-    @pl.when(me_c < C - 1)
-    def _():
-        dkv_right(me_c + 1).wait_send()
-
-    @pl.when(me_c > 0)
-    def _():
-        dkv_left(me_c - 1).wait_send()
+    for at in range(HC):
+        dkv_pass(at, 2).wait_send()
+
+    @pl.when(place < HC - 1)
+    def _():
+        dkv_right(place + 1).wait_send()
+
+    @pl.when(place > 0)
+    def _():
+        dkv_left(place - 1).wait_send()
 
 
 def run_layer(x_t, length, w_attn, w_mixer, w2, w3, out_grad, b_attn, b_expand, **vectors):
@@ -819,7 +959,7 @@
     HS = D // H
     dims = SimpleNamespace(
         R=R, C=C, T=T, S=S, F=F, U=U, RB=RB, HS=HS, NH=F // HS,
-        flat=flat, HB=RB // 2 if flat else RB, TQ=min(256, S), TR=256, NB=min(C - 1, 3),
+        flat=flat, HB=RB // 2 if flat else RB, TQ=min(256, S), TR=256, NB=max(1, min(C // 2 - 1, 3)),
     )
     HB = dims.HB
     NH = dims.NH
@@ -861,9 +1001,9 @@
         total=((NH, S, 1), F32),
         acc=((NH, S, HS), F32),
         ctx=((S, F), BF16),
-        stage=((3, R - 1, T, D), BF16),
-        landing=((3, R - 1, T, D), BF16),
-        own=((T, D), F32),
+        own_0=((T, D), F32),
+        own_1=((T, D), F32),
+        own_dx=((D, T), F32),
         n1=((T, D), F32),
         r1=((T, 1), F32),
         hidden=((T, D), F32),
@@ -882,7 +1022,6 @@
         gsum=((16, wide), F32),
         grow=((R, 8, wide), F32),
         dw_f=((D, U), F32),
-        dw_s=((D, 2 * F), F32),
         dwqm_sum=((RB, 2 * F), F32),
         dwkv_sum=((RB, 2 * F), F32),
         g_first=((T, D), F32),
@@ -891,20 +1030,25 @@
         inner_sum=((NH, S, 1), F32),
         dq=((NH, S, HS), F32),
         dkv=((3, 2 * F, S), F32),
+        dkv_par=((3, 2 * F, S), BF16),
+        lens=((2, 8, 128), F32),
+        x_in=((D, T), BF16),
+        og_in=((D, T), BF16),
+        lo_out=((D, T), BF16),
         dkv_in=((2, dims.NB, 2 * F, S), BF16),
         dqkv=((3 * F, S), BF16),
-        dx_stage=((R - 1, D, T), BF16),
-        dx_land=((R - 1, D, T), BF16),
-        dx_own=((D, T), F32),
         ab=((3, 8, 3 * F), F32),
         abcol=((C, 8, 3 * F), F32),
     )
+    for k, (rows, width) in enumerate(((T, D), (T, D), (D, T))):
+        scratch[f"out_{k}"] = ((3, rows, width), BF16)
+        scratch[f"land_{k}"] = ((3, rows, width), BF16)
     for name, width in (("wkv", 2 * F), ("wqm", 2 * F), ("w2", U), ("w3", U)):
         for part in ("out", "in", "land"):
             scratch["d" + name + "_" + part] = ((C, HB, width), BF16)
         if not dims.flat:
             scratch[name + "_f"] = ((C * RB, width), BF16)
-    names = list(inputs) + list(outputs) + list(scratch) + ["send_sems", "recv_sems", "credits"]
+    names = list(inputs) + list(outputs) + list(scratch) + ["send_sems", "recv_sems", "credits", "pass_credits"]
     vmem = pl.BlockSpec(memory_space=pltpu.VMEM)
     in_specs = [
         pl.BlockSpec(memory_space=pltpu.SMEM) if name == "length" else vmem for name in inputs
@@ -916,7 +1060,7 @@
         out_specs=[vmem] * len(outputs),
         scratch_shapes=[pltpu.VMEM(s, t) for s, t in scratch.values()]
         + [pltpu.SemaphoreType.DMA((slots.total,)), pltpu.SemaphoreType.DMA((slots.total,))]
-        + [pltpu.SemaphoreType.REGULAR((2,))],
+        + [pltpu.SemaphoreType.REGULAR((2,)), pltpu.SemaphoreType.REGULAR((2,))],
         compiler_params=pltpu.CompilerParams(
             collective_id=0, has_side_effects=True, vmem_limit_bytes=63 * 2**20
         ),

time: 176 us -> 150 us (0.85)
  the two profiles are of different devices: /device:TPU:25 before, /device:TPU:0 now
where the time goes in v5:
time: 150 us
  Pallas kernels  149 us (99%)
    pallas_call x1, Pallas kernels, run_layer(): pl.pallas_call(functools.partial(layer_kernel, dims, names), out_shape=[j...  145 us
    pallas_call x1, Pallas kernels, finish(): pl.pallas_call(finish_kernel, out_shape=shapes, in_specs=[vmem] * 9, out_...  3.24 us

profile of v5, /device:TPU:0, one launch (start us, length us, event | category | flops | bytes accessed | tf_op | source)
XLA Modules:
  0.0 150.2 jit_solution(13530329263031939569)
XLA Ops:
  1.3 145.5 %layer.1 = (bf16[768,128]{1,0:T(8,128)(2,1)}, f32[768,128]{1,0:T(8,128)}, f32[3,192,192]{2,1,0:T(8,128)}, f32[192,192]{1,0:T(8,128)}, f32[192,768]{1,0:T(8,128)}...) custom-call(bf16[768,128]{1,0:T(8,128)(2,1)} %refs_0_.1, s32[1]{0:T(128)S(6)} %copy.29.refs_1_, ...), custom_call_target="tpu_custom_call" | custom-call | tf_op jit(solution)/shard_map/layer/pallas_call | solution.py:1056
  146.8 3.2 %finish.1 = (bf16[768,128]{1,0:T(8,128)(2,1)}, f32[768,128]{1,0:T(8,128)}, f32[3,192,192]{2,1,0:T(8,128)}, f32[192,192]{1,0:T(8,128)}, f32[192,768]{1,0:T(8,128)...) custom-call(bf16[768,128]{1,0:T(8,128)(2,1)} %get-tuple-element.37.r, ...), custom_call_target="tpu_custom_call" | custom-call | tf_op jit(solution)/shard_map/finish/pallas_call | solution.py:1093

commit v6 on v5

--- a/solution.py
+++ b/solution.py
@@ -69,16 +69,18 @@
     for name in ("mix", "red", "gh", "dx"):
         slots.add(name, 3)
     slots.add("gv_row", R)
-    for name in ("vec", "gv_col", "ab_col", "kv_right", "kv_left", "dkv_right", "dkv_left"):
+    for name in ("vec", "gv_col", "ab_col", "dkv_right", "dkv_left"):
         slots.add(name, C)
     for name in ("wkv", "wqm", "w2", "w3"):
-        slots.add(name, C)
+        slots.add(name + "_right", C)
+        slots.add(name + "_left", C)
         slots.add(name + "_dp", C)
         slots.add("d" + name, C)
         slots.add("d" + name + "_dp", 1)
         slots.add("d" + name + "_out", 1)
-    for name in ("kv_pass", "dkv_pass"):
-        slots.add(name, C)
+    slots.add("dkv_pass", C)
+    for name in ("kv_pass", "kv_right", "kv_left"):
+        slots.add(name, C * R)
     for name in ("gv_dp", "ab_dp", "len"):
         slots.add(name, 1)
     slots.add("swap", 4)
@@ -165,20 +167,6 @@
             return ref.at[c]
         return ref.at[pl.ds(pl.multiple_of(c * RB + d * HB, HB), HB)]
 
-    def weight_copy(name, i):
-        own = getattr(e, name)
-        if dims.flat:
-            own = own.at[pl.ds(pl.multiple_of(me_d * HB, HB), HB)]
-        return copy(own, w_rows(getattr(e, name + "_g"), me_c, me_d), name, i, to_col(i))
-
-    def weight_pass(name, i):
-        there = w_rows(getattr(e, name + "_g"), lax.rem(me_c - i + C, C), me_d)
-        return copy(there, there, name + "_dp", i, partner)
-
-    def weight_start(name):
-        for i in range(1, C):
-            weight_copy(name, i).start()
-
     def weight_own(name):
         full = getattr(e, name + "_g")
         if dims.flat:
@@ -186,26 +174,70 @@
         else:
             full[me_c] = getattr(e, name)[...]
 
-    def weight_share(name):
-        for i in range(1, C):
-            weight_copy(name, i).wait_recv()
-            if dims.flat:
-                weight_pass(name, i).start()
-
-    def weight_end(name):
+    right = {"col": lax.rem(me_c + 1, C)}
+    left = {"col": lax.rem(me_c + C - 1, C)}
+
+    def line_copy(name, way, b):
+        there = w_rows(getattr(e, name + "_g"), b, me_d)
+        return copy(there, there, name + way, b, right if way == "_right" else left)
+
+    def line_pass(name, b):
+        there = w_rows(getattr(e, name + "_g"), b, me_d)
+        return copy(there, there, name + "_dp", b, partner)
+
+    def line_on(name, way, b):
+        pl.when(me_c < C - 1 if way == "_right" else me_c > 0)(line_copy(name, way, b).start)
+
+    def line_start(name):
+        line_on(name, "_right", me_c)
+        line_on(name, "_left", me_c)
+
+    def line_step(name, step):
+        for way, b, there in (
+            ("_right", me_c - step, me_c >= step),
+            ("_left", me_c + step, me_c + step < C),
+        ):
+
+            @pl.when(there)
+            def _(way=way, b=b):
+                line_copy(name, way, b).wait_recv()
+                line_on(name, way, b)
+                if dims.flat:
+                    line_pass(name, b).start()
+
+    def line_end(name, first=3):
+        def step(i, carry):
+            line_step(name, i)
+            return carry
+
+        lax.fori_loop(min(first, C), C, step, 0)
         if dims.flat:
             for i in range(1, C):
-                weight_pass(name, i).wait_recv()
+                line_pass(name, lax.rem(me_c + i, C)).wait_recv()
         else:
             full = getattr(e, name + "_g")
             flat = full[...].astype(F32).reshape(C * RB, full.shape[2])
             getattr(e, name + "_f")[...] = flat.astype(BF16)
 
-    def weight_close(name):
-        for i in range(1, C):
-            weight_copy(name, i).wait_send()
+    def line_close(name):
+        def step(b, carry):
+            @pl.when((b <= me_c) & (me_c < C - 1))
+            def _():
+                line_copy(name, "_right", b).wait_send()
+
+            @pl.when((b >= me_c) & (me_c > 0))
+            def _():
+                line_copy(name, "_left", b).wait_send()
+
             if dims.flat:
-                weight_pass(name, i).wait_send()
+
+                @pl.when(b != me_c)
+                def _():
+                    line_pass(name, b).wait_send()
+
+            return carry
+
+        lax.fori_loop(0, C, step, 0)
 
     wkv, wqm, w2f, w3f = [
         getattr(e, name + ("_g" if dims.flat else "_f")) for name in ("wkv", "wqm", "w2", "w3")
@@ -245,6 +277,13 @@
         for at in range(4):
             gather_copy(ref, family, at).wait_send()
 
+    def each(count, body):
+        def step(j, carry):
+            body(j)
+            return carry
+
+        lax.fori_loop(0, count, step, 0)
+
     def gathered(ref, family):
         yield "own", me_r
         gather_near(ref, family)
@@ -282,15 +321,16 @@
 
     e.sums = [
         (getattr(e, f"out_{k}"), getattr(e, f"land_{k}"), own)
-        for k, own in ((0, e.own_0), (1, e.own_1), (0, e.own_0), (2, e.own_dx))
+        for k, own in ((0, e.own), (1, e.own), (0, e.own), (2, e.own_dx))
     ]
 
     def vec_copy(i):
         return copy(e.vecr.at[me_c], e.vecr.at[me_c], "vec", i, to_col(i))
 
-    weight_start("wkv")
     for name in ("wkv", "wqm", "w2", "w3"):
         weight_own(name)
+    line_start("wkv")
+    line_start("wqm")
 
     @pl.when(swapped)
     def _():
@@ -298,29 +338,51 @@
 
     e.xg[me_r] = turned(e.x_in[...]).astype(BF16)
     gather_start(e.xg, "x")
-    weight_share("wkv")
-    weight_start("wqm")
-
-    @pl.when(swapped)
-    def _():
-        swap_copy(e.out_grad, e.og_in, 1).start()
+    for step in range(1, min(3, C)):
+        line_step("wkv", step)
+        line_step("wqm", step)
 
     len_copy().wait_recv()
     length = e.lens[half][0:1, 0:1]
     for i in range(1, C):
         vec_copy(i).start()
-    weight_end("wkv")
-
-    for _, rb in gathered(e.xg, "x"):
+    gather_near(e.xg, "x")
+    gather_over(e.xg, "x")
+    line_end("wkv")
+
+    def of_core(d, at):
+        return d * HC + at
+
+    def kv_copy(b, i, family, where):
+        part = e.kv.at[b, :, pl.ds(pl.multiple_of(i * T, T), T)]
+        return copy(part, part, family, b * R + i, where)
+
+    def kv_right(b, i):
+        return kv_copy(b, i, "kv_right", right)
+
+    def kv_left(b, i):
+        return kv_copy(b, i, "kv_left", left)
+
+    def kv_pass(b, i):
+        return kv_copy(b, i, "kv_pass", partner)
+
+    def kv_on(b, i):
+        pl.when(place < HC - 1)(kv_right(b, i).start)
+        pl.when(place > 0)(kv_left(b, i).start)
+        kv_pass(b, i).start()
+
+    for kind, rb in (("own", me_r), ("near", near), ("over", over), ("far", far)):
+        if kind == "far":
+            gather_far(e.xg, "x")
         tokens = pl.ds(pl.multiple_of(rb * T, T), T)
         both = dot_nn(e.xg[rb], wkv[...])
         values = both[:, F:] + e.b_attn[1:2, :].astype(F32)
         e.kv[mine, pl.ds(0, F), tokens] = both[:, :F].T.astype(BF16)
         e.kv[mine, pl.ds(F, F), tokens] = values.T.astype(BF16)
+        kv_on(mine, rb)
 
     def make_queries():
-        weight_share("wqm")
-        weight_end("wqm")
+        line_end("wqm")
         e.mix[...] = wqm[:, F:]
         for i in range(R):
             tokens = pl.ds(i * T, T)
@@ -332,136 +394,120 @@
                 e.q_h[h, tokens, :] = q[:, h * HS : (h + 1) * HS].astype(BF16)
             e.x_rows_t[:, tokens] = turned(block).astype(BF16)
 
-    right = {"col": lax.rem(me_c + 1, C)}
-    left = {"col": lax.rem(me_c + C - 1, C)}
-
-    def kv_right(b):
-        return copy(e.kv.at[b], e.kv.at[b], "kv_right", b, right)
-
-    def kv_left(b):
-        return copy(e.kv.at[b], e.kv.at[b], "kv_left", b, left)
-
-    def kv_pass(b):
-        return copy(e.kv.at[b], e.kv.at[b], "kv_pass", b, partner)
-
     def key_valid(b):
         lane = lax.broadcasted_iota(jnp.int32, (1, S), 1)
         return (lane // T * (T * C) + b * T + lane % T).astype(F32) < length
 
     TQ = dims.TQ
     e.top[...] = jnp.full(e.top.shape, -3e38, F32)
-    e.total[...] = jnp.zeros(e.total.shape, F32)
     e.acc[...] = jnp.zeros(e.acc.shape, F32)
-
-    def attend(b):
-        valid = key_valid(b)
+    ones = jnp.ones((16, S), BF16)
+
+    def tiles(body):
+        if TQ == S:
+            body(0, 0)
+        else:
+            lax.fori_loop(0, S // TQ, body, 0)
+
+    def attend(at):
+        blocks = (of_core(0, at), of_core(1, at))
+        valid = [key_valid(b) for b in blocks]
 
         def tile(t, carry):
             rows = pl.ds(pl.multiple_of(t * TQ, TQ), TQ)
             for h in range(NH):
-                keys = e.kv[b, h * HS : (h + 1) * HS, :]
-                values = e.kv[b, F + h * HS : F + (h + 1) * HS, :]
-                scores = dot_nn(e.q_h[h, rows, :], keys)
-                scores = jnp.where(valid, scores, NEGATIVE)
+                scores = [
+                    jnp.where(
+                        ok,
+                        dot_nn(e.q_h[h, rows, :], e.kv[b, h * HS : (h + 1) * HS, :]),
+                        NEGATIVE,
+                    )
+                    for b, ok in zip(blocks, valid)
+                ]
                 old = e.top[h, rows, :]
-                new = jnp.maximum(old, jnp.max(scores, 1, keepdims=True))
-                shrink = jnp.exp(old - new)
-                probs = jnp.exp(scores - new)
+                new = jnp.maximum(
+                    old, jnp.max(jnp.maximum(*scores), 1, keepdims=True)
+                )
                 e.top[h, rows, :] = new
-                e.total[h, rows, :] = shrink * e.total[h, rows, :] + jnp.sum(
-                    probs, 1, keepdims=True
-                )
-                e.acc[h, rows, :] = shrink * e.acc[h, rows, :] + dot_nt(
-                    probs.astype(BF16), values
-                )
+                part = jnp.exp(old - new) * e.acc[h, rows, :]
+                for b, score in zip(blocks, scores):
+                    values = e.kv[b, F + h * HS : F + (h + 1) * HS, :]
+                    part = part + dot_nt(
+                        jnp.exp(score - new).astype(BF16), jnp.concatenate([values, ones], 0)
+                    )
+                e.acc[h, rows, :] = part
             return carry
 
-        lax.fori_loop(0, S // TQ, tile, 0)
-
-    @pl.when(place < HC - 1)
-    def _():
-        kv_right(mine).start()
-
-    @pl.when(place > 0)
-    def _():
-        kv_left(mine).start()
-
-    kv_pass(mine).start()
+        tiles(tile)
+
     make_queries()
-    attend(mine)
-
-    def of_core(d, at):
-        return d * HC + at
-
-    kv_pass(of_core(1 - me_d, place)).wait_recv()
-    attend(of_core(1 - me_d, place))
 
     def kv_step(s, carry):
         from_left = place - s
         from_right = place + s
 
-        @pl.when(from_left >= 0)
+        @pl.when((s > 0) & (from_left >= 0))
         def _():
             b = of_core(me_d, from_left)
-            kv_right(b).wait_recv()
-            kv_pass(b).start()
-
-            @pl.when(place < HC - 1)
-            def _():
-                kv_right(b).start()
-
-        @pl.when(from_right < HC)
+
+            @functools.partial(each, R)
+            def _(i):
+                kv_right(b, i).wait_recv()
+                kv_pass(b, i).start()
+                pl.when(place < HC - 1)(kv_right(b, i).start)
+
+        @pl.when((s > 0) & (from_right < HC))
         def _():
             b = of_core(me_d, from_right)
-            kv_left(b).wait_recv()
-            kv_pass(b).start()
-
-            @pl.when(place > 0)
-            def _():
-                kv_left(b).start()
+
+            @functools.partial(each, R)
+            def _(i):
+                kv_left(b, i).wait_recv()
+                kv_pass(b, i).start()
+                pl.when(place > 0)(kv_left(b, i).start)
 
         @pl.when(s == HC - 1)
         def _():
-            weight_start("w2")
-            weight_start("w3")
-
-        @pl.when(from_left >= 0)
-        def _():
-            attend(of_core(me_d, from_left))
-            kv_pass(of_core(1 - me_d, from_left)).wait_recv()
-            attend(of_core(1 - me_d, from_left))
-
-        @pl.when(from_right < HC)
-        def _():
-            attend(of_core(me_d, from_right))
-            kv_pass(of_core(1 - me_d, from_right)).wait_recv()
-            attend(of_core(1 - me_d, from_right))
+            line_start("w2")
+            line_start("w3")
+
+        @functools.partial(each, 2)
+        def _(k):
+            at = jnp.where(k == 0, from_left, from_right)
+
+            @pl.when((at >= 0) & (at < HC) & ((s > 0) | (k == 0)))
+            def _():
+                each(R, lambda i: kv_pass(of_core(1 - me_d, at), i).wait_recv())
+                attend(at)
 
         return carry
 
-    lax.fori_loop(1, HC, kv_step, 0)
+    lax.fori_loop(0, HC, kv_step, 0)
 
     def kv_close(at, carry):
         b = of_core(me_d, at)
-        kv_pass(b).wait_send()
-
-        @pl.when((at <= place) & (place < HC - 1))
-        def _():
-            kv_right(b).wait_send()
-
-        @pl.when((at >= place) & (place > 0))
-        def _():
-            kv_left(b).wait_send()
+
+        @functools.partial(each, R)
+        def _(i):
+            kv_pass(b, i).wait_send()
+
+            @pl.when((at <= place) & (place < HC - 1))
+            def _():
+                kv_right(b, i).wait_send()
+
+            @pl.when((at >= place) & (place > 0))
+            def _():
+                kv_left(b, i).wait_send()
 
         return carry
 
     lax.fori_loop(0, HC, kv_close, 0)
 
     for h in range(NH):
-        inverse = 1.0 / e.total[h]
+        inverse = 1.0 / e.acc[h, :, HS : HS + 1]
         e.total[h] = inverse
-        context = e.acc[h] * inverse
-        e.acc[h] = context
+        context = e.acc[h, :, :HS] * inverse
+        e.acc[h, :, :HS] = context
         e.ctx[:, h * HS : (h + 1) * HS] = context.astype(BF16)
 
     for i in range(1, C):
@@ -478,6 +524,8 @@
     for kind, rb in (("far", far), ("near", near), ("over", over), ("own", me_r)):
         sum_add(0, "mix", kind, dot_nt(e.ctx[blk_rows(rb), :], e.mix[...]))
 
+    line_step("w2", 1)
+    line_step("w3", 1)
     first_sum = turned(e.x_in[...]) + sum_collect(0, "mix") + vector(0)
     normed, scale = normalize(first_sum)
     hidden = normed * vector(1) + vector(2)
@@ -487,8 +535,15 @@
     e.hid_g[me_r] = hidden.astype(BF16)
 
     gather_start(e.hid_g, "hid")
-    weight_share("w2")
-    weight_end("w2")
+
+    @pl.when(swapped)
+    def _():
+        swap_copy(e.out_grad, e.og_in, 1).start()
+
+    if C > 2:
+        line_step("w2", 2)
+        line_step("w3", 2)
+    line_end("w2")
 
     for kind, rb in gathered(e.hid_g, "hid"):
         inner = dot_nn(e.hid_g[rb], w2f[...]) + e.bias[...]
@@ -500,8 +555,7 @@
         if kind == "own":
             continue
         if kind == "near":
-            weight_share("w3")
-            weight_end("w3")
+            line_end("w3")
             sum_add(1, "red", "own", dot_nt(e.active[blk_rows(me_r), :], w3f[...]))
         sum_add(1, "red", kind, dot_nt(e.active[blk_rows(rb), :], w3f[...]))
     for i in range(R):
@@ -635,8 +689,8 @@
     def gv_dp():
         return copy(e.gall.at[0], e.gall.at[1], "gv_dp", 0, partner)
 
-    e.gall[0, 0:8, :D] = e.gv[...]
-    e.gall[0, 8:16, :U] = jnp.broadcast_to(e.gu[0:1, :], (8, U))
+    e.gall[0, :, :D] = e.gv[...]
+    e.gall[0, 6:7, :U] = e.gu[0:1, :]
     gv_dp().start()
 
     for _, rb in gathered(e.hid_g, "gm"):
@@ -646,7 +700,7 @@
         for h in range(NH):
             part = g_context[:, h * HS : (h + 1) * HS]
             e.gc_h[h, rows, :] = part.astype(BF16)
-            e.inner_sum[h, rows, :] = jnp.sum(part * e.acc[h, rows, :], 1, keepdims=True)
+            e.inner_sum[h, rows, :] = jnp.sum(part * e.acc[h, rows, :HS], 1, keepdims=True)
         e.gr_t[:, rows] = turned(e.hid_g[rb]).astype(BF16)
 
     def gv_col(i):
@@ -676,7 +730,10 @@
                 return d_keys, d_values
 
             zero = jnp.zeros((HS, S), F32)
-            d_keys, d_values = lax.fori_loop(0, S // TQ, tile, (zero, zero))
+            if TQ == S:
+                d_keys, d_values = tile(0, (zero, zero))
+            else:
+                d_keys, d_values = lax.fori_loop(0, S // TQ, tile, (zero, zero))
             e.dkv[to, krows, :] = d_keys
             e.dkv[to, vrows, :] = d_values
 
@@ -736,59 +793,66 @@
         return copy(e.kv.at[b], e.dkv_par.at[to], "dkv_pass", at, partner)
 
     def both_cores(at, to):
-        other = of_core(1 - me_d, at)
-        attend_back(other, to)
-        e.kv[other] = e.dkv[to].astype(BF16)
-        again = at < HC - 1 if to == 0 else at > 0
-        if HC > 2 and to < 2:
-
-            @pl.when(again)
+        first = jnp.where(to == 0, at == HC - 1, at == 0)
+        last = jnp.where(to == 0, at == place + 1, at == place - 1)
+
+        @functools.partial(each, 2)
+        def _(k):
+            b = of_core(jnp.where(k == 0, 1 - me_d, me_d), at)
+            attend_back(b, to)
+
+            @pl.when(k == 0)
             def _():
-                pl.semaphore_wait(e.pass_credits.at[to], 1)
-
-        dkv_pass(at, to).start()
-        attend_back(of_core(me_d, at), to)
+                e.kv[b] = e.dkv[to].astype(BF16)
+                if HC > 2:
+
+                    @pl.when((to < 2) & jnp.logical_not(first))
+                    def _():
+                        pl.semaphore_wait(e.pass_credits.at[to], 1)
+
+                dkv_pass(at, to).start()
+
         dkv_pass(at, to).wait_recv()
         e.dkv[to] += e.dkv_par[to].astype(F32)
-        more = at > place + 1 if to == 0 else at < place - 1
-        if HC > 2 and to < 2:
-
-            @pl.when(more)
+        if HC > 2:
+
+            @pl.when((to < 2) & jnp.logical_not(last))
             def _():
                 pl.semaphore_signal(
                     e.pass_credits.at[to], inc=1, device_id=partner, device_id_type=MESH
                 )
 
-    def dkv_step(s, carry):
-        from_left = HC - 1 + place - s
-        from_right = s - (HC - 1 - place)
-
-        @pl.when(s >= place)
+    def dkv_step(n, carry):
+        s, way = n // 2, lax.rem(n, 2)
+        own = s == HC - 1
+        at = jnp.where(way == 0, HC - 1 + place - s, s - (HC - 1 - place))
+        there = jnp.where(own, way == 0, jnp.where(way == 0, s >= place, at >= 0))
+
+        @pl.when(there)
         def _():
-            both_cores(from_left, 0)
-
-            @pl.when(place > 0)
+            both_cores(at, jnp.where(own, 2, way))
+
+            @pl.when(jnp.logical_not(own) & (way == 0))
             def _():
-                dkv_take(0, from_left, 0)
-
-            e.kv[of_core(me_d, from_left)] = e.dkv[0].astype(BF16)
-            dkv_send(0, from_left)
-
-        @pl.when(from_right >= 0)
-        def _():
-            both_cores(from_right, 1)
-
-            @pl.when(place < HC - 1)
+                @pl.when(place > 0)
+                def _():
+                    dkv_take(0, at, 0)
+
+                e.kv[of_core(me_d, at)] = e.dkv[0].astype(BF16)
+                dkv_send(0, at)
+
+            @pl.when(jnp.logical_not(own) & (way == 1))
             def _():
-                dkv_take(1, from_right, 1)
-
-            e.kv[of_core(me_d, from_right)] = e.dkv[1].astype(BF16)
-            dkv_send(1, from_right)
+                @pl.when(place < HC - 1)
+                def _():
+                    dkv_take(1, at, 1)
+
+                e.kv[of_core(me_d, at)] = e.dkv[1].astype(BF16)
+                dkv_send(1, at)
 
         return carry
 
-    lax.fori_loop(0, HC - 1, dkv_step, 0)
-    both_cores(place, 2)
+    lax.fori_loop(0, 2 * HC, dkv_step, 0)
 
     for h in range(NH):
         e.dqkv[h * HS : (h + 1) * HS, :] = (e.dq[h] * (HS ** (-0.5))).T.astype(BF16)
@@ -837,7 +901,7 @@
     e.gsum[...] = gsum
 
     def gv_row(i):
-        return copy(e.gsum.at[pl.ds(0, 8)], e.grow.at[i], "gv_row", i, to_row(i))
+        return copy(e.gsum, e.grow.at[i], "gv_row", i, to_row(i))
 
     for i in range(1, R):
         gv_row(i).start()
@@ -885,7 +949,7 @@
     for c in range(1, C):
         picked = jnp.where(me_c == c, vsum[:, c * RB : (c + 1) * RB], picked)
     e.g_vec[...] = picked
-    e.g_unit[...] = e.gsum[8:9, :U]
+    e.g_unit[...] = e.gsum[6:7, :U]
     asum = e.ab[2]
     for i in range(1, C):
         ab_col(i).wait_recv()
@@ -914,7 +978,7 @@
 
     len_copy().wait_send()
     for name in ("wkv", "wqm", "w2", "w3"):
-        weight_close(name)
+        line_close(name)
     gather_close(e.xg, "x")
     gather_close(e.gr_g, "gr")
     gather_close(e.hid_g, "gm")
@@ -999,10 +1063,9 @@
         x_rows_t=((D, S), BF16),
         top=((NH, S, 1), F32),
         total=((NH, S, 1), F32),
-        acc=((NH, S, HS), F32),
+        acc=((NH, S, HS + 16), F32),
         ctx=((S, F), BF16),
-        own_0=((T, D), F32),
-        own_1=((T, D), F32),
+        own=((T, D), F32),
         own_dx=((D, T), F32),
         n1=((T, D), F32),
         r1=((T, 1), F32),
@@ -1017,9 +1080,9 @@
         g_inner=((S, U), BF16),
         gv=((8, D), F32),
         gu=((8, U), F32),
-        gall=((3, 16, wide), F32),
-        gcol=((C, 16, wide), F32),
-        gsum=((16, wide), F32),
+        gall=((3, 8, wide), F32),
+        gcol=((C, 8, wide), F32),
+        gsum=((8, wide), F32),
         grow=((R, 8, wide), F32),
         dw_f=((D, U), F32),
         dwqm_sum=((RB, 2 * F), F32),
@@ -1062,7 +1125,7 @@
         + [pltpu.SemaphoreType.DMA((slots.total,)), pltpu.SemaphoreType.DMA((slots.total,))]
         + [pltpu.SemaphoreType.REGULAR((2,)), pltpu.SemaphoreType.REGULAR((2,))],
         compiler_params=pltpu.CompilerParams(
-            collective_id=0, has_side_effects=True, vmem_limit_bytes=63 * 2**20
+            collective_id=0, has_side_effects=True, vmem_limit_bytes=639 * 2**20 // 10
         ),
         name="layer",
     )(*inputs.values())

time: 150 us -> 144 us (0.960)
  the two profiles are of different devices: /device:TPU:0 before, /device:TPU:25 now
where the time goes in v6:
time: 144 us; the launch traced here: 142 us
  Pallas kernels  140 us (97%)
  between operations  1.46 us (1%)
    pallas_call x1, Pallas kernels, run_layer(): pl.pallas_call(functools.partial(layer_kernel, dims, names), out_shape=[j...  137 us
    pallas_call x1, Pallas kernels, finish(): pl.pallas_call(finish_kernel, out_shape=shapes, in_specs=[vmem] * 9, out_...  3.24 us

profile of v6, /device:TPU:25, one launch (start us, length us, event | category | flops | bytes accessed | tf_op | source)
XLA Modules:
  0.0 141.7 jit_solution(14158782320343781861)
XLA Ops:
  1.3 137.0 %layer.1 = (bf16[768,128]{1,0:T(8,128)(2,1)}, f32[768,128]{1,0:T(8,128)}, f32[3,192,192]{2,1,0:T(8,128)}, f32[192,192]{1,0:T(8,128)}, f32[192,768]{1,0:T(8,128)}...) custom-call(bf16[768,128]{1,0:T(8,128)(2,1)} %refs_0_.1, s32[1]{0:T(128)S(6)} %copy.29.refs_1_, ...), custom_call_target="tpu_custom_call" | custom-call | tf_op jit(solution)/shard_map/layer/pallas_call | solution.py:1119
  138.3 3.2 %finish.1 = (bf16[768,128]{1,0:T(8,128)(2,1)}, f32[768,128]{1,0:T(8,128)}, f32[3,192,192]{2,1,0:T(8,128)}, f32[192,192]{1,0:T(8,128)}, f32[192,768]{1,0:T(8,128)...) custom-call(bf16[768,128]{1,0:T(8,128)(2,1)} %get-tuple-element.37.r, ...), custom_call_target="tpu_custom_call" | custom-call | tf_op jit(solution)/shard_map/finish/pallas_call | solution.py:1156

commit v7 on v6

--- a/solution.py
+++ b/solution.py
@@ -869,6 +869,8 @@
     for i in range(1, C):
         gv_col(i).start()
     weight_send("dwqm", query_grad)
+    weight_collect("dw3")
+    weight_collect("dw2")
 
     @pl.when(place > 0)
     def _():
@@ -937,8 +939,6 @@
     def _():
         e.grad_input[...] = e.own_dx[...]
 
-    weight_collect("dw3")
-    weight_collect("dw2")
     weight_collect("dwqm")
 
     vsum = e.gsum[0:8, :D]

time: 144 us -> 144 us (level)
  no operation moved by 1% of the time
where the time goes in v7:
time: 144 us; the launch traced here: 142 us
  Pallas kernels  140 us (97%)
  between operations  1.46 us (1%)
    pallas_call x1, Pallas kernels, run_layer(): pl.pallas_call(functools.partial(layer_kernel, dims, names), out_shape=[j...  137 us
    pallas_call x1, Pallas kernels, finish(): pl.pallas_call(finish_kernel, out_shape=shapes, in_specs=[vmem] * 9, out_...  3.24 us

profile of v7, /device:TPU:25, one launch (start us, length us, event | category | flops | bytes accessed | tf_op | source)
XLA Modules:
  0.0 141.7 jit_solution(14739008611068974267)
XLA Ops:
  1.3 137.0 %layer.1 = (bf16[768,128]{1,0:T(8,128)(2,1)}, f32[768,128]{1,0:T(8,128)}, f32[3,192,192]{2,1,0:T(8,128)}, f32[192,192]{1,0:T(8,128)}, f32[192,768]{1,0:T(8,128)}...) custom-call(bf16[768,128]{1,0:T(8,128)(2,1)} %refs_0_.1, s32[1]{0:T(128)S(6)} %copy.29.refs_1_, ...), custom_call_target="tpu_custom_call" | custom-call | tf_op jit(solution)/shard_map/layer/pallas_call | solution.py:1119
  138.3 3.2 %finish.1 = (bf16[768,128]{1,0:T(8,128)(2,1)}, f32[768,128]{1,0:T(8,128)}, f32[3,192,192]{2,1,0:T(8,128)}, f32[192,192]{1,0:T(8,128)}, f32[192,768]{1,0:T(8,128)...) custom-call(bf16[768,128]{1,0:T(8,128)(2,1)} %get-tuple-element.37.r, ...), custom_call_target="tpu_custom_call" | custom-call | tf_op jit(solution)/shard_map/finish/pallas_call | solution.py:1156
